TPU v7x, 128 devices: a whole 4x4x4 slice. The times are simulated.
128 devices in a mesh: fsdp: 64 (over z, y, x_lo, core), tp: 2 (over x_hi).
Axes of the slice: x: 4 (x_hi: 2, x_lo: 2; x = x_hi * 2 + x_lo), y: 4, z: 4, core: 2. Of those that a mesh axis runs over, the one named last changes fastest.
Arguments:
- latents: bfloat16 [128, 128, 1152], P('fsdp', 'tp'), may hold values from -6 to 6
- condition: bfloat16 [96, 1152], replicated, may hold values from -6 to 6
- counts: int32 [64], replicated, may hold values from 1 to 2, 96 in all
- order: int32 [96], replicated, may hold values from 0 to 95, each once
- w_ada: bfloat16 [1152, 6, 1152], P(None, None, ('fsdp', 'tp')), may hold values from -0.1875 to 0.1875
- b_ada: float32 [6, 1152], P(None, ('fsdp', 'tp')), may hold values from -1.8 to 1.8
- w_qkv: bfloat16 [3, 1152, 1152], P(None, 'fsdp', 'tp'), may hold values from -0.1875 to 0.1875
- b_qv: float32 [2, 1152], P(None, 'tp'), may hold values from -1.8 to 1.8
- w_proj: bfloat16 [1152, 1152], P('tp', 'fsdp'), may hold values from -0.75 to 0.75
- b_proj: float32 [1152], replicated, may hold values from -1.8 to 1.8
- w_up: bfloat16 [1152, 4608], P('fsdp', 'tp'), may hold values from -0.1875 to 0.1875
- b_up: float32 [4608], P('tp'), may hold values from -1.8 to 1.8
- w_down: bfloat16 [4608, 1152], P('tp', 'fsdp'), may hold values from -0.09375 to 0.09375
- b_down: float32 [1152], replicated, may hold values from -1.8 to 1.8
- cotangent: bfloat16 [128, 128, 1152], P('fsdp', 'tp'), may hold values from -6 to 6
Outputs:
- block_output: bfloat16 [128, 128, 1152], P('fsdp', 'tp')
- grad_latents: float32 [128, 128, 1152], P('fsdp', 'tp')
- grad_condition: float32 [96, 1152], replicated
- grad_w_ada: float32 [1152, 6, 1152], P(None, None, ('fsdp', 'tp'))
- grad_b_ada: float32 [6, 1152], P(None, ('fsdp', 'tp'))
- grad_w_qkv: float32 [3, 1152, 1152], P(None, 'fsdp', 'tp')
- grad_b_qv: float32 [2, 1152], P(None, 'tp')
- grad_w_proj: float32 [1152, 1152], P('tp', 'fsdp')
- grad_b_proj: float32 [1152], replicated
- grad_w_up: float32 [1152, 4608], P('fsdp', 'tp')
- grad_b_up: float32 [4608], P('tp')
- grad_w_down: float32 [4608, 1152], P('tp', 'fsdp')
- grad_b_down: float32 [1152], replicated
Inputs may be any that keep to these rules, and one draw needn't show every extreme that they name: counts[g] latents sit in the first slots of group g; they add up to 96, and some group holds 2. Each latent number appears once; group g holds latents order[o] to order[o + counts[g] - 1], o the sum of counts before g. Tokens in empty slots are read by no output.
All inputs are finite; a program needn't handle non-finite values.
Results may differ from a plain program's by a relative error of at most 0.015.
The roundings to bfloat16 on the way count: a program that leaves them out, or rounds other values in their place, can miss the bound.
Values may be sent and summed in bfloat16 or wider, within the bound.
A program may use at most 128 MiB of HBM per device.

v0:
```python
import jax
import jax.numpy as jnp
from jax import lax
from jax.sharding import PartitionSpec as P

HEAD_DIM = 72


highest = lax.Precision.HIGHEST
norm_eps = 1e-06


def modulate(rows, shift, scale):
    centred = rows - jnp.mean(rows, axis=-1, keepdims=True)
    normed = centred * lax.rsqrt(jnp.mean(centred * centred, axis=-1, keepdims=True) + norm_eps)
    return normed * (1.0 + scale) + shift


def gelu_tanh(values):
    return jax.nn.gelu(values, approximate=True)


def widen(rows):
    return lax.all_gather(rows, "tp", axis=1, tiled=True)


def narrow(terms):
    return lax.psum_scatter(
        terms.astype(jnp.bfloat16), "tp", scatter_dimension=1, tiled=True
    ).astype(jnp.float32)


def attend_forward(pieces):
    queries, keys, values = pieces
    factor = queries.shape[-1] ** (-0.5)
    scores = jnp.einsum("lhe,mhe->hlm", queries, keys, preferred_element_type=jnp.float32) * factor
    peak = jnp.max(scores, axis=-1, keepdims=True)
    raised = jnp.exp(scores - peak)
    total = jnp.sum(raised, axis=-1, keepdims=True)
    weights = (raised / total).astype(jnp.bfloat16)
    mixed = jnp.einsum("hlm,mhe->lhe", weights, values, preferred_element_type=jnp.float32)
    return (mixed.astype(jnp.bfloat16), (peak + jnp.log(total))[..., 0])


def attend_backward(pieces):
    queries, keys, values, log_total, grad_mixed = pieces
    factor = queries.shape[-1] ** (-0.5)
    scores = jnp.einsum("lhe,mhe->hlm", queries, keys, preferred_element_type=jnp.float32) * factor
    probs = jnp.exp(scores - log_total[..., None])
    grad_probs = jnp.einsum("lhe,mhe->hlm", grad_mixed, values, preferred_element_type=jnp.float32)
    inner = jnp.sum(probs * grad_probs, axis=-1, keepdims=True)
    grad_scores = (probs * (grad_probs - inner)).astype(jnp.bfloat16)
    grad_queries = (
        jnp.einsum("hlm,mhe->lhe", grad_scores, keys, preferred_element_type=jnp.float32) * factor
    ).astype(jnp.bfloat16)
    grad_keys = (
        jnp.einsum("hlm,lhe->mhe", grad_scores, queries, preferred_element_type=jnp.float32)
        * factor
    ).astype(jnp.bfloat16)
    grad_values = jnp.einsum(
        "hlm,lhe->mhe", probs.astype(jnp.bfloat16), grad_mixed, preferred_element_type=jnp.float32
    ).astype(jnp.bfloat16)
    return (grad_queries, grad_keys, grad_values)


def local(
    latents,
    condition,
    counts,
    order,
    w_ada,
    b_ada,
    w_qkv,
    b_qv,
    w_proj,
    b_proj,
    w_up,
    b_up,
    w_down,
    b_down,
    cotangent,
):
    slots = latents.shape[0]
    latent_count = condition.shape[0]
    group = lax.axis_index("fsdp")
    ranks = jnp.arange(counts.shape[0], dtype=jnp.int32)
    held = jnp.sum(jnp.where(ranks == group, counts, 0))
    before = jnp.sum(jnp.where(ranks < group, counts, 0))
    slot_rank = jnp.arange(slots, dtype=jnp.int32)
    live = (slot_rank < held).astype(jnp.float32)
    place = jnp.clip(before + slot_rank, 0, latent_count - 1)
    numbers = jnp.arange(latent_count, dtype=jnp.int32)
    owner = jnp.sum(jnp.where(numbers[None, :] == place[:, None], order[None, :], 0), axis=1)
    choose = (numbers[None, :] == owner[:, None]).astype(jnp.float32)
    soft_cond = jax.nn.silu(condition.astype(jnp.float32))
    ada_local = w_ada.astype(jnp.float32)
    mod_part = jnp.einsum("nd,dke->nke", soft_cond, ada_local, precision=highest) + b_ada
    mod_all = lax.all_gather(mod_part.astype(jnp.bfloat16), ("fsdp", "tp"), axis=2, tiled=True)
    slot_mod = jnp.einsum("sn,nke->ske", choose, mod_all.astype(jnp.float32), precision=highest)
    shift_one = slot_mod[:, 0:1]
    scale_one = slot_mod[:, 1:2]
    gate_one = slot_mod[:, 2:3]
    shift_two = slot_mod[:, 3:4]
    scale_two = slot_mod[:, 4:5]
    gate_two = slot_mod[:, 5:6]
    rows = latents.astype(jnp.float32)
    qkv_all, proj_all = (
        lax.all_gather(w_qkv, "fsdp", axis=1, tiled=True),
        lax.all_gather(w_proj, "fsdp", axis=1, tiled=True),
    )
    normed_one = widen(modulate(rows, shift_one, scale_one).astype(jnp.bfloat16))
    length = normed_one.shape[1]
    head_dim = HEAD_DIM
    head_part = qkv_all.shape[2]
    head_count = head_part // head_dim
    bias_three = jnp.stack([b_qv[0], jnp.zeros_like(b_qv[0]), b_qv[1]])
    triple = (
        jnp.einsum("bld,kde->kble", normed_one, qkv_all, preferred_element_type=jnp.float32)
        + bias_three[:, None, None, :]
    ).astype(jnp.bfloat16)
    heads_shape = (slots, length, head_count, head_dim)
    queries = triple[0].reshape(heads_shape)
    keys = triple[1].reshape(heads_shape)
    values = triple[2].reshape(heads_shape)
    attended_heads, log_total = lax.map(attend_forward, (queries, keys, values))
    attended = attended_heads.reshape(slots, length, head_part)
    branch = (
        narrow(jnp.einsum("ble,ed->bld", attended, proj_all, preferred_element_type=jnp.float32))
        + b_proj
    )
    middle = rows + gate_one * branch
    up_all, down_all = (
        lax.all_gather(w_up, "fsdp", axis=0, tiled=True),
        lax.all_gather(w_down, "fsdp", axis=1, tiled=True),
    )
    normed_two = widen(modulate(middle, shift_two, scale_two).astype(jnp.bfloat16))
    upper = jnp.einsum("bld,df->blf", normed_two, up_all, preferred_element_type=jnp.float32) + b_up
    acted = gelu_tanh(upper).astype(jnp.bfloat16)
    down = (
        narrow(jnp.einsum("blf,fd->bld", acted, down_all, preferred_element_type=jnp.float32))
        + b_down
    )
    alive = live[:, None, None]
    block_output = ((middle + gate_two * down) * alive).astype(jnp.bfloat16)
    grad_rows = cotangent.astype(jnp.float32) * alive
    grad_gate_two = jnp.sum(grad_rows * down, axis=1, keepdims=True)
    down_low = (gate_two * grad_rows).astype(jnp.bfloat16)
    grad_b_down = jnp.sum(down_low.astype(jnp.float32), axis=(0, 1))
    down_wide = widen(down_low)
    up_use, down_use = (up_all, down_all)
    grad_acted = jnp.einsum("bld,fd->blf", down_wide, down_use, preferred_element_type=jnp.float32)
    grad_upper = jax.vjp(gelu_tanh, upper)[1](grad_acted)[0]
    upper_low = grad_upper.astype(jnp.bfloat16)
    grad_b_up_local = jnp.sum(upper_low.astype(jnp.float32), axis=(0, 1))
    grad_w_down = jnp.einsum("blf,bld->fd", acted, down_wide, preferred_element_type=jnp.float32)
    grad_w_up = jnp.einsum("bld,blf->df", normed_two, upper_low, preferred_element_type=jnp.float32)
    grad_normed_two = narrow(
        jnp.einsum("blf,df->bld", upper_low, up_use, preferred_element_type=jnp.float32)
    )
    grad_middle_norm, grad_shift_two, grad_scale_two = jax.vjp(
        modulate, middle, shift_two, scale_two
    )[1](grad_normed_two)
    grad_middle = grad_rows + grad_middle_norm
    grad_gate_one = jnp.sum(grad_middle * branch, axis=1, keepdims=True)
    branch_low = (gate_one * grad_middle).astype(jnp.bfloat16)
    grad_b_proj = jnp.sum(branch_low.astype(jnp.float32), axis=(0, 1))
    branch_wide = widen(branch_low)
    qkv_use, proj_use = (qkv_all, proj_all)
    grad_attended = jnp.einsum(
        "bld,ed->ble", branch_wide, proj_use, preferred_element_type=jnp.float32
    ).astype(jnp.bfloat16)
    grad_w_proj = jnp.einsum(
        "ble,bld->ed", attended, branch_wide, preferred_element_type=jnp.float32
    )
    grad_queries, grad_keys, grad_values = lax.map(
        attend_backward, (queries, keys, values, log_total, grad_attended.reshape(heads_shape))
    )
    flat_shape = (slots, length, head_part)
    grad_triple = jnp.stack(
        [
            grad_queries.reshape(flat_shape),
            grad_keys.reshape(flat_shape),
            grad_values.reshape(flat_shape),
        ]
    )
    grad_b_qv_local = jnp.stack(
        [
            jnp.sum(grad_queries.astype(jnp.float32), axis=(0, 1)).reshape(-1),
            jnp.sum(grad_values.astype(jnp.float32), axis=(0, 1)).reshape(-1),
        ]
    )
    grad_w_qkv = jnp.einsum(
        "bld,kble->kde", normed_one, grad_triple, preferred_element_type=jnp.float32
    )
    grad_normed_one = narrow(
        jnp.einsum("kble,kde->bld", grad_triple, qkv_use, preferred_element_type=jnp.float32)
    )
    grad_rows_norm, grad_shift_one, grad_scale_one = jax.vjp(modulate, rows, shift_one, scale_one)[
        1
    ](grad_normed_one)
    grad_latents = grad_middle + grad_rows_norm
    grad_w_qkv, grad_w_proj, grad_w_up, grad_w_down = (
        lax.psum_scatter(grad_w_qkv, "fsdp", scatter_dimension=1, tiled=True),
        lax.psum_scatter(grad_w_proj, "fsdp", scatter_dimension=1, tiled=True),
        lax.psum_scatter(grad_w_up, "fsdp", scatter_dimension=0, tiled=True),
        lax.psum_scatter(grad_w_down, "fsdp", scatter_dimension=1, tiled=True),
    )
    grad_mod = jnp.concatenate(
        [
            grad_shift_one,
            grad_scale_one,
            grad_gate_one,
            grad_shift_two,
            grad_scale_two,
            grad_gate_two,
        ],
        axis=1,
    )
    grad_table = jnp.einsum("sn,ske->nke", choose, grad_mod, precision=highest)
    grad_mod_part = lax.psum_scatter(grad_table, ("fsdp", "tp"), scatter_dimension=2, tiled=True)
    grad_b_ada = jnp.sum(grad_mod_part, axis=0)
    grad_w_ada = jnp.einsum("nd,nke->dke", soft_cond, grad_mod_part, precision=highest)
    grad_soft_part = jnp.einsum("nke,dke->nd", grad_mod_part, ada_local, precision=highest)
    tensor_rank = lax.axis_index("tp")
    zero_index = jnp.zeros((), jnp.int32)
    up_half = grad_b_up_local.shape[0]
    qv_place = lax.dynamic_update_slice(
        jnp.zeros((2, head_part * lax.axis_size("tp")), jnp.float32),
        grad_b_qv_local,
        (zero_index, tensor_rank * head_part),
    )
    up_place = lax.dynamic_update_slice(
        jnp.zeros((up_half * lax.axis_size("tp"),), jnp.float32),
        grad_b_up_local,
        (tensor_rank * up_half,),
    )
    grad_soft, grad_b_proj, grad_b_down, qv_full, up_full = lax.psum(
        (grad_soft_part, grad_b_proj, grad_b_down, qv_place, up_place), ("fsdp", "tp")
    )
    grad_b_qv = lax.dynamic_slice_in_dim(qv_full, tensor_rank * head_part, head_part, 1)
    grad_b_up = lax.dynamic_slice_in_dim(up_full, tensor_rank * up_half, up_half, 0)
    grad_condition = jax.vjp(jax.nn.silu, condition.astype(jnp.float32))[1](grad_soft)[0]
    return (
        block_output,
        grad_latents,
        grad_condition,
        grad_w_ada,
        grad_b_ada,
        grad_w_qkv,
        grad_b_qv,
        grad_w_proj,
        grad_b_proj,
        grad_w_up,
        grad_b_up,
        grad_w_down,
        grad_b_down,
    )


def solution(mesh):
    in_specs = (
        P("fsdp", "tp", None),
        P(),
        P(),
        P(),
        P(None, None, ("fsdp", "tp")),
        P(None, ("fsdp", "tp")),
        P(None, "fsdp", "tp"),
        P(None, "tp"),
        P("tp", "fsdp"),
        P(),
        P("fsdp", "tp"),
        P("tp"),
        P("tp", "fsdp"),
        P(),
        P("fsdp", "tp", None),
    )
    out_specs = (
        P("fsdp", "tp", None),
        P("fsdp", "tp", None),
        P(),
        P(None, None, ("fsdp", "tp")),
        P(None, ("fsdp", "tp")),
        P(None, "fsdp", "tp"),
        P(None, "tp"),
        P("tp", "fsdp"),
        P(),
        P("fsdp", "tp"),
        P("tp"),
        P("tp", "fsdp"),
        P(),
    )
    return jax.shard_map(local, mesh=mesh, in_specs=in_specs, out_specs=out_specs, check_vma=False)
```

profile of v0, /device:TPU:1, one launch (start us, length us, event | category | flops | bytes accessed | tf_op | source)
XLA Modules:
  0.0 2372.4 jit_solution(4263945944564813195)
XLA Ops:
  13.1 103.7 %all-gather.13.cloned.1.call-done = bf16[64,18,576]{2,1,0:T(8,128)(2,1)} async-done(((bf16[1,18,576]{2,1,0:T(8,128)(2,1)}), bf16[64,18,576]{2,1,0:T(8,128)(2,1)}) %all-gather.13.cloned.1.call-update) | async-done | bytes 1327120 | tf_op jit(solution)/shard_map/all_gather | solution.py:109
  116.8 2.8 reshape.142
  119.6 298.5 %all-gather.9.cloned.1.call-done = bf16[96,6,1152]{0,1,2:T(8,128)(2,1)} async-done(((bf16[96,6,9]{0,1,2:T(8,128)(2,1)}), bf16[96,6,1152]{0,1,2:T(8,128)(2,1)}) %all-gather.9.cloned.1.call-update) | async-done | bytes 1327120 | tf_op jit(solution)/shard_map/all_gather | solution.py:98
  418.1 2.3 fusion.63
  420.6 10.7 all_gather.28
  431.3 97.3 %all-gather.11.cloned.1.call-done = bf16[3,1152,576]{2,0,1:T(4,128)(2,1)} async-done(((bf16[3,18,576]{2,0,1:T(4,128)(2,1)}), bf16[3,1152,576]{2,0,1:T(4,128)(2,1)}) %all-gather.11.cloned.1.call-update) | async-done | bytes 3981328 | tf_op jit(solution)/shard_map/all_gather | solution.py:108
  528.6 4.6 fusion.70
  534.8 1.5 convolution_convert_fusion.2
  538.4 13.3 all_gather.34
  551.8 5.1 reduce-scatter.13.cloned.1.call-done
  560.5 12.0 all_gather.31
  572.6 95.1 %all-gather.15.cloned.1.call-done = bf16[64,18,2304]{2,1,0:T(8,128)(2,1)} async-done(((bf16[1,18,2304]{2,1,0:T(8,128)(2,1)}), bf16[64,18,2304]{2,1,0:T(8,128)(2,1)}) %all-gather.15.cloned.1.call-update) | async-done | bytes 5308432 | tf_op jit(solution)/shard_map/all_gather | solution.py:133
  667.7 8.3 reshape.152
  676.0 5.9 convolution_add_fusion
  681.9 96.0 %all-gather.17.cloned.1.call-done = bf16[64,18,2304]{2,1,0:T(8,128)(2,1)} async-done(((bf16[1,18,2304]{2,1,0:T(8,128)(2,1)}), bf16[64,18,2304]{2,1,0:T(8,128)(2,1)}) %all-gather.17.cloned.1.call-update) | async-done | bytes 5308432 | tf_op jit(solution)/shard_map/all_gather | solution.py:134
  777.9 8.2 reshape.153
  786.1 6.1 convert_reduce_fusion
  793.2 5.0 convolution_convert_fusion.3
  798.3 6.1 convolution_convert_fusion.4
  804.6 11.7 reduce-scatter.17.cloned.1.call-done
  818.9 18.5 reduce-scatter.15.cloned.1.call-done
  837.4 2.3 convert_reduce_fusion.5
  839.7 10.2 all_gather.35
  853.0 7.6 while.27
  860.6 5.4 fusion.53
  866.1 19.7 reduce-scatter.19.cloned.1.call-done
  887.0 2.0 fusion.90
  889.2 3.0 fusion.110
  892.1 7.5 copy.96
  900.7 7.0 convolution_bitcast_fusion.1
  907.7 5.7 convolution_bitcast_fusion
  913.4 631.5 %reduce-scatter.21.cloned.1.call-done = f32[96,6,9]{0,1,2:T(8,128)} async-done(((f32[96,6,1152]{0,1,2:T(8,128)}), f32[96,6,9]{0,1,2:T(8,128)}) %reduce-scatter.21.cloned.1.call-update) | async-done | bytes 20752
  1544.9 2.0 convolution_bitcast_fusion.4
  1547.0 4.4 convolution_bitcast_fusion.2
  1551.4 13.8 copy.98
  1565.2 2.2 convolution_bitcast_fusion.3
  1567.5 448.6 %fusion.125 = (f32[24,2304]{1,0:T(8,128)S(1)}, f32[2304,24]{0,1:T(8,128)S(1)}) fusion(f32[1152,2304]{1,0:T(8,128)} %convolution_bitcast_fusion.1, f32[2304,1152]{0,1:T(8,128)} %convolution_bitcast_fusion), kind=kCustom, calls=%all-reduce-scatter.2 | all-reduce-scatter fusion | flops 7077889 | bytes 21676544
  2024.0 17.6 collective-permute-done.15
  2043.0 2.0 collective-permute-done.14
  2048.9 9.7 collective-permute-start.6
  2058.7 17.1 collective-permute-start.5
  2077.1 8.3 collective-permute-start.3
  2086.8 3.1 collective-permute-start.1
  2089.9 3.1 collective-permute-start
  2093.0 7.4 collective-permute-start.30
  2100.4 3.0 collective-permute-start.29
  2103.4 4.2 collective-permute-done.2
  2108.9 1.7 collective-permute-start.27
  2110.6 7.0 collective-permute-start.26
  2117.6 33.8 %collective-permute-done.30 = f32[2304,24]{0,1:T(8,128)S(1)} collective-permute-done((f32[2304,24]{0,1:T(8,128)S(1)}, f32[2304,24]{0,1:T(8,128)S(1)}, u32[]{:S(2)}, u32[]{:S(2)}) %collective-permute-start.30) | collective-permute-done | bytes 221216
  2155.4 9.3 collective-permute-start.22
  2166.0 4.5 collective-permute-start.20
  2170.5 2.0 collective-permute-start.19
  2172.5 2.0 collective-permute-start.18
  2174.5 4.1 collective-permute-start.17
  2178.6 8.5 collective-permute-start.16
  2189.5 28.4 %concatenate.4 = f32[402,2304]{1,0:T(8,128)} concatenate(f32[18,2304]{1,0:T(8,128)S(1)} %collective-permute-done.15, f32[24,2304]{1,0:T(8,128)S(1)} %collective-permute-done.14, f32[24,2304]{1,0:T(8,128)S(1)} %collective-permute-done.13, f32[24,2304]{1,0:T(8,128)} %copy-done.28, f32[24,2304]{1,0:T(8,128)} %copy-done.29, f32[24,2304]{1,0:T(8,128)} %copy-done.30, ...), dimensions={0} | concatenate | bytes 7409664
  2218.0 28.5 %concatenate.5 = f32[2304,402]{0,1:T(8,128)} concatenate(f32[2304,18]{0,1:T(8,128)S(1)} %collective-permute-done.31, f32[2304,24]{0,1:T(8,128)} %copy-done.39, f32[2304,24]{0,1:T(8,128)} %copy-done.41, f32[2304,24]{0,1:T(8,128)} %copy-done.43, f32[2304,24]{0,1:T(8,128)} %copy-done.44, f32[2304,24]{0,1:T(8,128)} %copy-done.45, f32[2304,24]{0,1:T(8,128)} %copy-done.46, ...), dimensions={1} | concatenate | bytes 7409664
  2246.5 1.7 constant_dynamic-slice_fusion.1
  2248.2 1.7 constant_dynamic-slice_fusion
  2250.7 70.8 %all-reduce.7 = (f32[2,1152]{1,0:T(2,128)S(1)}, f32[1152]{0:T(1024)}, f32[4608]{0:T(1024)S(1)}, f32[1152]{0:T(1024)}) all-reduce(f32[2,1152]{1,0:T(2,128)S(1)} %dynamic_update_slice.23, f32[1152]{0:T(1024)S(1)} %get-tuple-element.218, f32[4608]{0:T(1024)S(1)} %dynamic_update_slice.24, ...), channel_id=1, replica_groups=mesh['fsdp'=64,'tp'=2] {'fsdp','tp'}, use_global_device_ids=true, to_apply=%region_34.35 | all-reduce | flops 9216 | bytes 73728 | tf_op jit(solution)/shard_map/psum | solution.py:237
  2326.3 2.0 fusion.99
  2328.3 33.9 %all-reduce.15.cloned.1.call-done = (f32[3,1152,576]{2,0,1:T(4,128)}, f32[576,1152]{0,1:T(8,128)}) async-done(((f32[3,1152,576]{2,0,1:T(4,128)}, f32[576,1152]{0,1:T(8,128)}), (f32[3,1152,576]{2,0,1:T(4,128)}, f32[576,1152]{0,1:T(8,128)})) %all-reduce.15.cloned.1.call-update) | async-done | bytes 10616848
  2363.1 1.5 constant_dynamic-slice_fusion.3
  (290 shorter events, 61.7 us)
Async XLA Ops:
  7.2 109.5 %all-gather.13.cloned.1.call-start = ((), (), s32[]{:S(2)}) async-start(), calls=%async_computation.12 | async-start | bytes 1996800 | tf_op jit(solution)/shard_map/all_gather | solution.py:109
  8.0 410.1 %all-gather.9.cloned.1.call-start = ((), (), s32[]{:S(2)}) async-start(), calls=%async_computation.5 | async-start | bytes 2377728 | tf_op jit(solution)/shard_map/all_gather | solution.py:98
  10.2 518.5 %all-gather.11.cloned.1.call-start = ((), (), s32[]{:S(2)}) async-start(), calls=%async_computation.6 | async-start | bytes 5990400 | tf_op jit(solution)/shard_map/all_gather | solution.py:108
  11.0 546.0 %reduce-scatter.13.cloned.1.call-start = ((), (), s32[]{:S(2)}) async-start(), calls=%async_computation.7 | async-start | bytes 884736 | tf_op jit(solution)/shard_map/reduce_scatter | solution.py:28
  12.6 405.5 %copy-start.56 = (s32[2]{0:T(128)}, s32[2]{0:T(128)S(1)}, u32[]{:S(2)}) copy-start(s32[2]{0:T(128)S(1)} %fusion.113) | copy-start | bytes 28
  431.3 97.3 %copy-start.19 = (bf16[2,128,1152]{2,1,0:T(8,128)(2,1)}, bf16[2,128,1152]{2,1,0:T(8,128)(2,1)S(1)}, u32[]{:S(2)}) copy-start(bf16[2,128,1152]{2,1,0:T(8,128)(2,1)S(1)} %all_gather.28) | copy-start | bytes 1769476
  536.4 131.3 %all-gather.15.cloned.1.call-start = ((), (), s32[]{:S(2)}) async-start(), calls=%async_computation.13 | async-start | bytes 7188480 | tf_op jit(solution)/shard_map/all_gather | solution.py:133
  537.0 240.9 %all-gather.17.cloned.1.call-start = ((), (), s32[]{:S(2)}) async-start(), calls=%async_computation.14 | async-start | bytes 7188480 | tf_op jit(solution)/shard_map/all_gather | solution.py:134
  537.6 278.7 %reduce-scatter.17.cloned.1.call-start = ((), (), s32[]{:S(2)}) async-start(), calls=%async_computation.9 | async-start | bytes 884736 | tf_op jit(solution)/shard_map/reduce_scatter | solution.py:28
  572.6 103.5 %copy-start.60 = (f32[2304]{0:T(1024)S(1)}, f32[2304]{0:T(1024)}, u32[]{:S(2)}) copy-start(f32[2304]{0:T(1024)} %param.30) | copy-start | bytes 27652
  798.3 39.2 %reduce-scatter.15.cloned.1.call-start = ((), (), s32[]{:S(2)}) async-start(), calls=%async_computation.8 | async-start | bytes 884736 | tf_op jit(solution)/shard_map/reduce_scatter | solution.py:28
  804.5 81.3 %reduce-scatter.19.cloned.1.call-start = ((), (), s32[]{:S(2)}) async-start(), calls=%async_computation.10 | async-start | bytes 884736 | tf_op jit(solution)/shard_map/reduce_scatter | solution.py:28
  866.1 678.8 %reduce-scatter.21.cloned.1.call-start = ((), (), s32[]{:S(2)}) async-start(), calls=%async_computation.15 | async-start | bytes 4755456
  899.7 1426.6 %all-reduce.13.cloned.1.call-start = ((), (), s32[]{:S(2)}) async-start(), calls=%async_computation.11 | async-start | bytes 884736 | tf_op jit(solution)/shard_map/psum | solution.py:237
  907.7 639.2 %copy-start.11 = (bf16[2,128,8,72]{1,3,2,0:T(8,128)(2,1)S(1)}, bf16[2,128,8,72]{1,3,2,0:T(8,128)(2,1)}, u32[]{:S(2)}) copy-start(bf16[2,128,8,72]{1,3,2,0:T(8,128)(2,1)} %get-tuple-element.99) | copy-start | bytes 884740
  907.7 639.2 %copy-start.14 = (bf16[2,128,8,72]{1,3,2,0:T(8,128)(2,1)S(1)}, bf16[2,128,8,72]{1,3,2,0:T(8,128)(2,1)}, u32[]{:S(2)}) copy-start(bf16[2,128,8,72]{1,3,2,0:T(8,128)(2,1)} %get-tuple-element.97) | copy-start | bytes 884740
  907.7 639.2 %copy-start.25 = (bf16[2,128,8,72]{1,3,2,0:T(8,128)(2,1)S(1)}, bf16[2,128,8,72]{1,3,2,0:T(8,128)(2,1)}, u32[]{:S(2)}) copy-start(bf16[2,128,8,72]{1,3,2,0:T(8,128)(2,1)} %get-tuple-element.98) | copy-start | bytes 884740
  913.4 633.6 %copy-start.20 = (bf16[2,128,1152]{2,1,0:T(8,128)(2,1)S(1)}, bf16[2,128,1152]{2,1,0:T(8,128)(2,1)}, u32[]{:S(2)}) copy-start(bf16[2,128,1152]{2,1,0:T(8,128)(2,1)} %copy-done.19) | copy-start | bytes 1769476
  1546.9 815.3 %all-reduce.15.cloned.1.call-start = ((), (), s32[]{:S(2)}) async-start(), calls=%async_computation.16 | async-start | bytes 29491200
  1567.5 619.8 %copy-start.58 = (u32[128]{0:T(128)S(1)}, u32[128]{0:T(128)}, u32[]{:S(2)}) copy-start(u32[128]{0:T(128)} %constant.110) | copy-start | bytes 1540
  2016.1 6.6 collective-permute-start.31
  2017.4 24.2 %collective-permute-start.15 = (f32[18,2304]{1,0:T(8,128)S(1)}, f32[18,2304]{1,0:T(8,128)S(1)}, u32[]{:S(2)}, u32[]{:S(2)}) collective-permute-start(f32[18,2304]{1,0:T(8,128)S(1)} %slice.53), channel_id=1, source_target_pairs={{0,32},{2,34},{4,36},{6,38},{8,40},{10,42},{12,44},{14,46},{16,48}... | collective-permute-start | bytes 497672
  2018.8 26.2 %collective-permute-start.14 = (f32[24,2304]{1,0:T(8,128)S(1)}, f32[24,2304]{1,0:T(8,128)S(1)}, u32[]{:S(2)}, u32[]{:S(2)}) collective-permute-start(f32[24,2304]{1,0:T(8,128)S(1)} %get-tuple-element.214), channel_id=1, source_target_pairs={{0,30},{2,32},{4,34},{6,36},{8,38},{10,40},{12,42},{14,44},{16,46}... | collective-permute-start | bytes 663560
  2020.1 26.2 %collective-permute-start.13 = (f32[24,2304]{1,0:T(8,128)S(1)}, f32[24,2304]{1,0:T(8,128)S(1)}, u32[]{:S(2)}, u32[]{:S(2)}) collective-permute-start(f32[24,2304]{1,0:T(8,128)S(1)} %get-tuple-element.214), channel_id=1, source_target_pairs={{0,28},{2,30},{4,32},{6,34},{8,36},{10,38},{12,40},{14,42},{16,44}... | collective-permute-start | bytes 663560
  2021.4 26.2 %collective-permute-start.12 = (f32[24,2304]{1,0:T(8,128)S(1)}, f32[24,2304]{1,0:T(8,128)S(1)}, u32[]{:S(2)}, u32[]{:S(2)}) collective-permute-start(f32[24,2304]{1,0:T(8,128)S(1)} %get-tuple-element.214), channel_id=1, source_target_pairs={{0,26},{2,28},{4,30},{6,32},{8,34},{10,36},{12,38},{14,40},{16,42}... | collective-permute-start | bytes 663560
  2022.7 26.2 %collective-permute-start.11 = (f32[24,2304]{1,0:T(8,128)S(1)}, f32[24,2304]{1,0:T(8,128)S(1)}, u32[]{:S(2)}, u32[]{:S(2)}) collective-permute-start(f32[24,2304]{1,0:T(8,128)S(1)} %get-tuple-element.214), channel_id=1, source_target_pairs={{0,24},{2,26},{4,28},{6,30},{8,32},{10,34},{12,36},{14,38},{16,40}... | collective-permute-start | bytes 663560
  2041.7 17.0 collective-permute-start.10
  2045.0 30.8 %collective-permute-start.9 = (f32[24,2304]{1,0:T(8,128)S(1)}, f32[24,2304]{1,0:T(8,128)S(1)}, u32[]{:S(2)}, u32[]{:S(2)}) collective-permute-start(f32[24,2304]{1,0:T(8,128)S(1)} %get-tuple-element.214), channel_id=1, source_target_pairs={{0,20},{2,22},{4,24},{6,26},{8,28},{10,30},{12,32},{14,34},{16,36}... | collective-permute-start | bytes 663560
  2046.3 30.8 %collective-permute-start.8 = (f32[24,2304]{1,0:T(8,128)S(1)}, f32[24,2304]{1,0:T(8,128)S(1)}, u32[]{:S(2)}, u32[]{:S(2)}) collective-permute-start(f32[24,2304]{1,0:T(8,128)S(1)} %get-tuple-element.214), channel_id=1, source_target_pairs={{0,18},{2,20},{4,22},{6,24},{8,26},{10,28},{12,30},{14,32},{16,34}... | collective-permute-start | bytes 663560
  2047.6 131.0 %copy-start.28 = (f32[24,2304]{1,0:T(8,128)}, f32[24,2304]{1,0:T(8,128)S(1)}, u32[]{:S(2)}) copy-start(f32[24,2304]{1,0:T(8,128)S(1)} %collective-permute-done.12) | copy-start | bytes 663556
  2047.6 37.8 %collective-permute-start.7 = (f32[24,2304]{1,0:T(8,128)S(1)}, f32[24,2304]{1,0:T(8,128)S(1)}, u32[]{:S(2)}, u32[]{:S(2)}) collective-permute-start(f32[24,2304]{1,0:T(8,128)S(1)} %get-tuple-element.214), channel_id=1, source_target_pairs={{0,16},{2,18},{4,20},{6,22},{8,24},{10,26},{12,28},{14,30},{16,32}... | collective-permute-start | bytes 663560
  2048.9 138.1 %copy-start.29 = (f32[24,2304]{1,0:T(8,128)}, f32[24,2304]{1,0:T(8,128)S(1)}, u32[]{:S(2)}) copy-start(f32[24,2304]{1,0:T(8,128)S(1)} %collective-permute-done.11) | copy-start | bytes 663556
  2048.9 37.8 %collective-permute-start.6 = (f32[24,2304]{1,0:T(8,128)S(1)}, f32[24,2304]{1,0:T(8,128)S(1)}, u32[]{:S(2)}, u32[]{:S(2)}) collective-permute-start(f32[24,2304]{1,0:T(8,128)S(1)} %get-tuple-element.214), channel_id=1, source_target_pairs={{0,14},{2,16},{4,18},{6,20},{8,22},{10,24},{12,26},{14,28},{16,30}... | collective-permute-start | bytes 663560
  2058.7 128.4 %copy-start.30 = (f32[24,2304]{1,0:T(8,128)}, f32[24,2304]{1,0:T(8,128)S(1)}, u32[]{:S(2)}) copy-start(f32[24,2304]{1,0:T(8,128)S(1)} %collective-permute-done.10) | copy-start | bytes 663556
  2058.7 31.2 %collective-permute-start.5 = (f32[24,2304]{1,0:T(8,128)S(1)}, f32[24,2304]{1,0:T(8,128)S(1)}, u32[]{:S(2)}, u32[]{:S(2)}) collective-permute-start(f32[24,2304]{1,0:T(8,128)S(1)} %get-tuple-element.214), channel_id=1, source_target_pairs={{0,12},{2,14},{4,16},{6,18},{8,20},{10,22},{12,24},{14,26},{16,28}... | collective-permute-start | bytes 663560
  2075.8 111.3 %copy-start.31 = (f32[24,2304]{1,0:T(8,128)}, f32[24,2304]{1,0:T(8,128)S(1)}, u32[]{:S(2)}) copy-start(f32[24,2304]{1,0:T(8,128)S(1)} %collective-permute-done.9) | copy-start | bytes 663556
  2075.8 17.2 collective-permute-start.4
  2077.1 110.0 %copy-start.32 = (f32[24,2304]{1,0:T(8,128)}, f32[24,2304]{1,0:T(8,128)S(1)}, u32[]{:S(2)}) copy-start(f32[24,2304]{1,0:T(8,128)S(1)} %collective-permute-done.8) | copy-start | bytes 663556
  2077.1 23.3 collective-permute-start.3
  2085.4 101.7 %copy-start.33 = (f32[24,2304]{1,0:T(8,128)}, f32[24,2304]{1,0:T(8,128)S(1)}, u32[]{:S(2)}) copy-start(f32[24,2304]{1,0:T(8,128)S(1)} %collective-permute-done.7) | copy-start | bytes 663556
  2085.4 22.1 collective-permute-start.2
  2086.7 100.4 %copy-start.34 = (f32[24,2304]{1,0:T(8,128)}, f32[24,2304]{1,0:T(8,128)S(1)}, u32[]{:S(2)}) copy-start(f32[24,2304]{1,0:T(8,128)S(1)} %collective-permute-done.6) | copy-start | bytes 663556
  2086.8 22.1 collective-permute-start.1
  2089.9 97.2 %copy-start.35 = (f32[24,2304]{1,0:T(8,128)}, f32[24,2304]{1,0:T(8,128)S(1)}, u32[]{:S(2)}) copy-start(f32[24,2304]{1,0:T(8,128)S(1)} %collective-permute-done.5) | copy-start | bytes 663556
  2089.9 20.7 collective-permute-start
  2093.0 94.1 %copy-start.36 = (f32[24,2304]{1,0:T(8,128)}, f32[24,2304]{1,0:T(8,128)S(1)}, u32[]{:S(2)}) copy-start(f32[24,2304]{1,0:T(8,128)S(1)} %collective-permute-done.4) | copy-start | bytes 663556
  2093.0 58.4 %collective-permute-start.30 = (f32[2304,24]{0,1:T(8,128)S(1)}, f32[2304,24]{0,1:T(8,128)S(1)}, u32[]{:S(2)}, u32[]{:S(2)}) collective-permute-start(f32[2304,24]{0,1:T(8,128)S(1)} %get-tuple-element.215), channel_id=1, source_target_pairs={{0,30},{2,32},{4,34},{6,36},{8,38},{10,40},{12,42},{14,44},{16,46}... | collective-permute-start | bytes 663560
  2100.4 86.7 %copy-start.37 = (f32[24,2304]{1,0:T(8,128)}, f32[24,2304]{1,0:T(8,128)S(1)}, u32[]{:S(2)}) copy-start(f32[24,2304]{1,0:T(8,128)S(1)} %collective-permute-done.3) | copy-start | bytes 663556
  2100.4 52.3 %collective-permute-start.29 = (f32[2304,24]{0,1:T(8,128)S(1)}, f32[2304,24]{0,1:T(8,128)S(1)}, u32[]{:S(2)}, u32[]{:S(2)}) collective-permute-start(f32[2304,24]{0,1:T(8,128)S(1)} %get-tuple-element.215), channel_id=1, source_target_pairs={{0,28},{2,30},{4,32},{6,34},{8,36},{10,38},{12,40},{14,42},{16,44}... | collective-permute-start | bytes 663560
  2107.6 79.6 %copy-start.38 = (f32[24,2304]{1,0:T(8,128)}, f32[24,2304]{1,0:T(8,128)S(1)}, u32[]{:S(2)}) copy-start(f32[24,2304]{1,0:T(8,128)S(1)} %collective-permute-done.2) | copy-start | bytes 663556
  2107.6 46.4 %collective-permute-start.28 = (f32[2304,24]{0,1:T(8,128)S(1)}, f32[2304,24]{0,1:T(8,128)S(1)}, u32[]{:S(2)}, u32[]{:S(2)}) collective-permute-start(f32[2304,24]{0,1:T(8,128)S(1)} %get-tuple-element.215), channel_id=1, source_target_pairs={{0,26},{2,28},{4,30},{6,32},{8,34},{10,36},{12,38},{14,40},{16,42}... | collective-permute-start | bytes 663560
  2108.9 46.5 %collective-permute-start.27 = (f32[2304,24]{0,1:T(8,128)S(1)}, f32[2304,24]{0,1:T(8,128)S(1)}, u32[]{:S(2)}, u32[]{:S(2)}) collective-permute-start(f32[2304,24]{0,1:T(8,128)S(1)} %get-tuple-element.215), channel_id=1, source_target_pairs={{0,24},{2,26},{4,28},{6,30},{8,32},{10,34},{12,36},{14,38},{16,40}... | collective-permute-start | bytes 663560
  2110.6 54.0 %collective-permute-start.26 = (f32[2304,24]{0,1:T(8,128)S(1)}, f32[2304,24]{0,1:T(8,128)S(1)}, u32[]{:S(2)}, u32[]{:S(2)}) collective-permute-start(f32[2304,24]{0,1:T(8,128)S(1)} %get-tuple-element.215), channel_id=1, source_target_pairs={{0,22},{2,24},{4,26},{6,28},{8,30},{10,32},{12,34},{14,36},{16,38}... | collective-permute-start | bytes 663560
  2151.4 14.6 collective-permute-start.25
  2152.7 17.8 collective-permute-start.24
  2154.0 18.5 collective-permute-start.23
  2155.4 19.1 collective-permute-start.22
  2164.6 13.9 collective-permute-start.21
  2166.0 52.0 %collective-permute-start.20 = (f32[2304,24]{0,1:T(8,128)S(1)}, f32[2304,24]{0,1:T(8,128)}, u32[]{:S(2)}, u32[]{:S(2)}) collective-permute-start(f32[2304,24]{0,1:T(8,128)S(1)} %get-tuple-element.215), channel_id=1, source_target_pairs={{0,10},{2,12},{4,14},{6,16},{8,18},{10,20},{12,22},{14,24},{16,26}... | collective-permute-start | bytes 663560
  2170.5 47.4 %collective-permute-start.19 = (f32[2304,24]{0,1:T(8,128)S(1)}, f32[2304,24]{0,1:T(8,128)}, u32[]{:S(2)}, u32[]{:S(2)}) collective-permute-start(f32[2304,24]{0,1:T(8,128)S(1)} %get-tuple-element.215), channel_id=1, source_target_pairs={{0,8},{2,10},{4,12},{6,14},{8,16},{10,18},{12,20},{14,22},{16,24},... | collective-permute-start | bytes 663560
  2172.5 45.4 %collective-permute-start.18 = (f32[2304,24]{0,1:T(8,128)S(1)}, f32[2304,24]{0,1:T(8,128)}, u32[]{:S(2)}, u32[]{:S(2)}) collective-permute-start(f32[2304,24]{0,1:T(8,128)S(1)} %get-tuple-element.215), channel_id=1, source_target_pairs={{0,6},{2,8},{4,10},{6,12},{8,14},{10,16},{12,18},{14,20},{16,22},{... | collective-permute-start | bytes 663560
  2174.5 43.5 %collective-permute-start.17 = (f32[2304,24]{0,1:T(8,128)S(1)}, f32[2304,24]{0,1:T(8,128)}, u32[]{:S(2)}, u32[]{:S(2)}) collective-permute-start(f32[2304,24]{0,1:T(8,128)S(1)} %get-tuple-element.215), channel_id=1, source_target_pairs={{0,4},{2,6},{4,8},{6,10},{8,12},{10,14},{12,16},{14,18},{16,20},{1... | collective-permute-start | bytes 663560
  2178.6 39.4 %collective-permute-start.16 = (f32[2304,24]{0,1:T(8,128)S(1)}, f32[2304,24]{0,1:T(8,128)}, u32[]{:S(2)}, u32[]{:S(2)}) collective-permute-start(f32[2304,24]{0,1:T(8,128)S(1)} %get-tuple-element.215), channel_id=1, source_target_pairs={{0,2},{2,4},{4,6},{6,8},{8,10},{10,12},{12,14},{14,16},{16,18},{18... | collective-permute-start | bytes 663560
  2217.9 104.9 %copy-start.15 = (bf16[2,64,1152]{2,1,0:T(8,128)(2,1)S(1)}, bf16[2,64,1152]{2,1,0:T(8,128)(2,1)}, u32[]{:S(2)}) copy-start(bf16[2,64,1152]{2,1,0:T(8,128)(2,1)} %reduce-scatter.19.cloned.1.call-done) | copy-start | bytes 884740
  (48 other events, 828.4 us)
Sparse Core Ops, SparseCore 0:
  9.8 106.9 all-gather.12
  119.1 298.9 all-gather.8
  420.4 108.2 all-gather.10
  536.5 20.3 reduce-scatter.12
  558.6 109.0 all-gather.14
  669.4 108.4 all-gather.16
  798.4 17.8 reduce-scatter.16
  818.7 18.7 reduce-scatter.14
  866.2 19.5 reduce-scatter.18
  899.8 645.0 reduce-scatter.20
  1551.0 140.5 all-reduce.12
  1694.0 668.0 all-reduce.14
where the time goes:
time: 2380 us; the launch traced here: 2370 us
  waiting for transfers between devices  1470 us (62%)
  blocking collectives  566 us (24%)
  local copies, waits for them, and re-layouts  116 us (5%)
  starting transfers between devices  113 us (5%)
  matrix products  70.7 us (3%)
    unnamed x46, waiting for transfers between devices  725 us
    unnamed x1, blocking collectives  449 us
    all_gather x1, waiting for transfers between devices, local(): lax.all_gather(mod_part.astype(jnp.bfloat16), ('fsdp', 'tp'), axis=2, til...  299 us
    unnamed x34, starting transfers between devices  113 us
    all_gather x1, waiting for transfers between devices, local(): lax.all_gather(w_proj, 'fsdp', axis=1, tiled=True)  104 us
    all_gather x1, waiting for transfers between devices, local(): lax.all_gather(w_qkv, 'fsdp', axis=1, tiled=True)  97.3 us
    all_gather x1, waiting for transfers between devices, local(): lax.all_gather(w_down, 'fsdp', axis=1, tiled=True)  96 us
    all_gather x1, waiting for transfers between devices, local(): lax.all_gather(w_up, 'fsdp', axis=0, tiled=True)  95.1 us
  transfers between devices with their start and end apart: 44, of which 15 were waited for; matrix products, arithmetic and copies ran while one was open for 25% of the time, Pallas kernels for 0%

commit v1 on v0

--- a/solution.py
+++ b/solution.py
@@ -1,7 +1,428 @@
+import functools
+
 import jax
 import jax.numpy as jnp
 from jax import lax
+from jax.experimental import pallas as pl
+from jax.experimental.pallas import tpu as pltpu
 from jax.sharding import PartitionSpec as P
+
+MESH = pl.DeviceIdType.MESH
+OFFS = (0, 3, 1, 2)
+
+
+def place_of():
+    f = lax.axis_index("fsdp")
+    return f // 16, (f // 4) % 4, (f // 2) % 2, f % 2, lax.axis_index("tp")
+
+
+def peers(z, y, x, c, t):
+    def at(z, y, x, c):
+        return (z * 16 + y * 4 + x * 2 + c, t)
+
+    return {
+        "z": (at((z + 3) % 4, y, x, c), at((z + 1) % 4, y, x, c)),
+        "y": (at(z, (y + 3) % 4, x, c), at(z, (y + 1) % 4, x, c)),
+        "x": at(z, y, 1 - x, c),
+        "c": at(z, y, x, 1 - c),
+    }
+
+
+def greet(near):
+    barrier = pltpu.get_barrier_semaphore()
+    group = (*near["z"], *near["y"], near["x"], near["c"])
+    for peer in group:
+        pl.semaphore_signal(barrier, inc=1, device_id=peer, device_id_type=MESH)
+    pl.semaphore_wait(barrier, len(group))
+
+
+def gather_kernel(firsts, *refs):
+    n = len(firsts)
+    ins, outs = refs[:n], refs[n : 2 * n]
+    local_sem, send_sem, recv_sem, core_send, core_recv = refs[2 * n :]
+    z, y, x, c, t = place_of()
+    near = peers(z, y, x, c, t)
+    greet(near)
+    started = []
+
+    def spot(p, u, v):
+        return (c, u, v) if firsts[p] == "z" else (c, v, u)
+
+    def remote(src, dst, ssem, rsem, peer):
+        return pltpu.make_async_remote_copy(
+            src_ref=src, dst_ref=dst, send_sem=ssem, recv_sem=rsem, device_id=peer, device_id_type=MESH
+        )
+
+    def send(p, k, ref, peer, src=None):
+        cp = remote(ref if src is None else src, ref, send_sem.at[p, k], recv_sem.at[p, k], peer)
+        cp.start()
+        started.append(cp)
+
+    def arrive(p, k, ref):
+        remote(ref, ref, send_sem.at[p, k], recv_sem.at[p, k], near["x"]).wait_recv()
+
+    def share(p, k, ref):
+        cp = remote(ref, ref, core_send.at[p, k], core_recv.at[p, k], near["c"])
+        cp.start()
+        started.append(cp)
+
+    def axes(p):
+        if firsts[p] == "z":
+            return z, y, near["z"], near["y"]
+        return y, z, near["y"], near["z"]
+
+    locals_ = []
+    for p in range(n):
+        own = outs[p].at[c, z, y, x]
+        send(p, 0, own, near["x"], ins[p])
+        cp = pltpu.make_async_copy(ins[p], own, local_sem.at[p])
+        cp.start()
+        locals_.append(cp)
+    for p in range(n):
+        u, v, one, two = axes(p)
+        locals_[p].wait()
+        arrive(p, 0, outs[p].at[c, z, y, 1 - x])
+        pair = outs[p].at[spot(p, u, v)]
+        send(p, 1, pair, one[1])
+        send(p, 2, pair, one[0])
+        share(p, 0, pair)
+    for p in range(n):
+        u, v, one, two = axes(p)
+        pair = outs[p].at[spot(p, u, v)]
+        send(p, 5, pair, two[1])
+        send(p, 6, pair, two[0])
+    for p in range(n):
+        u, v, one, two = axes(p)
+        for k, way in ((1, 1), (2, 0)):
+            uu = (u + OFFS[k]) % 4
+            pair = outs[p].at[spot(p, uu, v)]
+            arrive(p, k, pair)
+            send(p, 2 + k, outs[p].at[(*spot(p, uu, v), 1 - way)], one[way])
+            send(p, 5 + 4 * k, pair, two[1])
+            send(p, 6 + 4 * k, pair, two[0])
+            share(p, 4 * k, pair)
+    for p in range(n):
+        u, v, one, two = axes(p)
+        uu = (u + 2) % 4
+        arrive(p, 3, outs[p].at[(*spot(p, uu, v), 0)])
+        arrive(p, 4, outs[p].at[(*spot(p, uu, v), 1)])
+        pair = outs[p].at[spot(p, uu, v)]
+        send(p, 17, pair, two[1])
+        send(p, 18, pair, two[0])
+        share(p, 12, pair)
+    for k in range(4):
+        for p in range(n):
+            u, v, one, two = axes(p)
+            uu = (u + OFFS[k]) % 4
+            for side, way in ((1, 1), (2, 0)):
+                vv = (v + OFFS[side]) % 4
+                pair = outs[p].at[spot(p, uu, vv)]
+                arrive(p, 4 + 4 * k + side, pair)
+                send(p, 6 + 4 * k + side, outs[p].at[(*spot(p, uu, vv), 1 - way)], two[way])
+                share(p, 4 * k + side, pair)
+    for k in range(4):
+        for p in range(n):
+            u, v, one, two = axes(p)
+            uu, vv = (u + OFFS[k]) % 4, (v + 2) % 4
+            arrive(p, 7 + 4 * k, outs[p].at[(*spot(p, uu, vv), 0)])
+            arrive(p, 8 + 4 * k, outs[p].at[(*spot(p, uu, vv), 1)])
+            share(p, 4 * k + 3, outs[p].at[spot(p, uu, vv)])
+    for p in range(n):
+        for k in range(16):
+            ref = outs[p].at[1 - c, k // 4, k % 4]
+            remote(ref, ref, core_send.at[p, k], core_recv.at[p, k], near["c"]).wait_recv()
+    for cp in started:
+        cp.wait_send()
+
+
+def gather_blocks(firsts, parts, collective_id):
+    n = len(parts)
+    return pl.pallas_call(
+        functools.partial(gather_kernel, firsts),
+        out_shape=[jax.ShapeDtypeStruct((2, 4, 4, 2) + part.shape, part.dtype) for part in parts],
+        in_specs=[pl.BlockSpec(memory_space=pl.ANY)] * n,
+        out_specs=[pl.BlockSpec(memory_space=pl.ANY)] * n,
+        scratch_shapes=[
+            pltpu.SemaphoreType.DMA((n,)),
+            pltpu.SemaphoreType.DMA((n, 21)),
+            pltpu.SemaphoreType.DMA((n, 21)),
+            pltpu.SemaphoreType.DMA((n, 16)),
+            pltpu.SemaphoreType.DMA((n, 16)),
+        ],
+        compiler_params=pltpu.CompilerParams(collective_id=collective_id, has_side_effects=True),
+    )(*parts)
+
+
+def add_into(dst, *srcs):
+    width = dst.shape[-1]
+
+    def step(i, carry):
+        cols = pl.ds(pl.multiple_of(i * 128, 128), 128)
+        lead = (slice(None),) * (len(dst.shape) - 1)
+        total = srcs[0][(*lead, cols)].astype(jnp.float32)
+        for src in srcs[1:]:
+            total = total + src[(*lead, cols)].astype(jnp.float32)
+        dst[(*lead, cols)] = total.astype(dst.dtype)
+        return carry
+
+    lax.fori_loop(0, width // 128, step, 0)
+
+
+def scatter_kernel(firsts, *refs):
+    n = len(firsts)
+    grads, outs = refs[:n], refs[n : 2 * n]
+    refs = refs[2 * n :]
+    twins, sums, inner, mids, outer, ends, last = (refs[i * n : (i + 1) * n] for i in range(7))
+    send_sem, recv_sem, core_send, core_recv = refs[7 * n :]
+    z, y, x, c, t = place_of()
+    near = peers(z, y, x, c, t)
+    greet(near)
+    started = []
+
+    def remote(src, dst, ssem, rsem, peer):
+        return pltpu.make_async_remote_copy(
+            src_ref=src, dst_ref=dst, send_sem=ssem, recv_sem=rsem, device_id=peer, device_id_type=MESH
+        )
+
+    def axes(p):
+        if firsts[p] == "z":
+            return z, y, near["z"], near["y"]
+        return y, z, near["y"], near["z"]
+
+    def spot(p, u, v):
+        return (u, v) if firsts[p] == "z" else (v, u)
+
+    def send(p, k, src, dst, peer):
+        cp = remote(src, dst, send_sem.at[p, k], recv_sem.at[p, k], peer)
+        cp.start()
+        started.append(cp)
+
+    def arrive(p, k, ref):
+        remote(ref, ref, send_sem.at[p, k], recv_sem.at[p, k], near["x"]).wait_recv()
+
+    order = (3, 2, 1, 0)
+    sides = (3, 2, 1, 0)
+    for side in sides:
+        for k in order:
+            for p in range(n):
+                u, v, one, two = axes(p)
+                at = spot(p, (u + OFFS[k]) % 4, (v + OFFS[side]) % 4)
+                j = 4 * k + side
+                cp = remote(
+                    grads[p].at[(1 - c, *at)], twins[p].at[at], core_send.at[p, j], core_recv.at[p, j], near["c"]
+                )
+                cp.start()
+                started.append(cp)
+
+    def combine(p, k, side):
+        u, v, one, two = axes(p)
+        at = spot(p, (u + OFFS[k]) % 4, (v + OFFS[side]) % 4)
+        j = 4 * k + side
+        twin = twins[p].at[at]
+        remote(twin, twin, core_send.at[p, j], core_recv.at[p, j], near["c"]).wait_recv()
+        add_into(sums[p].at[at], grads[p].at[(c, *at)], twin)
+
+    for k in order:
+        for p in range(n):
+            u, v, one, two = axes(p)
+            combine(p, k, 3)
+            src = sums[p].at[spot(p, (u + OFFS[k]) % 4, (v + 2) % 4)]
+            send(p, 6 * k, src.at[0], inner[p].at[k, 0], two[1])
+            send(p, 6 * k + 1, src.at[1], inner[p].at[k, 1], two[0])
+    for k in order:
+        for p in range(n):
+            u, v, one, two = axes(p)
+            combine(p, k, 2)
+            src = sums[p].at[spot(p, (u + OFFS[k]) % 4, (v + 1) % 4)]
+            send(p, 6 * k + 2, src.at[1], inner[p].at[k, 2], two[1])
+            combine(p, k, 1)
+            src = sums[p].at[spot(p, (u + OFFS[k]) % 4, (v + 3) % 4)]
+            send(p, 6 * k + 4, src.at[0], inner[p].at[k, 4], two[0])
+    for k in order:
+        for p in range(n):
+            u, v, one, two = axes(p)
+            arrive(p, 6 * k, inner[p].at[k, 0])
+            src = sums[p].at[spot(p, (u + OFFS[k]) % 4, (v + 1) % 4)].at[0]
+            add_into(src, src, inner[p].at[k, 0])
+            send(p, 6 * k + 3, src, inner[p].at[k, 3], two[1])
+            arrive(p, 6 * k + 1, inner[p].at[k, 1])
+            src = sums[p].at[spot(p, (u + OFFS[k]) % 4, (v + 3) % 4)].at[1]
+            add_into(src, src, inner[p].at[k, 1])
+            send(p, 6 * k + 5, src, inner[p].at[k, 5], two[0])
+    for k in order:
+        for p in range(n):
+            combine(p, k, 0)
+    for k in order:
+        for p in range(n):
+            u, v, one, two = axes(p)
+            own = sums[p].at[spot(p, (u + OFFS[k]) % 4, v)]
+            for j in range(2, 6):
+                arrive(p, 6 * k + j, inner[p].at[k, j])
+            add_into(mids[p].at[k, 0], own.at[0], inner[p].at[k, 3], inner[p].at[k, 4])
+            add_into(mids[p].at[k, 1], own.at[1], inner[p].at[k, 2], inner[p].at[k, 5])
+            if k == 3:
+                send(p, 24, mids[p].at[3, 0], outer[p].at[0], one[1])
+                send(p, 25, mids[p].at[3, 1], outer[p].at[1], one[0])
+            if k == 2:
+                send(p, 26, mids[p].at[2, 1], outer[p].at[2], one[1])
+            if k == 1:
+                send(p, 28, mids[p].at[1, 0], outer[p].at[4], one[0])
+    for p in range(n):
+        u, v, one, two = axes(p)
+        arrive(p, 24, outer[p].at[0])
+        add_into(mids[p].at[2, 0], mids[p].at[2, 0], outer[p].at[0])
+        send(p, 27, mids[p].at[2, 0], outer[p].at[3], one[1])
+        arrive(p, 25, outer[p].at[1])
+        add_into(mids[p].at[1, 1], mids[p].at[1, 1], outer[p].at[1])
+        send(p, 29, mids[p].at[1, 1], outer[p].at[5], one[0])
+    for p in range(n):
+        for j in range(2, 6):
+            arrive(p, 24 + j, outer[p].at[j])
+        add_into(ends[p].at[0], mids[p].at[0, 0], outer[p].at[3], outer[p].at[4])
+        add_into(ends[p].at[1], mids[p].at[0, 1], outer[p].at[2], outer[p].at[5])
+        send(p, 30, ends[p].at[1 - x], last[p], near["x"])
+    for p in range(n):
+        arrive(p, 30, last[p])
+        add_into(outs[p], ends[p].at[x], last[p])
+    for cp in started:
+        cp.wait_send()
+
+
+def scatter_blocks(firsts, parts, collective_id):
+    n = len(parts)
+    rows = [part.shape[4:] for part in parts]
+
+    def room(*lead):
+        return [pltpu.VMEM(lead + row, jnp.bfloat16) for row in rows]
+
+    return pl.pallas_call(
+        functools.partial(scatter_kernel, firsts),
+        out_shape=[jax.ShapeDtypeStruct(row, jnp.float32) for row in rows],
+        in_specs=[pl.BlockSpec(memory_space=pltpu.VMEM)] * n,
+        out_specs=[pl.BlockSpec(memory_space=pltpu.VMEM)] * n,
+        scratch_shapes=[
+            *room(4, 4, 2),
+            *room(4, 4, 2),
+            *room(4, 6),
+            *room(4, 2),
+            *room(6),
+            *room(2),
+            *room(),
+            pltpu.SemaphoreType.DMA((n, 31)),
+            pltpu.SemaphoreType.DMA((n, 31)),
+            pltpu.SemaphoreType.DMA((n, 16)),
+            pltpu.SemaphoreType.DMA((n, 16)),
+        ],
+        compiler_params=pltpu.CompilerParams(
+            collective_id=collective_id, has_side_effects=True, vmem_limit_bytes=60 * 1024 * 1024
+        ),
+    )(*parts)
+
+
+def everyone():
+    f, t = lax.axis_index("fsdp"), lax.axis_index("tp")
+    me = f * 2 + t
+    count = lax.axis_size("fsdp") * lax.axis_size("tp")
+
+    def peer(i):
+        other = lax.rem(me + i, count)
+        return other, (other // 2, other % 2)
+
+    return me, count, peer
+
+
+def greet_all(count, peer):
+    barrier = pltpu.get_barrier_semaphore()
+
+    def hello(i, carry):
+        pl.semaphore_signal(barrier, inc=1, device_id=peer(i)[1], device_id_type=MESH)
+        return carry
+
+    lax.fori_loop(1, count, hello, 0)
+    pl.semaphore_wait(barrier, count - 1)
+
+
+def spread(count, peer, source, target, send_sem, recv_sem):
+    def go(i, carry):
+        other, where = peer(i)
+        pltpu.make_async_remote_copy(
+            src_ref=source(other),
+            dst_ref=target,
+            send_sem=send_sem,
+            recv_sem=recv_sem,
+            device_id=where,
+            device_id_type=MESH,
+        ).start()
+        return carry
+
+    lax.fori_loop(1, count, go, 0)
+
+
+def settle(count, buffer, sem):
+    ref = buffer.at[pl.ds(0, count - 1)]
+    pltpu.make_async_copy(ref, ref, sem).wait()
+
+
+def exchange_kernel(halve, in_ref, out_ref, send_sem, recv_sem):
+    me, count, peer = everyone()
+    greet_all(count, peer)
+
+    def source(other):
+        return in_ref.at[other // 2 if halve else other]
+
+    spread(count, peer, source, out_ref.at[me], send_sem, recv_sem)
+    out_ref[me] = source(me)[...]
+    settle(count, out_ref, recv_sem)
+    settle(count, out_ref, send_sem)
+
+
+def exchange(parts, halve, count, collective_id):
+    return pl.pallas_call(
+        functools.partial(exchange_kernel, halve),
+        out_shape=jax.ShapeDtypeStruct((count,) + parts.shape[1:], parts.dtype),
+        in_specs=[pl.BlockSpec(memory_space=pltpu.VMEM)],
+        out_specs=pl.BlockSpec(memory_space=pltpu.VMEM),
+        scratch_shapes=[pltpu.SemaphoreType.DMA, pltpu.SemaphoreType.DMA],
+        compiler_params=pltpu.CompilerParams(collective_id=collective_id, has_side_effects=True),
+    )(parts)
+
+
+def total_kernel(in_ref, out_ref, held, mine, send_one, recv_one, send_two, recv_two):
+    me, count, peer = everyone()
+    greet_all(count, peer)
+    spread(count, peer, lambda other: in_ref.at[other], held.at[me], send_one, recv_one)
+    held[me] = in_ref[me]
+    settle(count, held, recv_one)
+
+    def add(i, total):
+        return total + held[i]
+
+    total = lax.fori_loop(0, count, add, jnp.zeros(mine.shape, jnp.float32))
+    mine[...] = total
+    out_ref[me] = total
+    spread(count, peer, lambda other: mine, out_ref.at[me], send_two, recv_two)
+    settle(count, out_ref, recv_two)
+    settle(count, held, send_one)
+    settle(count, out_ref, send_two)
+
+
+def total_everywhere(parts, collective_id):
+    return pl.pallas_call(
+        total_kernel,
+        out_shape=jax.ShapeDtypeStruct(parts.shape, parts.dtype),
+        in_specs=[pl.BlockSpec(memory_space=pltpu.VMEM)],
+        out_specs=pl.BlockSpec(memory_space=pltpu.VMEM),
+        scratch_shapes=[
+            pltpu.VMEM(parts.shape, parts.dtype),
+            pltpu.VMEM(parts.shape[1:], parts.dtype),
+            pltpu.SemaphoreType.DMA,
+            pltpu.SemaphoreType.DMA,
+            pltpu.SemaphoreType.DMA,
+            pltpu.SemaphoreType.DMA,
+        ],
+        compiler_params=pltpu.CompilerParams(collective_id=collective_id, has_side_effects=True),
+    )(parts)
+
 
 HEAD_DIM = 72
 
@@ -28,6 +449,75 @@
     return lax.psum_scatter(
         terms.astype(jnp.bfloat16), "tp", scatter_dimension=1, tiled=True
     ).astype(jnp.float32)
+
+FIRSTS = ("z", "y")
+MAIN = 1024
+CHUNK = 896
+LEFT = 3968
+
+
+def shuffle_matrix(width):
+    place = jnp.arange(width, dtype=jnp.int32)
+    tail = place - MAIN
+    block = jnp.where(place < MAIN, place // 16, tail // 2)
+    row = jnp.where(place < MAIN, place % 16, 16 + tail % 2)
+    fsdp = ((block // 8) % 4) * 16 + ((block // 2) % 4) * 4 + (block % 2) * 2 + block // 32
+    source = fsdp * 18 + row
+    return (jnp.arange(width, dtype=jnp.int32)[:, None] == source[None, :]).astype(jnp.bfloat16)
+
+
+def shuffled(rows, matrix):
+    return jnp.einsum("...d,de->...e", rows, matrix, preferred_element_type=jnp.float32).astype(jnp.bfloat16)
+
+
+def shuffled_wide(rows, matrix):
+    return jnp.einsum("...d,de->...e", rows, matrix.astype(jnp.float32), precision=highest)
+
+
+def straight(rows, matrix):
+    return jnp.einsum("...e,de->...d", rows, matrix, preferred_element_type=jnp.float32).astype(jnp.bfloat16)
+
+
+def straight_wide(rows, matrix):
+    return jnp.einsum("...e,de->...d", rows, matrix.astype(jnp.float32), precision=highest)
+
+
+def pack_rows(all_rows):
+    main, tail = all_rows[:16], all_rows[16:]
+    tail = jnp.pad(tail, ((0, 0), (0, 8 * CHUNK - tail.shape[1]))).reshape(16, CHUNK)
+    whole = jnp.concatenate([tail, main], axis=1)
+    return whole[:, :LEFT], whole[:, LEFT:]
+
+
+def unpack_rows(left, right, width):
+    whole = jnp.concatenate([left, right], axis=1)
+    return jnp.concatenate([whole[:, CHUNK:], whole[:, :CHUNK].reshape(2, 8 * CHUNK)[:, :width]], axis=0)
+
+
+def unpack_all(left, right, width):
+    left, right = left.reshape(MAIN, -1), right.reshape(MAIN, -1)
+    tail = left[:, :CHUNK].reshape(128, 8 * CHUNK)[:, :width]
+    third = width // 3
+    most = third - (right.shape[1] - third)
+    one = jnp.concatenate([left[:, CHUNK : CHUNK + third], tail[:, :third]], axis=0)
+    two = jnp.concatenate(
+        [
+            jnp.concatenate([left[:, CHUNK + third :], right[:, : right.shape[1] - third]], axis=1),
+            tail[:, third : 2 * third],
+        ],
+        axis=0,
+    )
+    three = jnp.concatenate([right[:, right.shape[1] - third :], tail[:, 2 * third :]], axis=0)
+    return one, two, three
+
+
+def pack_all(grads):
+    whole = jnp.concatenate(grads, axis=1)
+    main, tail = whole[:MAIN], whole[MAIN:]
+    tail = jnp.pad(tail, ((0, 0), (0, 8 * CHUNK - tail.shape[1]))).reshape(MAIN, CHUNK)
+    whole = jnp.concatenate([tail, main], axis=1)
+    shape = (2, 4, 4, 2, 16)
+    return whole[:, :LEFT].reshape(*shape, LEFT), whole[:, LEFT:].reshape(*shape, -1)
 
 
 def attend_forward(pieces):
@@ -91,33 +581,48 @@
     place = jnp.clip(before + slot_rank, 0, latent_count - 1)
     numbers = jnp.arange(latent_count, dtype=jnp.int32)
     owner = jnp.sum(jnp.where(numbers[None, :] == place[:, None], order[None, :], 0), axis=1)
-    choose = (numbers[None, :] == owner[:, None]).astype(jnp.float32)
+    offsets = jnp.cumsum(counts) - counts
+    every = jnp.clip(offsets[:, None] + slot_rank[None, :], 0, latent_count - 1).reshape(-1)
+    owners = jnp.sum(jnp.where(numbers[None, :] == every[:, None], order[None, :], 0), axis=1)
+    choose_all = (numbers[None, :] == owners[:, None]).astype(jnp.bfloat16)
+    groups = counts.shape[0]
+    devices = groups * 2
+    matrix = shuffle_matrix(latents.shape[2])
     soft_cond = jax.nn.silu(condition.astype(jnp.float32))
     ada_local = w_ada.astype(jnp.float32)
     mod_part = jnp.einsum("nd,dke->nke", soft_cond, ada_local, precision=highest) + b_ada
-    mod_all = lax.all_gather(mod_part.astype(jnp.bfloat16), ("fsdp", "tp"), axis=2, tiled=True)
-    slot_mod = jnp.einsum("sn,nke->ske", choose, mod_all.astype(jnp.float32), precision=highest)
+    mod_low = mod_part.astype(jnp.bfloat16).reshape(latent_count, -1)
+    mod_send = jnp.dot(choose_all, mod_low, preferred_element_type=jnp.float32).astype(jnp.bfloat16)
+    columns = mod_part.shape[2]
+    mod_send = jnp.pad(mod_send.reshape(groups, slots, -1), ((0, 0), (0, 16 - slots), (0, 128 - 6 * columns)))
+    mod_got = exchange(mod_send, True, devices, 1)[:, :slots, : 6 * columns]
+    slot_mod = jnp.transpose(mod_got.reshape(devices, slots, 6, columns), (1, 2, 0, 3)).reshape(slots, 6, -1)
+    slot_mod = shuffled(slot_mod, matrix).astype(jnp.float32)
     shift_one = slot_mod[:, 0:1]
     scale_one = slot_mod[:, 1:2]
     gate_one = slot_mod[:, 2:3]
     shift_two = slot_mod[:, 3:4]
     scale_two = slot_mod[:, 4:5]
     gate_two = slot_mod[:, 5:6]
-    rows = latents.astype(jnp.float32)
-    qkv_all, proj_all = (
-        lax.all_gather(w_qkv, "fsdp", axis=1, tiled=True),
-        lax.all_gather(w_proj, "fsdp", axis=1, tiled=True),
-    )
+    rows = shuffled(latents, matrix).astype(jnp.float32)
+    cotangent = shuffled(cotangent, matrix)
+    b_proj, b_down = shuffled_wide(jnp.stack([b_proj, b_down]), matrix)
+    own_rows = jnp.concatenate([w_qkv[0], w_qkv[1], w_qkv[2], w_proj.T, w_up, w_down.T], axis=1)
+    width = own_rows.shape[1]
+    head_part = w_qkv.shape[2]
+    left, right = gather_blocks(FIRSTS, pack_rows(own_rows), 2)
+    inner_all, up_all, down_all = unpack_all(left, right, width)
+    qkv_all, proj_all = inner_all[:, : 3 * head_part], inner_all[:, 3 * head_part :]
     normed_one = widen(modulate(rows, shift_one, scale_one).astype(jnp.bfloat16))
     length = normed_one.shape[1]
     head_dim = HEAD_DIM
-    head_part = qkv_all.shape[2]
     head_count = head_part // head_dim
     bias_three = jnp.stack([b_qv[0], jnp.zeros_like(b_qv[0]), b_qv[1]])
     triple = (
-        jnp.einsum("bld,kde->kble", normed_one, qkv_all, preferred_element_type=jnp.float32)
-        + bias_three[:, None, None, :]
+        jnp.einsum("bld,de->ble", normed_one, qkv_all, preferred_element_type=jnp.float32)
+        + bias_three.reshape(-1)
     ).astype(jnp.bfloat16)
+    triple = [triple[..., i * head_part : (i + 1) * head_part] for i in range(3)]
     heads_shape = (slots, length, head_count, head_dim)
     queries = triple[0].reshape(heads_shape)
     keys = triple[1].reshape(heads_shape)
@@ -125,34 +630,30 @@
     attended_heads, log_total = lax.map(attend_forward, (queries, keys, values))
     attended = attended_heads.reshape(slots, length, head_part)
     branch = (
-        narrow(jnp.einsum("ble,ed->bld", attended, proj_all, preferred_element_type=jnp.float32))
+        narrow(jnp.einsum("ble,de->bld", attended, proj_all, preferred_element_type=jnp.float32))
         + b_proj
     )
     middle = rows + gate_one * branch
-    up_all, down_all = (
-        lax.all_gather(w_up, "fsdp", axis=0, tiled=True),
-        lax.all_gather(w_down, "fsdp", axis=1, tiled=True),
-    )
     normed_two = widen(modulate(middle, shift_two, scale_two).astype(jnp.bfloat16))
     upper = jnp.einsum("bld,df->blf", normed_two, up_all, preferred_element_type=jnp.float32) + b_up
     acted = gelu_tanh(upper).astype(jnp.bfloat16)
     down = (
-        narrow(jnp.einsum("blf,fd->bld", acted, down_all, preferred_element_type=jnp.float32))
+        narrow(jnp.einsum("blf,df->bld", acted, down_all, preferred_element_type=jnp.float32))
         + b_down
     )
     alive = live[:, None, None]
-    block_output = ((middle + gate_two * down) * alive).astype(jnp.bfloat16)
+    block_output = straight(((middle + gate_two * down) * alive).astype(jnp.bfloat16), matrix)
     grad_rows = cotangent.astype(jnp.float32) * alive
     grad_gate_two = jnp.sum(grad_rows * down, axis=1, keepdims=True)
     down_low = (gate_two * grad_rows).astype(jnp.bfloat16)
     grad_b_down = jnp.sum(down_low.astype(jnp.float32), axis=(0, 1))
     down_wide = widen(down_low)
     up_use, down_use = (up_all, down_all)
-    grad_acted = jnp.einsum("bld,fd->blf", down_wide, down_use, preferred_element_type=jnp.float32)
+    grad_acted = jnp.einsum("bld,df->blf", down_wide, down_use, preferred_element_type=jnp.float32)
     grad_upper = jax.vjp(gelu_tanh, upper)[1](grad_acted)[0]
     upper_low = grad_upper.astype(jnp.bfloat16)
     grad_b_up_local = jnp.sum(upper_low.astype(jnp.float32), axis=(0, 1))
-    grad_w_down = jnp.einsum("blf,bld->fd", acted, down_wide, preferred_element_type=jnp.float32)
+    grad_w_down = jnp.einsum("bld,blf->df", down_wide, acted, preferred_element_type=jnp.float32)
     grad_w_up = jnp.einsum("bld,blf->df", normed_two, upper_low, preferred_element_type=jnp.float32)
     grad_normed_two = narrow(
         jnp.einsum("blf,df->bld", upper_low, up_use, preferred_element_type=jnp.float32)
@@ -167,21 +668,22 @@
     branch_wide = widen(branch_low)
     qkv_use, proj_use = (qkv_all, proj_all)
     grad_attended = jnp.einsum(
-        "bld,ed->ble", branch_wide, proj_use, preferred_element_type=jnp.float32
+        "bld,de->ble", branch_wide, proj_use, preferred_element_type=jnp.float32
     ).astype(jnp.bfloat16)
     grad_w_proj = jnp.einsum(
-        "ble,bld->ed", attended, branch_wide, preferred_element_type=jnp.float32
+        "bld,ble->de", branch_wide, attended, preferred_element_type=jnp.float32
     )
     grad_queries, grad_keys, grad_values = lax.map(
         attend_backward, (queries, keys, values, log_total, grad_attended.reshape(heads_shape))
     )
     flat_shape = (slots, length, head_part)
-    grad_triple = jnp.stack(
+    grad_triple = jnp.concatenate(
         [
             grad_queries.reshape(flat_shape),
             grad_keys.reshape(flat_shape),
             grad_values.reshape(flat_shape),
-        ]
+        ],
+        axis=-1,
     )
     grad_b_qv_local = jnp.stack(
         [
@@ -190,21 +692,24 @@
         ]
     )
     grad_w_qkv = jnp.einsum(
-        "bld,kble->kde", normed_one, grad_triple, preferred_element_type=jnp.float32
+        "bld,ble->de", normed_one, grad_triple, preferred_element_type=jnp.float32
     )
     grad_normed_one = narrow(
-        jnp.einsum("kble,kde->bld", grad_triple, qkv_use, preferred_element_type=jnp.float32)
+        jnp.einsum("ble,de->bld", grad_triple, qkv_use, preferred_element_type=jnp.float32)
     )
     grad_rows_norm, grad_shift_one, grad_scale_one = jax.vjp(modulate, rows, shift_one, scale_one)[
         1
     ](grad_normed_one)
-    grad_latents = grad_middle + grad_rows_norm
-    grad_w_qkv, grad_w_proj, grad_w_up, grad_w_down = (
-        lax.psum_scatter(grad_w_qkv, "fsdp", scatter_dimension=1, tiled=True),
-        lax.psum_scatter(grad_w_proj, "fsdp", scatter_dimension=1, tiled=True),
-        lax.psum_scatter(grad_w_up, "fsdp", scatter_dimension=0, tiled=True),
-        lax.psum_scatter(grad_w_down, "fsdp", scatter_dimension=1, tiled=True),
-    )
+    grad_latents = straight_wide(grad_middle + grad_rows_norm, matrix)
+    packed = pack_all(
+        [grads.astype(jnp.bfloat16) for grads in (grad_w_qkv, grad_w_proj, grad_w_up, grad_w_down)]
+    )
+    summed = unpack_rows(*scatter_blocks(FIRSTS, packed, 3), width)
+    grad_w_qkv = jnp.stack([summed[:, i * head_part : (i + 1) * head_part] for i in range(3)])
+    grad_w_proj = summed[:, 3 * head_part : 4 * head_part].T
+    up_part = w_up.shape[1]
+    grad_w_up = summed[:, 4 * head_part : 4 * head_part + up_part]
+    grad_w_down = summed[:, 4 * head_part + up_part :].T
     grad_mod = jnp.concatenate(
         [
             grad_shift_one,
@@ -216,8 +721,18 @@
         ],
         axis=1,
     )
-    grad_table = jnp.einsum("sn,ske->nke", choose, grad_mod, precision=highest)
-    grad_mod_part = lax.psum_scatter(grad_table, ("fsdp", "tp"), scatter_dimension=2, tiled=True)
+    grad_mod = straight_wide(grad_mod, matrix).reshape(slots, 6, devices, columns)
+    grad_send = jnp.transpose(grad_mod, (2, 0, 1, 3)).reshape(devices, slots, 6 * columns)
+    grad_send = jnp.pad(grad_send, ((0, 0), (0, 8 - slots), (0, 128 - 6 * columns)))
+    grad_got = exchange(grad_send, False, devices, 4)[:, :slots, : 6 * columns]
+    grad_got = jnp.sum(grad_got.reshape(groups, 2, slots, 6 * columns), axis=1).reshape(groups * slots, -1)
+    alive_all = (slot_rank[None, :] < counts[:, None]).reshape(-1, 1)
+    grad_mod_part = jnp.einsum(
+        "sn,se->ne",
+        choose_all.astype(jnp.float32),
+        jnp.where(alive_all, grad_got, 0.0),
+        precision=highest,
+    ).reshape(latent_count, 6, columns)
     grad_b_ada = jnp.sum(grad_mod_part, axis=0)
     grad_w_ada = jnp.einsum("nd,nke->dke", soft_cond, grad_mod_part, precision=highest)
     grad_soft_part = jnp.einsum("nke,dke->nd", grad_mod_part, ada_local, precision=highest)
@@ -234,9 +749,16 @@
         grad_b_up_local,
         (tensor_rank * up_half,),
     )
-    grad_soft, grad_b_proj, grad_b_down, qv_full, up_full = lax.psum(
-        (grad_soft_part, grad_b_proj, grad_b_down, qv_place, up_place), ("fsdp", "tp")
-    )
+    sums = [grad_soft_part, grad_b_proj, grad_b_down, qv_place, up_place]
+    flat = jnp.concatenate([each.reshape(-1) for each in sums])
+    flat = jnp.pad(flat, (0, devices * 1024 - flat.shape[0])).reshape(devices, 8, 128)
+    flat = total_everywhere(flat, 5).reshape(-1)
+    parts, start = [], 0
+    for each in sums:
+        parts.append(flat[start : start + each.size].reshape(each.shape))
+        start += each.size
+    grad_soft, grad_b_proj, grad_b_down, qv_full, up_full = parts
+    grad_b_proj, grad_b_down = straight_wide(jnp.stack([grad_b_proj, grad_b_down]), matrix)
     grad_b_qv = lax.dynamic_slice_in_dim(qv_full, tensor_rank * head_part, head_part, 1)
     grad_b_up = lax.dynamic_slice_in_dim(up_full, tensor_rank * up_half, up_half, 0)
     grad_condition = jax.vjp(jax.nn.silu, condition.astype(jnp.float32))[1](grad_soft)[0]

time: 2380 us -> 480 us (0.20)
  waiting for transfers between devices: 1470 us -> 20.4 us
  blocking collectives: 566 us -> 38.1 us
  Pallas kernels: 0 us -> 189 us
  starting transfers between devices: 113 us -> 0.63 us
    unnamed x46 -> x4, waiting for transfers between devices: 725 us -> 0.07 us
    all_gather x5 -> x0, waiting for transfers between devices: 691 us -> none  [the longest x1 299 us: local(): lax.all_gather(mod_part.astype(jnp.bfloat16), ('fsdp', 'tp'), axis=2, til...]
    unnamed x1 -> x0, blocking collectives: 449 us -> none
    pallas_call x0 -> x5, Pallas kernels: none -> 189 us  [the longest x1 64.8 us: scatter_blocks(): pl.pallas_call(functools.partial(scatter_kernel, firsts), out_shape=[jax....]
    unnamed x34 -> x0, starting transfers between devices: 113 us -> none
    unnamed x132 -> x170, local copies, waits for them, and re-layouts: 87 us -> 11 us
    psum x1 -> x0, blocking collectives: 70.8 us -> none  [local(): lax.psum((grad_soft_part, grad_b_proj, grad_b_down, qv_place, up_place),...]
    slice x1 -> x20, local copies, waits for them, and re-layouts: 0.06 us -> 38.6 us  [the longest x3 12.9 us: pack_all(): main, tail = (whole[:MAIN], whole[MAIN:])]
  transfers between devices with their start and end apart: 44 -> 4, of which waited for: 15 -> 2; matrix products, arithmetic and copies ran while one was open for 25% -> 13% of each run, Pallas kernels for 0% -> 14%
where the time goes in v1:
time: 480 us; the launch traced here: 471 us
  Pallas kernels  189 us (39%)
  local copies, waits for them, and re-layouts  105 us (22%)
  matrix products  64 us (13%)
  blocking collectives  38.1 us (8%)
  other arithmetic  37.6 us (8%)
  waiting for transfers between devices  20.4 us (4%)
  between operations  15.2 us (3%)
    pallas_call x1, Pallas kernels, scatter_blocks(): pl.pallas_call(functools.partial(scatter_kernel, firsts), out_shape=[jax....  64.8 us
    pallas_call x1, Pallas kernels, gather_blocks(): pl.pallas_call(functools.partial(gather_kernel, firsts), out_shape=[jax.S...  62.4 us
    all_gather x4, blocking collectives, widen(): return lax.all_gather(rows, 'tp', axis=1, tiled=True)  38.1 us
    pallas_call x2, Pallas kernels, exchange(): pl.pallas_call(functools.partial(exchange_kernel, halve), out_shape=jax.S...  33.8 us
    pallas_call x1, Pallas kernels, total_everywhere(): pl.pallas_call(total_kernel, out_shape=jax.ShapeDtypeStruct(parts.shape,...  27.9 us
    concatenate x1, local copies, waits for them, and re-layouts, pack_all(): whole = jnp.concatenate(grads, axis=1)  25 us
    reduce_scatter x4, waiting for transfers between devices, narrow(): lax.psum_scatter(terms.astype(jnp.bfloat16), 'tp', scatter_dimension=1, t...  20.3 us
    slice x3, local copies, waits for them, and re-layouts, pack_all(): main, tail = (whole[:MAIN], whole[MAIN:])  12.9 us
  transfers between devices with their start and end apart: 4, of which 2 were waited for; matrix products, arithmetic and copies ran while one was open for 13% of the time, Pallas kernels for 14%

profile of v1, /device:TPU:1, one launch (start us, length us, event | category | flops | bytes accessed | tf_op | source)
XLA Modules:
  0.0 470.5 jit_solution(517883136774985623)
XLA Ops:
  8.1 1.5 pad_maximum_fusion.11.refs_1_
  9.6 1.1 concatenate.45
  11.5 62.4 %shard_map.247 = (bf16[2,4,4,2,16,3968]{5,4,3,2,1,0:T(8,128)(2,1)}, bf16[2,4,4,2,16,3840]{5,4,3,2,1,0:T(8,128)(2,1)}) custom-call(bf16[16,3968]{1,0:T(8,128)(2,1)} %pad_maximum_fusion.10.refs_0_, bf16[16,3840]{1,0:T(8,128)(2,1)} %pad_maximum_fusion.11.refs_1_), custom_call_target="tpu_custom_call" | custom-call | tf_op jit(solution)/shard_map/pallas_call | solution.py:140
  73.9 1.6 slice.207
  75.6 4.8 %slice.206 = bf16[1024,2304]{1,0:T(8,128)(2,1)} slice(bf16[1024,3968]{1,0:T(8,128)(2,1)} %bitcast.278), slice={[0:1024], [896:3200]} | slice | bytes 9437184 | tf_op jit(solution)/shard_map/slice | solution.py:502
  83.5 16.5 %shard_map.246 = bf16[128,16,128]{2,1,0:T(8,128)(2,1)} custom-call(bf16[64,16,128]{2,1,0:T(8,128)(2,1)} %pad.20.in_ref), custom_call_target="tpu_custom_call" | custom-call | tf_op jit(solution)/shard_map/pallas_call | solution.py:380
  103.0 1.2 fusion.216
  105.3 10.2 %all_gather.12 = bf16[2,128,1152]{2,1,0:T(8,128)(2,1)} all-gather(bf16[2,64,1152]{2,1,0:T(8,128)(2,1)S(1)} %add_convert_fusion.1), channel_id=1, replica_groups=mesh['fsdp'=64,'tp'=2] {'tp'}, dimensions={1}, use_global_device_ids=true | all-gather | bytes 884736 | tf_op jit(solution)/shard_map/all_gather | solution.py:445
  115.5 6.7 %copy.98 = bf16[1024,2304]{0,1:T(8,128)(2,1)} copy(bf16[1024,2304]{1,0:T(8,128)(2,1)} %slice.206) | data formatting | bytes 9437184
  122.2 1.8 reshape.416
  124.0 2.6 fusion.211
  126.9 1.6 fusion.114
  128.5 1.2 copy-done.2
  129.9 1.7 fusion.76
  131.7 1.4 while.26
  133.2 1.5 convolution_convert_fusion.3
  135.0 2.7 slice.217
  137.7 3.7 slice.218
  141.4 4.9 %slice.220 = bf16[1024,2304]{1,0:T(8,128)(2,1)} slice(bf16[1024,3840]{1,0:T(8,128)(2,1)} %bitcast.281), slice={[0:1024], [1536:3840]} | slice | bytes 9437184 | tf_op jit(solution)/shard_map/slice | solution.py:510
  147.7 1.7 fusion.45
  150.1 2.6 convert_reduce_fusion.5
  152.6 9.1 %all_gather.14 = bf16[2,128,1152]{2,1,0:T(8,128)(2,1)} all-gather(bf16[2,64,1152]{2,1,0:T(8,128)(2,1)S(1)} %get-tuple-element.188), channel_id=1, replica_groups=mesh['fsdp'=64,'tp'=2] {'tp'}, dimensions={1}, use_global_device_ids=true | all-gather | bytes 884736 | tf_op jit(solution)/shard_map/all_gather | solution.py:445
  161.8 1.3 fusion.209
  164.1 8.3 %all_gather.13 = bf16[2,128,1152]{2,1,0:T(8,128)(2,1)S(1)} all-gather(bf16[2,64,1152]{2,1,0:T(8,128)(2,1)S(1)} %add_convert_fusion), channel_id=1, replica_groups=mesh['fsdp'=64,'tp'=2] {'tp'}, dimensions={1}, use_global_device_ids=true | all-gather | bytes 884736 | tf_op jit(solution)/shard_map/all_gather | solution.py:445
  172.4 4.4 convolution_add_fusion
  176.9 3.1 convert_reduce_fusion
  180.1 1.1 copy-done.13
  181.1 5.3 %fusion.74 = bf16[2,128,1152]{2,1,0:T(8,128)(2,1)} fusion(bf16[2,128,2304]{2,1,0:T(8,128)(2,1)S(1)} %get-tuple-element.230, bf16[128,2304]{1,0:T(8,128)(2,1)S(1)} %copy-done.21, bf16[1024,1536]{1,0:T(8,128)(2,1)S(1)} %copy-done.4, bf16[1024,768]{1,0:T(8,128)(2,1)S(1)} %copy-done.11), kind=kOutput, calls=%fused_computation.95 | convolution fusion | flops 1375174656 | bytes 7077888 | tf_op jit(solution)/shard_map/blf,df->bld/dot_general | solution.py:659
  186.8 5.3 %fusion.42 = bf16[1152,2304]{1,0:T(8,128)(2,1)} fusion(bf16[2,128,1152]{2,1,0:T(8,128)(2,1)S(1)} %all_gather.13, bf16[2,128,2304]{2,1,0:T(8,128)(2,1)} %copy-done.13), kind=kOutput, calls=%fused_computation.56 | convolution fusion | flops 1361608704 | bytes 7077888 | tf_op jit(solution)/shard_map/bld,blf->df/dot_general | solution.py:657
  192.1 4.0 fusion.43
  196.2 2.9 fusion.75
  199.6 7.1 %pad_maximum_fusion.1 = bf16[1024,3840]{1,0:T(8,128)(2,1)} fusion(bf16[1152,2304]{1,0:T(8,128)(2,1)} %fusion.43, bf16[1152,2304]{1,0:T(8,128)(2,1)} %fusion.42), kind=kLoop, calls=%fused_computation.60 | loop fusion | flops 15728640 | bytes 18481152 | tf_op jit(solution)/shard_map/concatenate | solution.py:515
  206.6 1.7 reduce-scatter.9.cloned.1.call-done
  208.4 1.2 fusion.121
  209.6 2.0 fusion.122
  211.5 18.6 %reduce-scatter.7.cloned.1.call-done = bf16[2,64,1152]{2,1,0:T(8,128)(2,1)} async-done(((bf16[2,128,1152]{2,1,0:T(8,128)(2,1)}), bf16[2,64,1152]{2,1,0:T(8,128)(2,1)}) %reduce-scatter.7.cloned.1.call-update) | async-done | bytes 294928 | tf_op jit(solution)/shard_map/reduce_scatter | solution.py:449
  230.1 2.9 convert_reduce_fusion.6
  233.0 10.5 %all_gather.15 = bf16[2,128,1152]{2,1,0:T(8,128)(2,1)S(1)} all-gather(bf16[2,64,1152]{2,1,0:T(8,128)(2,1)S(1)} %get-tuple-element.190), channel_id=1, replica_groups=mesh['fsdp'=64,'tp'=2] {'tp'}, dimensions={1}, use_global_device_ids=true | all-gather | bytes 884736 | tf_op jit(solution)/shard_map/all_gather | solution.py:445
  243.6 1.9 convolution_convert_fusion.4
  245.5 1.6 fusion.64
  248.7 5.6 %while.27 = (s32[]{:T(128)}, bf16[2,128,8,72]{1,3,2,0:T(8,128)(2,1)}, bf16[2,128,8,72]{1,3,2,0:T(8,128)(2,1)}, bf16[2,128,8,72]{1,3,2,0:T(8,128)(2,1)S(1)}, bf16...) while((s32[]{:T(128)}, ...), condition=%wide.region_18.19_spmd, body=%wide.region_16.18_spmd.sunk | while | flops 95788032 | bytes 10151137 | solution.py:676
  254.5 1.2 convert_reduce_fusion.4
  255.7 4.5 convolution_convert_fusion.2
  260.2 3.2 fusion.44
  263.4 2.1 copy.82
  265.5 6.5 %copy.81 = bf16[1152,1728]{1,0:T(8,128)(2,1)} copy(bf16[1152,1728]{0,1:T(8,128)(2,1)} %fusion.44) | data formatting | bytes 7962624 | tf_op jit(solution)/shard_map/convert_element_type | solution.py:705
  272.0 25.0 %concatenate.55 = bf16[1152,6912]{1,0:T(8,128)(2,1)} concatenate(bf16[1152,1728]{1,0:T(8,128)(2,1)} %copy.81, bf16[1152,576]{1,0:T(8,128)(2,1)S(1)} %copy.82, bf16[1152,2304]{1,0:T(8,128)(2,1)} %fusion.42, bf16[1152,2304]{1,0:T(8,128)(2,1)} %fusion.43), dimensions={1} | concatenate | bytes 31850496 | tf_op jit(solution)/shard_map/concatenate | solution.py:515
  297.0 12.9 %slice.223 = bf16[1024,6912]{1,0:T(8,128)(2,1)} slice(bf16[1152,6912]{1,0:T(8,128)(2,1)} %concatenate.55), slice={[0:1024], [0:6912]} | slice | bytes 28311552 | tf_op jit(solution)/shard_map/slice | solution.py:516
  310.7 1.4 pad.24
  312.1 3.9 reshape.438
  316.0 7.0 %pad_maximum_fusion = bf16[1024,3968]{1,0:T(8,128)(2,1)} fusion(bf16[1024,6912]{1,0:T(8,128)(2,1)} %slice.223, bf16[1024,896]{1,0:T(8,128)(2,1)} %reshape.438), kind=kLoop, calls=%fused_computation.59 | loop fusion | flops 16252928 | bytes 24117248 | tf_op jit(solution)/shard_map/concatenate | solution.py:518
  323.1 64.8 %shard_map.250 = (f32[16,3968]{1,0:T(8,128)}, f32[16,3840]{1,0:T(8,128)}) custom-call(bf16[2,4,4,2,16,3968]{5,4,3,2,1,0:T(8,128)(2,1)} %bitcast.273, bf16[2,4,4,2,16,3840]{5,4,3,2,1,0:T(8,128)(2,1)} %bitcast.274), custom_call_target="tpu_custom_call" | custom-call | tf_op jit(solution)/shard_map/pallas_call | solution.py:298
  388.9 1.6 maximum_bitcast_fusion.12
  391.2 2.0 fusion.86
  394.0 1.2 fusion.120
  395.2 1.4 fusion.123
  396.7 2.5 fusion.48
  401.2 17.2 %shard_map.248 = f32[128,8,128]{2,1,0:T(8,128)} custom-call(f32[128,8,128]{2,1,0:T(8,128)} %pad.22.in_ref), custom_call_target="tpu_custom_call" | custom-call | tf_op jit(solution)/shard_map/pallas_call | solution.py:380
  418.5 1.1 bitcast_reduce_fusion
  420.7 1.3 fusion.134
  423.4 27.9 %shard_map.249 = f32[128,8,128]{2,1,0:T(8,128)} custom-call(f32[128,8,128]{2,1,0:T(8,128)} %pad_bitcast_fusion.in_ref), custom_call_target="tpu_custom_call" | custom-call | tf_op jit(solution)/shard_map/pallas_call | solution.py:410
  453.6 1.0 slice.183
  455.4 2.4 fusion.46
  460.1 3.7 fusion.50
  (318 shorter events, 34.9 us)
Async XLA Ops:
  7.2 142.9 %copy-start = (bf16[2,64,1152]{2,1,0:T(8,128)(2,1)S(1)}, bf16[2,64,1152]{2,1,0:T(8,128)(2,1)}, u32[]{:S(2)}) copy-start(bf16[2,64,1152]{2,1,0:T(8,128)(2,1)} %param.33) | copy-start | bytes 884740
  7.2 154.6 %reduce-scatter.5.cloned.1.call-start = ((), (), s32[]{:S(2)}) async-start(), calls=%async_computation.4 | async-start | bytes 884736 | tf_op jit(solution)/shard_map/reduce_scatter | solution.py:449
  7.3 142.8 %copy-start.65 = (s32[1152]{0:T(1024)}, s32[1152]{0:T(1024)S(1)}, u32[]{:S(2)}) copy-start(s32[1152]{0:T(1024)S(1)} %fusion.172) | copy-start | bytes 13828
  75.6 4.8 %copy-start.68 = (f32[2,576]{1,0:T(2,128)S(1)}, f32[2,576]{1,0:T(2,128)}, u32[]{:S(2)}) copy-start(f32[2,576]{1,0:T(2,128)} %param.26) | copy-start | bytes 13828
  75.6 5.1 %copy-start.27 = (bf16[1152,6,9]{0,1,2:T(8,128)(2,1)S(1)}, bf16[1152,6,9]{0,1,2:T(8,128)(2,1)}, u32[]{:S(2)}) copy-start(bf16[1152,6,9]{0,1,2:T(8,128)(2,1)} %param.23) | copy-start | bytes 373252
  75.6 5.1 %copy-start.33 = (bf16[96,1152]{1,0:T(8,128)(2,1)S(1)}, bf16[96,1152]{1,0:T(8,128)(2,1)}, u32[]{:S(2)}) copy-start(bf16[96,1152]{1,0:T(8,128)(2,1)} %param.20) | copy-start | bytes 663556
  75.6 5.1 %copy-start.74 = (f32[6,9]{1,0:T(8,128)S(1)}, f32[6,9]{1,0:T(8,128)}, u32[]{:S(2)}) copy-start(f32[6,9]{1,0:T(8,128)} %param.24) | copy-start | bytes 652
  81.2 21.9 %copy-start.73 = (bf16[2,64,1152]{2,1,0:T(8,128)(2,1)S(1)}, bf16[2,64,1152]{2,1,0:T(8,128)(2,1)}, u32[]{:S(2)}) copy-start(bf16[2,64,1152]{2,1,0:T(8,128)(2,1)} %param.19) | copy-start | bytes 884740
  104.3 17.9 %copy-start.51 = (f32[2,64]{1,0:T(2,128)}, f32[2,64]{1,0:T(2,128)S(1)}, u32[]{:S(2)}) copy-start(f32[2,64]{1,0:T(2,128)S(1)} %broadcast_multiply_fusion.1) | copy-start | bytes 1540
  104.5 17.6 %copy-start.61 = (f32[2,64]{1,0:T(2,128)}, f32[2,64]{1,0:T(2,128)S(1)}, u32[]{:S(2)}) copy-start(f32[2,64]{1,0:T(2,128)S(1)} %fusion.195) | copy-start | bytes 1540
  105.1 17.1 %copy-start.35 = (f32[2,1152]{1,0:T(2,128)}, f32[2,1152]{1,0:T(2,128)S(1)}, u32[]{:S(2)}) copy-start(f32[2,1152]{1,0:T(2,128)S(1)} %get-tuple-element.236) | copy-start | bytes 27652
  133.1 4.5 copy-start.5
  133.2 4.5 copy-start.43
  134.7 73.7 %reduce-scatter.9.cloned.1.call-start = ((), (), s32[]{:S(2)}) async-start(), calls=%async_computation.6 | async-start | bytes 884736 | tf_op jit(solution)/shard_map/reduce_scatter | solution.py:449
  141.4 4.9 %copy-start.63 = (f32[1152]{0:T(1024)S(1)}, f32[1152]{0:T(1024)}, u32[]{:S(2)}) copy-start(f32[1152]{0:T(1024)} %param.28) | copy-start | bytes 13828
  141.4 4.9 %copy-start.64 = (f32[1152]{0:T(1024)S(1)}, f32[1152]{0:T(1024)}, u32[]{:S(2)}) copy-start(f32[1152]{0:T(1024)} %param.32) | copy-start | bytes 13828
  147.6 14.2 %copy-start.76 = (f32[2]{0:T(128)}, f32[2]{0:T(128)S(1)}, u32[]{:S(2)}) copy-start(f32[2]{0:T(128)S(1)} %compare_convert_fusion) | copy-start | bytes 28
  147.7 14.1 %copy-start.59 = (f32[2,1,1152]{2,0,1:T(2,128)}, f32[2,1,1152]{2,0,1:T(2,128)S(1)}, u32[]{:S(2)}) copy-start(f32[2,1,1152]{2,0,1:T(2,128)S(1)} %copy.112) | copy-start | bytes 27652
  147.7 14.2 %copy-start.37 = (f32[2,1,1152]{2,0,1:T(2,128)}, f32[2,1,1152]{2,0,1:T(2,128)S(1)}, u32[]{:S(2)}) copy-start(f32[2,1,1152]{2,0,1:T(2,128)S(1)} %copy.113) | copy-start | bytes 27652
  150.0 13.1 %copy-start.41 = (f32[1152]{0:T(1024)}, f32[1152]{0:T(1024)S(1)}, u32[]{:S(2)}) copy-start(f32[1152]{0:T(1024)S(1)} %get-tuple-element.156) | copy-start | bytes 13828
  161.8 10.6 %copy-start.4 = (bf16[1024,1536]{1,0:T(8,128)(2,1)S(1)}, bf16[1024,1536]{1,0:T(8,128)(2,1)}, u32[]{:S(2)}) copy-start(bf16[1024,1536]{1,0:T(8,128)(2,1)} %slice.218) | copy-start | bytes 9437188
  164.1 12.7 %slice-start.1 = ((s8[4718592]{0:T(1024)(128)(4,1)}), s8[4194304]{0:T(1024)(128)(4,1)S(1)}, s32[]{:S(2)}) async-start(s8[4718592]{0:T(1024)(128)(4,1)} %bitcast.283), calls=%async_computation.9 | async-start | bytes 8388608
  172.4 4.5 slice-start.2
  172.4 4.5 copy-start.20
  172.4 4.5 copy-start.24
  176.9 4.2 copy-start.11
  186.5 43.6 %reduce-scatter.7.cloned.1.call-start = ((), (), s32[]{:S(2)}) async-start(), calls=%async_computation.5 | async-start | bytes 884736 | tf_op jit(solution)/shard_map/reduce_scatter | solution.py:449
  186.8 5.4 %copy-start.25 = (bf16[2,128,1152]{2,1,0:T(8,128)(2,1)S(1)}, bf16[2,128,1152]{2,1,0:T(8,128)(2,1)}, u32[]{:S(2)}) copy-start(bf16[2,128,1152]{2,1,0:T(8,128)(2,1)} %all_gather.14) | copy-start | bytes 1769476
  186.8 5.4 %copy-start.79 = (f32[2,128,2304]{2,1,0:T(8,128)S(1)}, f32[2,128,2304]{2,1,0:T(8,128)}, u32[]{:S(2)}) copy-start(f32[2,128,2304]{2,1,0:T(8,128)} %copy-done.78) | copy-start | bytes 7077892
  186.8 9.3 %slice-start.3 = ((s8[4718592]{0:T(1024)(128)(4,1)}), s8[4194304]{0:T(1024)(128)(4,1)S(1)}, s32[]{:S(2)}) async-start(s8[4718592]{0:T(1024)(128)(4,1)} %bitcast.285), calls=%async_computation.11 | async-start | bytes 8388608
  199.1 194.9 %reduce-scatter.11.cloned.1.call-start = ((), (), s32[]{:S(2)}) async-start(), calls=%async_computation.7 | async-start | bytes 884736 | tf_op jit(solution)/shard_map/reduce_scatter | solution.py:449
  199.5 7.1 %copy-start.39 = (f32[4608]{0:T(1024)}, f32[4608]{0:T(1024)S(1)}, u32[]{:S(2)}) copy-start(f32[4608]{0:T(1024)S(1)} %dynamic_update_slice.24) | copy-start | bytes 55300
  199.5 10.0 %copy-start.58 = (f32[2,64]{1,0:T(2,128)S(1)}, f32[2,64]{1,0:T(2,128)}, u32[]{:S(2)}) copy-start(f32[2,64]{1,0:T(2,128)} %copy-done.57) | copy-start | bytes 1540
  199.5 10.0 %copy-start.54 = (f32[2,64]{1,0:T(2,128)S(1)}, f32[2,64]{1,0:T(2,128)}, u32[]{:S(2)}) copy-start(f32[2,64]{1,0:T(2,128)} %copy-done.53) | copy-start | bytes 1540
  199.5 30.6 %copy-start.26 = (f32[2,64,1152]{2,1,0:T(8,128)S(1)}, f32[2,64,1152]{2,1,0:T(8,128)}, u32[]{:S(2)}) copy-start(f32[2,64,1152]{2,1,0:T(8,128)} %get-tuple-element.228) | copy-start | bytes 1769476
  199.5 30.6 %copy-start.38 = (f32[2,1,1152]{2,0,1:T(2,128)S(1)}, f32[2,1,1152]{2,0,1:T(2,128)}, u32[]{:S(2)}) copy-start(f32[2,1,1152]{2,0,1:T(2,128)} %copy-done.37) | copy-start | bytes 27652
  199.5 30.6 %copy-start.48 = (f32[1152]{0:T(1024)S(1)}, f32[1152]{0:T(1024)}, u32[]{:S(2)}) copy-start(f32[1152]{0:T(1024)} %get-tuple-element.155) | copy-start | bytes 13828
  230.1 15.4 %copy-start.6 = (bf16[2,128,8,72]{1,3,2,0:T(8,128)(2,1)S(1)}, bf16[2,128,8,72]{1,3,2,0:T(8,128)(2,1)}, u32[]{:S(2)}) copy-start(bf16[2,128,8,72]{1,3,2,0:T(8,128)(2,1)} %copy-done.5) | copy-start | bytes 884740
  243.6 5.1 %copy-start.44 = (f32[2,8,128]{2,1,0:T(8,128)S(1)}, f32[2,8,128]{2,1,0:T(8,128)}, u32[]{:S(2)}) copy-start(f32[2,8,128]{2,1,0:T(8,128)} %copy-done.43) | copy-start | bytes 24580
  248.7 7.0 %copy-start.8 = (bf16[128,2304]{0,1:T(8,128)(2,1)S(1)}, bf16[128,2304]{0,1:T(8,128)(2,1)}, u32[]{:S(2)}) copy-start(bf16[128,2304]{0,1:T(8,128)(2,1)} %copy-done.7) | copy-start | bytes 1769476
  255.7 4.5 copy-start.16
  255.7 4.5 copy-start.23
  255.7 4.5 copy-start.31
  297.0 13.0 %copy-start.47 = (f32[2,1152]{1,0:T(2,128)S(1)}, f32[2,1152]{1,0:T(2,128)}, u32[]{:S(2)}) copy-start(f32[2,1152]{1,0:T(2,128)} %get-tuple-element.147) | copy-start | bytes 27652
  297.0 13.0 %copy-start.9 = (f32[2,64,1152]{2,1,0:T(8,128)S(1)}, f32[2,64,1152]{2,1,0:T(8,128)}, u32[]{:S(2)}) copy-start(f32[2,64,1152]{2,1,0:T(8,128)} %get-tuple-element.191) | copy-start | bytes 1769476
  297.0 13.0 %copy-start.17 = (bf16[2,64,1152]{2,1,0:T(8,128)(2,1)S(1)}, bf16[2,64,1152]{2,1,0:T(8,128)(2,1)}, u32[]{:S(2)}) copy-start(bf16[2,64,1152]{2,1,0:T(8,128)(2,1)} %reduce-scatter.5.cloned.1.call-done) | copy-start | bytes 884740
  297.0 13.0 %copy-start.42 = (f32[1152]{0:T(1024)S(1)}, f32[1152]{0:T(1024)}, u32[]{:S(2)}) copy-start(f32[1152]{0:T(1024)} %copy-done.41) | copy-start | bytes 13828
  297.0 13.1 %copy-start.45 = (f32[2,1152]{1,0:T(2,128)S(1)}, f32[2,1152]{1,0:T(2,128)}, u32[]{:S(2)}) copy-start(f32[2,1152]{1,0:T(2,128)} %get-tuple-element.204) | copy-start | bytes 27652
  297.0 13.1 %copy-start.46 = (f32[2,1152]{1,0:T(2,128)S(1)}, f32[2,1152]{1,0:T(2,128)}, u32[]{:S(2)}) copy-start(f32[2,1152]{1,0:T(2,128)} %get-tuple-element.151) | copy-start | bytes 27652
  297.0 13.7 %slice-start = ((bf16[1152,6912]{1,0:T(8,128)(2,1)}), bf16[128,6912]{1,0:T(8,128)(2,1)S(1)}, s32[]{:S(2)}) async-start(bf16[1152,6912]{1,0:T(8,128)(2,1)} %concatenate.55), calls=%async_computation.8 | async-start | bytes 3538944 | tf_op jit(solution)/shard_map/slice | solution.py:516
  323.1 68.1 %copy-start.32 = (bf16[2,64,1152]{2,1,0:T(8,128)(2,1)S(1)}, bf16[2,64,1152]{2,1,0:T(8,128)(2,1)}, u32[]{:S(2)}) copy-start(bf16[2,64,1152]{2,1,0:T(8,128)(2,1)} %reduce-scatter.7.cloned.1.call-done) | copy-start | bytes 884740
  323.1 68.1 %copy-start.49 = (f32[1152]{0:T(1024)S(1)}, f32[1152]{0:T(1024)}, u32[]{:S(2)}) copy-start(f32[1152]{0:T(1024)} %get-tuple-element.155) | copy-start | bytes 13828
  323.1 68.1 %copy-start.60 = (f32[2,1,1152]{2,0,1:T(2,128)S(1)}, f32[2,1,1152]{2,0,1:T(2,128)}, u32[]{:S(2)}) copy-start(f32[2,1,1152]{2,0,1:T(2,128)} %copy-done.59) | copy-start | bytes 27652
  323.1 68.1 %copy-start.66 = (s32[1152]{0:T(1024)S(1)}, s32[1152]{0:T(1024)}, u32[]{:S(2)}) copy-start(s32[1152]{0:T(1024)} %copy-done.65) | copy-start | bytes 13828
  323.1 68.1 %copy-start.77 = (f32[2]{0:T(128)S(1)}, f32[2]{0:T(128)}, u32[]{:S(2)}) copy-start(f32[2]{0:T(128)} %copy-done.76) | copy-start | bytes 28
  387.9 5.3 %copy-start.12 = (f32[16,3968]{1,0:T(8,128)S(1)}, f32[16,3968]{1,0:T(8,128)}, u32[]{:S(2)}) copy-start(f32[16,3968]{1,0:T(8,128)} %get-tuple-element.106) | copy-start | bytes 761860
  388.0 5.3 %copy-start.19 = (f32[16,3840]{1,0:T(8,128)S(1)}, f32[16,3840]{1,0:T(8,128)}, u32[]{:S(2)}) copy-start(f32[16,3840]{1,0:T(8,128)} %get-tuple-element.107) | copy-start | bytes 737284
  396.7 22.9 %copy-start.72 = (pred[128]{0:T(512)(128)(4,1)S(1)}, pred[128]{0:T(512)(128)(4,1)}, u32[]{:S(2)}) copy-start(pred[128]{0:T(512)(128)(4,1)} %lt.166) | copy-start | bytes 388
  399.2 20.6 %copy-start.71 = (s32[128]{0:T(128)S(1)}, s32[128]{0:T(128)}, u32[]{:S(2)}) copy-start(s32[128]{0:T(128)} %copy-done.70) | copy-start | bytes 1540
  399.2 21.5 %copy-start.34 = (bf16[96,1152]{1,0:T(8,128)(2,1)S(1)}, bf16[96,1152]{1,0:T(8,128)(2,1)}, u32[]{:S(2)}) copy-start(bf16[96,1152]{1,0:T(8,128)(2,1)} %param.20) | copy-start | bytes 663556
  400.2 21.8 %copy-start.28 = (bf16[1152,6,9]{0,1,2:T(8,128)(2,1)S(1)}, bf16[1152,6,9]{0,1,2:T(8,128)(2,1)}, u32[]{:S(2)}) copy-start(bf16[1152,6,9]{0,1,2:T(8,128)(2,1)} %param.23) | copy-start | bytes 373252
  451.3 8.9 %copy-start.10 = (f32[2,64,1152]{2,1,0:T(8,128)S(1)}, f32[2,64,1152]{2,1,0:T(8,128)}, u32[]{:S(2)}) copy-start(f32[2,64,1152]{2,1,0:T(8,128)} %get-tuple-element.191) | copy-start | bytes 1769476
  451.3 8.8 %copy-start.18 = (bf16[2,64,1152]{2,1,0:T(8,128)(2,1)S(1)}, bf16[2,64,1152]{2,1,0:T(8,128)(2,1)}, u32[]{:S(2)}) copy-start(bf16[2,64,1152]{2,1,0:T(8,128)(2,1)} %reduce-scatter.11.cloned.1.call-done) | copy-start | bytes 884740
  459.1 4.7 %copy-start.1 = (bf16[2,64,1152]{2,1,0:T(8,128)(2,1)S(1)}, bf16[2,64,1152]{2,1,0:T(8,128)(2,1)}, u32[]{:S(2)}) copy-start(bf16[2,64,1152]{2,1,0:T(8,128)(2,1)} %param.33) | copy-start | bytes 884740
  (29 other events, 59.9 us)
Sparse Core Ops, SparseCore 0:
  134.8 19.1 reduce-scatter.4
  186.6 21.7 reduce-scatter.8
  211.3 18.7 reduce-scatter.6
  310.3 19.6 reduce-scatter.10

commit v2 on v1

--- a/solution.py
+++ b/solution.py
@@ -9,6 +9,20 @@
 
 MESH = pl.DeviceIdType.MESH
 OFFS = (0, 3, 1, 2)
+WIDTHS = (2304, 2304, 2304, 896)
+PIECES = (
+    (3, 0, 896, "z"),
+    (0, 0, 1152, "z"),
+    (0, 1152, 1152, "y"),
+    (1, 0, 1152, "z"),
+    (1, 1152, 1152, "y"),
+    (2, 0, 1152, "z"),
+    (2, 1152, 1152, "y"),
+)
+
+
+highest = lax.Precision.HIGHEST
+norm_eps = 1e-06
 
 
 def place_of():
@@ -36,17 +50,21 @@
     pl.semaphore_wait(barrier, len(group))
 
 
-def gather_kernel(firsts, *refs):
-    n = len(firsts)
-    ins, outs = refs[:n], refs[n : 2 * n]
-    local_sem, send_sem, recv_sem, core_send, core_recv = refs[2 * n :]
+def gather_kernel(*refs):
+    n, m = len(PIECES), len(WIDTHS)
+    ins, outs = refs[:m], refs[m : 2 * m]
+    local_sem, send_sem, recv_sem, core_send, core_recv = refs[2 * m :]
     z, y, x, c, t = place_of()
     near = peers(z, y, x, c, t)
     greet(near)
     started = []
 
-    def spot(p, u, v):
-        return (c, u, v) if firsts[p] == "z" else (c, v, u)
+    def spot(p, u, v, core=c):
+        return core * 32 + (u * 8 + v * 2 if PIECES[p][3] == "z" else v * 8 + u * 2)
+
+    def block(p, at, count=1):
+        r, low, width, first = PIECES[p]
+        return outs[r].at[pl.ds(at, count), :, pl.ds(low, width)]
 
     def remote(src, dst, ssem, rsem, peer):
         return pltpu.make_async_remote_copy(
@@ -67,46 +85,48 @@
         started.append(cp)
 
     def axes(p):
-        if firsts[p] == "z":
+        if PIECES[p][3] == "z":
             return z, y, near["z"], near["y"]
         return y, z, near["y"], near["z"]
 
     locals_ = []
     for p in range(n):
-        own = outs[p].at[c, z, y, x]
-        send(p, 0, own, near["x"], ins[p])
-        cp = pltpu.make_async_copy(ins[p], own, local_sem.at[p])
+        r, low, width, first = PIECES[p]
+        mine = ins[r].at[:, :, pl.ds(low, width)]
+        own = block(p, c * 32 + z * 8 + y * 2 + x)
+        send(p, 0, own, near["x"], mine)
+        cp = pltpu.make_async_copy(mine, own, local_sem.at[p])
         cp.start()
         locals_.append(cp)
     for p in range(n):
         u, v, one, two = axes(p)
         locals_[p].wait()
-        arrive(p, 0, outs[p].at[c, z, y, 1 - x])
-        pair = outs[p].at[spot(p, u, v)]
+        arrive(p, 0, block(p, c * 32 + z * 8 + y * 2 + 1 - x))
+        pair = block(p, spot(p, u, v), 2)
         send(p, 1, pair, one[1])
         send(p, 2, pair, one[0])
         share(p, 0, pair)
     for p in range(n):
         u, v, one, two = axes(p)
-        pair = outs[p].at[spot(p, u, v)]
+        pair = block(p, spot(p, u, v), 2)
         send(p, 5, pair, two[1])
         send(p, 6, pair, two[0])
     for p in range(n):
         u, v, one, two = axes(p)
         for k, way in ((1, 1), (2, 0)):
             uu = (u + OFFS[k]) % 4
-            pair = outs[p].at[spot(p, uu, v)]
+            pair = block(p, spot(p, uu, v), 2)
             arrive(p, k, pair)
-            send(p, 2 + k, outs[p].at[(*spot(p, uu, v), 1 - way)], one[way])
+            send(p, 2 + k, block(p, spot(p, uu, v) + 1 - way), one[way])
             send(p, 5 + 4 * k, pair, two[1])
             send(p, 6 + 4 * k, pair, two[0])
             share(p, 4 * k, pair)
     for p in range(n):
         u, v, one, two = axes(p)
         uu = (u + 2) % 4
-        arrive(p, 3, outs[p].at[(*spot(p, uu, v), 0)])
-        arrive(p, 4, outs[p].at[(*spot(p, uu, v), 1)])
-        pair = outs[p].at[spot(p, uu, v)]
+        arrive(p, 3, block(p, spot(p, uu, v) + 0))
+        arrive(p, 4, block(p, spot(p, uu, v) + 1))
+        pair = block(p, spot(p, uu, v), 2)
         send(p, 17, pair, two[1])
         send(p, 18, pair, two[0])
         share(p, 12, pair)
@@ -116,32 +136,32 @@
             uu = (u + OFFS[k]) % 4
             for side, way in ((1, 1), (2, 0)):
                 vv = (v + OFFS[side]) % 4
-                pair = outs[p].at[spot(p, uu, vv)]
+                pair = block(p, spot(p, uu, vv), 2)
                 arrive(p, 4 + 4 * k + side, pair)
-                send(p, 6 + 4 * k + side, outs[p].at[(*spot(p, uu, vv), 1 - way)], two[way])
+                send(p, 6 + 4 * k + side, block(p, spot(p, uu, vv) + 1 - way), two[way])
                 share(p, 4 * k + side, pair)
     for k in range(4):
         for p in range(n):
             u, v, one, two = axes(p)
             uu, vv = (u + OFFS[k]) % 4, (v + 2) % 4
-            arrive(p, 7 + 4 * k, outs[p].at[(*spot(p, uu, vv), 0)])
-            arrive(p, 8 + 4 * k, outs[p].at[(*spot(p, uu, vv), 1)])
-            share(p, 4 * k + 3, outs[p].at[spot(p, uu, vv)])
+            arrive(p, 7 + 4 * k, block(p, spot(p, uu, vv) + 0))
+            arrive(p, 8 + 4 * k, block(p, spot(p, uu, vv) + 1))
+            share(p, 4 * k + 3, block(p, spot(p, uu, vv), 2))
     for p in range(n):
         for k in range(16):
-            ref = outs[p].at[1 - c, k // 4, k % 4]
+            ref = block(p, (1 - c) * 32 + 2 * k, 2)
             remote(ref, ref, core_send.at[p, k], core_recv.at[p, k], near["c"]).wait_recv()
     for cp in started:
         cp.wait_send()
 
 
-def gather_blocks(firsts, parts, collective_id):
-    n = len(parts)
+def gather_blocks(parts, collective_id):
+    n, m = len(PIECES), len(WIDTHS)
     return pl.pallas_call(
-        functools.partial(gather_kernel, firsts),
-        out_shape=[jax.ShapeDtypeStruct((2, 4, 4, 2) + part.shape, part.dtype) for part in parts],
-        in_specs=[pl.BlockSpec(memory_space=pl.ANY)] * n,
-        out_specs=[pl.BlockSpec(memory_space=pl.ANY)] * n,
+        gather_kernel,
+        out_shape=[jax.ShapeDtypeStruct((64, 16, width), jnp.bfloat16) for width in WIDTHS],
+        in_specs=[pl.BlockSpec(memory_space=pl.ANY)] * m,
+        out_specs=[pl.BlockSpec(memory_space=pl.ANY)] * m,
         scratch_shapes=[
             pltpu.SemaphoreType.DMA((n,)),
             pltpu.SemaphoreType.DMA((n, 21)),
@@ -168,10 +188,10 @@
     lax.fori_loop(0, width // 128, step, 0)
 
 
-def scatter_kernel(firsts, *refs):
-    n = len(firsts)
-    grads, outs = refs[:n], refs[n : 2 * n]
-    refs = refs[2 * n :]
+def scatter_kernel(*refs):
+    n, m = len(PIECES), len(WIDTHS)
+    grads, outs = refs[:m], refs[m : 2 * m]
+    refs = refs[2 * m :]
     twins, sums, inner, mids, outer, ends, last = (refs[i * n : (i + 1) * n] for i in range(7))
     send_sem, recv_sem, core_send, core_recv = refs[7 * n :]
     z, y, x, c, t = place_of()
@@ -185,12 +205,19 @@
         )
 
     def axes(p):
-        if firsts[p] == "z":
+        if PIECES[p][3] == "z":
             return z, y, near["z"], near["y"]
         return y, z, near["y"], near["z"]
 
     def spot(p, u, v):
-        return (u, v) if firsts[p] == "z" else (v, u)
+        return u * 8 + v * 2 if PIECES[p][3] == "z" else v * 8 + u * 2
+
+    def grad(p, at, count):
+        r, low, width, first = PIECES[p]
+        return grads[r].at[pl.ds(at, count), :, pl.ds(low, width)]
+
+    def total(p, at, count):
+        return sums[p].at[pl.ds(at, count)]
 
     def send(p, k, src, dst, peer):
         cp = remote(src, dst, send_sem.at[p, k], recv_sem.at[p, k], peer)
@@ -209,7 +236,7 @@
                 at = spot(p, (u + OFFS[k]) % 4, (v + OFFS[side]) % 4)
                 j = 4 * k + side
                 cp = remote(
-                    grads[p].at[(1 - c, *at)], twins[p].at[at], core_send.at[p, j], core_recv.at[p, j], near["c"]
+                    grad(p, (1 - c) * 32 + at, 2), twins[p].at[pl.ds(at, 2)], core_send.at[p, j], core_recv.at[p, j], near["c"]
                 )
                 cp.start()
                 started.append(cp)
@@ -218,35 +245,35 @@
         u, v, one, two = axes(p)
         at = spot(p, (u + OFFS[k]) % 4, (v + OFFS[side]) % 4)
         j = 4 * k + side
-        twin = twins[p].at[at]
+        twin = twins[p].at[pl.ds(at, 2)]
         remote(twin, twin, core_send.at[p, j], core_recv.at[p, j], near["c"]).wait_recv()
-        add_into(sums[p].at[at], grads[p].at[(c, *at)], twin)
+        add_into(total(p, at, 2), grad(p, c * 32 + at, 2), twin)
 
     for k in order:
         for p in range(n):
             u, v, one, two = axes(p)
             combine(p, k, 3)
-            src = sums[p].at[spot(p, (u + OFFS[k]) % 4, (v + 2) % 4)]
+            src = sums[p].at[pl.ds(spot(p, (u + OFFS[k]) % 4, (v + 2) % 4), 2)]
             send(p, 6 * k, src.at[0], inner[p].at[k, 0], two[1])
             send(p, 6 * k + 1, src.at[1], inner[p].at[k, 1], two[0])
     for k in order:
         for p in range(n):
             u, v, one, two = axes(p)
             combine(p, k, 2)
-            src = sums[p].at[spot(p, (u + OFFS[k]) % 4, (v + 1) % 4)]
+            src = sums[p].at[pl.ds(spot(p, (u + OFFS[k]) % 4, (v + 1) % 4), 2)]
             send(p, 6 * k + 2, src.at[1], inner[p].at[k, 2], two[1])
             combine(p, k, 1)
-            src = sums[p].at[spot(p, (u + OFFS[k]) % 4, (v + 3) % 4)]
+            src = sums[p].at[pl.ds(spot(p, (u + OFFS[k]) % 4, (v + 3) % 4), 2)]
             send(p, 6 * k + 4, src.at[0], inner[p].at[k, 4], two[0])
     for k in order:
         for p in range(n):
             u, v, one, two = axes(p)
             arrive(p, 6 * k, inner[p].at[k, 0])
-            src = sums[p].at[spot(p, (u + OFFS[k]) % 4, (v + 1) % 4)].at[0]
+            src = sums[p].at[spot(p, (u + OFFS[k]) % 4, (v + 1) % 4) + 0]
             add_into(src, src, inner[p].at[k, 0])
             send(p, 6 * k + 3, src, inner[p].at[k, 3], two[1])
             arrive(p, 6 * k + 1, inner[p].at[k, 1])
-            src = sums[p].at[spot(p, (u + OFFS[k]) % 4, (v + 3) % 4)].at[1]
+            src = sums[p].at[spot(p, (u + OFFS[k]) % 4, (v + 3) % 4) + 1]
             add_into(src, src, inner[p].at[k, 1])
             send(p, 6 * k + 5, src, inner[p].at[k, 5], two[0])
     for k in order:
@@ -255,7 +282,7 @@
     for k in order:
         for p in range(n):
             u, v, one, two = axes(p)
-            own = sums[p].at[spot(p, (u + OFFS[k]) % 4, v)]
+            own = sums[p].at[pl.ds(spot(p, (u + OFFS[k]) % 4, v), 2)]
             for j in range(2, 6):
                 arrive(p, 6 * k + j, inner[p].at[k, j])
             add_into(mids[p].at[k, 0], own.at[0], inner[p].at[k, 3], inner[p].at[k, 4])
@@ -283,26 +310,26 @@
         send(p, 30, ends[p].at[1 - x], last[p], near["x"])
     for p in range(n):
         arrive(p, 30, last[p])
-        add_into(outs[p], ends[p].at[x], last[p])
+        r, low, width, first = PIECES[p]
+        add_into(outs[r].at[:, pl.ds(low, width)], ends[p].at[x], last[p])
     for cp in started:
         cp.wait_send()
 
 
-def scatter_blocks(firsts, parts, collective_id):
-    n = len(parts)
-    rows = [part.shape[4:] for part in parts]
+def scatter_blocks(parts, collective_id):
+    n, m = len(PIECES), len(WIDTHS)
 
     def room(*lead):
-        return [pltpu.VMEM(lead + row, jnp.bfloat16) for row in rows]
+        return [pltpu.VMEM(lead + (16, piece[2]), jnp.bfloat16) for piece in PIECES]
 
     return pl.pallas_call(
-        functools.partial(scatter_kernel, firsts),
-        out_shape=[jax.ShapeDtypeStruct(row, jnp.float32) for row in rows],
-        in_specs=[pl.BlockSpec(memory_space=pltpu.VMEM)] * n,
-        out_specs=[pl.BlockSpec(memory_space=pltpu.VMEM)] * n,
+        scatter_kernel,
+        out_shape=[jax.ShapeDtypeStruct((16, width), jnp.float32) for width in WIDTHS],
+        in_specs=[pl.BlockSpec(memory_space=pltpu.VMEM)] * m,
+        out_specs=[pl.BlockSpec(memory_space=pltpu.VMEM)] * m,
         scratch_shapes=[
-            *room(4, 4, 2),
-            *room(4, 4, 2),
+            *room(32),
+            *room(32),
             *room(4, 6),
             *room(4, 2),
             *room(6),
@@ -424,36 +451,314 @@
     )(parts)
 
 
-HEAD_DIM = 72
-
-
-highest = lax.Precision.HIGHEST
-norm_eps = 1e-06
-
-
-def modulate(rows, shift, scale):
+GATE_ROWS = 8
+HEAD_LANES = 128
+
+
+def one_hot(shape, rule):
+    first = lax.broadcasted_iota(jnp.int32, shape, 0)
+    second = lax.broadcasted_iota(jnp.int32, shape, 1)
+    return jnp.where(rule(first, second), 1.0, 0.0).astype(jnp.bfloat16)
+
+
+def dot(a, b, ca=1, cb=0):
+    return lax.dot_general(a, b, (((ca,), (cb,)), ((), ())), preferred_element_type=jnp.float32)
+
+
+def normed(rows):
     centred = rows - jnp.mean(rows, axis=-1, keepdims=True)
-    normed = centred * lax.rsqrt(jnp.mean(centred * centred, axis=-1, keepdims=True) + norm_eps)
-    return normed * (1.0 + scale) + shift
-
-
-def gelu_tanh(values):
-    return jax.nn.gelu(values, approximate=True)
-
-
-def widen(rows):
-    return lax.all_gather(rows, "tp", axis=1, tiled=True)
-
-
-def narrow(terms):
-    return lax.psum_scatter(
-        terms.astype(jnp.bfloat16), "tp", scatter_dimension=1, tiled=True
-    ).astype(jnp.float32)
-
-FIRSTS = ("z", "y")
+    inverse = lax.rsqrt(jnp.mean(centred * centred, axis=-1, keepdims=True) + norm_eps)
+    return centred * inverse, inverse
+
+
+def norm_back(grad, unit, inverse):
+    first = jnp.mean(grad, axis=-1, keepdims=True)
+    second = jnp.mean(grad * unit, axis=-1, keepdims=True)
+    return inverse * (grad - first - unit * second)
+
+
+def gelu_slope(u):
+    a, b = 0.7978845608028654, 0.044715
+    wave = jnp.tanh(a * (u + b * (u * u * u)))
+    return 0.5 * (1.0 + wave) + 0.5 * u * (1.0 - wave * wave) * (a * (1.0 + 3.0 * b * (u * u)))
+
+
+def gelu_value(u):
+    a, b = 0.7978845608028654, 0.044715
+    return 0.5 * u * (1.0 + jnp.tanh(a * (u + b * (u * u * u))))
+
+
+def columns_loop(count, body):
+    def step(i, carry):
+        body(pl.ds(pl.multiple_of(i * 256, 256), 256))
+        return carry
+
+    lax.fori_loop(0, count, step, 0)
+
+
+def middle_kernel(*refs):
+    (lat, cot, mods, bias_d, bias_qkv, bias_up, w1, w2, w3, wt) = refs[:10]
+    (out, grad_lat, g1, g2, g3, gt, grad_mod, grad_bd, grad_bqkv, grad_bup) = refs[10:20]
+    (
+        tail_w, tail_g, wide1, wideg, wide2, wideb, flip1, flipg, flip2, flipb,
+        narrow_send, narrow_recv, part, qkvp, mixp, probs, gattp, gqkvp, qk, gqkv, att,
+        upper, acted, gup, middle, branch, down_keep, unit2, send_sem, recv_sem,
+    ) = refs[20:]
+    slots = lat.shape[0]
+    z, y, x, c, t = place_of()
+    partner = (lax.axis_index("fsdp"), 1 - t)
+    barrier = pltpu.get_barrier_semaphore()
+    pl.semaphore_signal(barrier, inc=1, device_id=partner, device_id_type=MESH)
+    pl.semaphore_wait(barrier, 1)
+
+    def remote(k, src, dst):
+        return pltpu.make_async_remote_copy(
+            src_ref=src, dst_ref=dst, send_sem=send_sem.at[k], recv_sem=recv_sem.at[k],
+            device_id=partner, device_id_type=MESH,
+        )
+
+    def widen_start(k, wide):
+        remote(k, wide.at[:, t], wide.at[:, t]).start()
+
+    def widen_end(k, wide):
+        remote(k, wide.at[:, 1 - t], wide.at[:, 1 - t]).wait()
+        return wide[...].reshape(256, wide.shape[-1])
+
+    def narrow_start(k, n):
+        for s in range(slots):
+            narrow_send[n, s] = part[s, 1 - t].astype(jnp.bfloat16)
+        remote(k, narrow_send.at[n], narrow_recv.at[n]).start()
+
+    def narrow_end(k, n):
+        remote(k, narrow_send.at[n], narrow_recv.at[n]).wait()
+
+    def narrowed(n, s):
+        return part[s, t].astype(jnp.bfloat16).astype(jnp.float32) + narrow_recv[n, s].astype(jnp.float32)
+
+    def mod(s, k):
+        return mods[s, k : k + 1, :]
+
+    for s in range(slots):
+        unit, inverse = normed(lat[s].astype(jnp.float32))
+        wide1[s, t] = (unit * (1.0 + mod(s, 1)) + mod(s, 0)).astype(jnp.bfloat16)
+    widen_start(0, wide1)
+    for s in range(slots):
+        grad = cot[s].astype(jnp.float32) * mod(s, 6)
+        wideg[s, t] = (mod(s, 5) * grad).astype(jnp.bfloat16)
+    widen_start(1, wideg)
+    grad_bd[1:2] = sum(jnp.sum(wideg[s, t].astype(jnp.float32), axis=0, keepdims=True) for s in range(slots))
+
+    for j in range(8):
+        pick = one_hot((128, 1024), lambda a, b: b == (a // 2) * 16 + (a % 2) * 8 + j)
+        tail_w[:, 896 * j : 896 * j + 896] = dot(pick, wt[...].reshape(1024, 896)).astype(jnp.bfloat16)
+
+    h1 = widen_end(0, wide1)
+    flip1[...] = h1.T
+
+    def project(rows, w, cols, offset):
+        return dot(rows[:, :1024], w[:, :, cols].reshape(1024, 256)) + dot(
+            rows[:, 1024:], tail_w[:, pl.ds(pl.multiple_of(offset + cols.start, 256), 256)]
+        )
+
+    def to_qkv(cols):
+        flat = project(wide1[...].reshape(256, 1152), w1, cols, 0) + bias_qkv[:, cols]
+        qk[:, cols] = flat.astype(jnp.bfloat16)
+
+    columns_loop(9, to_qkv)
+    for i, lane in enumerate((0, 576, 1152)):
+        low = lane // 128 * 128
+        spread_heads = one_hot(
+            (640, 1024), lambda a, b: (a - (lane - low) == (b // 128) * 72 + b % 128) & (b % 128 < 72)
+        )
+        qkvp[i] = dot(qk[:, low : low + 640], spread_heads).astype(jnp.bfloat16)
+
+    factor = 72 ** (-0.5)
+
+    def attend(i, carry):
+        rows = pl.ds(pl.multiple_of(i * 128, 128), 128)
+        for h in range(8):
+            lanes = slice(128 * h, 128 * h + 128)
+            q, k, v = qkvp[0, rows, lanes], qkvp[1, rows, lanes], qkvp[2, rows, lanes]
+            scores = dot(q, k, 1, 1) * factor
+            raised = jnp.exp(scores - jnp.max(scores, axis=-1, keepdims=True))
+            prob = raised / jnp.sum(raised, axis=-1, keepdims=True)
+            probs[i, h] = prob
+            mixp[rows, lanes] = dot(prob.astype(jnp.bfloat16), v).astype(jnp.bfloat16)
+        return carry
+
+    lax.fori_loop(0, slots, attend, 0)
+    join = one_hot((1024, 640), lambda a, b: (b - 64 == (a // 128) * 72 + a % 128) & (a % 128 < 72))
+    att[...] = dot(mixp[...], join).astype(jnp.bfloat16)
+
+    def back_to_width(rows, w, cols, tail_cols, add):
+        total = dot(rows, w[:, :, cols].reshape(1024, -1), 1, 1)
+        tail = dot(rows, tail_w[:, tail_cols], 1, 1)
+        main = part.at[:, :, :, 0:1024]
+        rest = part.at[:, :, :, 1024:1152]
+        total, tail = total.reshape(slots, 2, 64, 1024), tail.reshape(slots, 2, 64, 128)
+        main[...] = main[...] + total if add else total
+        rest[...] = rest[...] + tail if add else tail
+
+    back_to_width(att[...], w1, slice(1664, 2304), slice(1664, 2304), False)
+    narrow_start(2, 0)
+    narrow_end(2, 0)
+    for s in range(slots):
+        piece = narrowed(0, s) + bias_d[0:1]
+        branch[s] = piece
+        rows = lat[s].astype(jnp.float32) + mod(s, 2) * piece
+        middle[s] = rows
+        unit, inverse = normed(rows)
+        wide2[s, t] = (unit * (1.0 + mod(s, 4)) + mod(s, 3)).astype(jnp.bfloat16)
+    widen_start(3, wide2)
+    gd = widen_end(1, wideg)
+    flipg[...] = gd.T
+    h2 = widen_end(3, wide2)
+    flip2[...] = h2.T
+
+    def feed(cols):
+        up = project(wide2[...].reshape(256, 1152), w2, cols, 2304) + bias_up[:, cols]
+        upper[:, cols] = up
+        acted[:, cols] = gelu_value(up).astype(jnp.bfloat16)
+
+    columns_loop(9, feed)
+    back_to_width(acted[...], w3, slice(0, 2304), slice(4608, 6912), False)
+    narrow_start(4, 1)
+    for s in range(slots):
+        down_keep[s] = part[s, t]
+
+    def feed_back(cols):
+        grad = project(wideg[...].reshape(256, 1152), w3, cols, 4608)
+        low = (grad * gelu_slope(upper[:, cols])).astype(jnp.bfloat16)
+        gup[:, cols] = low
+        grad_bup[:, cols] = jnp.sum(low.astype(jnp.float32), axis=0, keepdims=True)
+
+    columns_loop(9, feed_back)
+
+    back_to_width(gup[...], w2, slice(0, 2304), slice(2304, 4608), False)
+    narrow_start(5, 2)
+
+    def weight_grad(flip, rows, cols, g, offset):
+        made = dot(flip[...], rows[:, cols]).astype(jnp.bfloat16)
+        g[:, :, cols] = made[:1024].reshape(64, 16, 256)
+        tail_g[:, pl.ds(pl.multiple_of(offset + cols.start, 256), 256)] = made[1024:]
+
+    columns_loop(9, lambda cols: weight_grad(flipg, acted, cols, g3, 4608))
+    columns_loop(9, lambda cols: weight_grad(flip2, gup, cols, g2, 2304))
+
+    narrow_end(4, 1)
+    for s in range(slots):
+        grad = cot[s].astype(jnp.float32) * mod(s, 6)
+        down = down_keep[s].astype(jnp.bfloat16).astype(jnp.float32) + narrow_recv[1, s].astype(jnp.float32)
+        down = down + bias_d[1:2]
+        out[s] = ((middle[s] + mod(s, 5) * down) * mod(s, 6)).astype(jnp.bfloat16)
+        grad_mod[s, 5:6] = jnp.sum(grad * down, axis=0, keepdims=True)
+    narrow_end(5, 2)
+    for s in range(slots):
+        grad = cot[s].astype(jnp.float32) * mod(s, 6)
+        gh = narrowed(2, s)
+        unit, inverse = normed(middle[s])
+        grad_mod[s, 3:4] = jnp.sum(gh, axis=0, keepdims=True)
+        grad_mod[s, 4:5] = jnp.sum(gh * unit, axis=0, keepdims=True)
+        gm = grad + norm_back(gh * (1.0 + mod(s, 4)), unit, inverse)
+        grad_mod[s, 2:3] = jnp.sum(gm * branch[s], axis=0, keepdims=True)
+        middle[s] = gm
+        wideb[s, t] = (mod(s, 2) * gm).astype(jnp.bfloat16)
+    widen_start(6, wideb)
+    grad_bd[0:1] = sum(jnp.sum(wideb[s, t].astype(jnp.float32), axis=0, keepdims=True) for s in range(slots))
+    gb = widen_end(6, wideb)
+    flipb[...] = gb.T
+    gatt = dot(gb[:, :1024], w1[:, :, 1664:2304].reshape(1024, 640)) + dot(gb[:, 1024:], tail_w[:, 1664:2304])
+    gattp[...] = dot(gatt.astype(jnp.bfloat16), join, 1, 1).astype(jnp.bfloat16)
+
+    def attend_back(i, carry):
+        rows = pl.ds(pl.multiple_of(i * 128, 128), 128)
+        for h in range(8):
+            lanes = slice(128 * h, 128 * h + 128)
+            q, k, v = qkvp[0, rows, lanes], qkvp[1, rows, lanes], qkvp[2, rows, lanes]
+            ga = gattp[rows, lanes]
+            prob = probs[i, h]
+            grad = dot(ga, v, 1, 1)
+            inner = jnp.sum(prob * grad, axis=-1, keepdims=True)
+            gs = (prob * (grad - inner)).astype(jnp.bfloat16)
+            gqkvp[0, rows, lanes] = (dot(gs, k) * factor).astype(jnp.bfloat16)
+            gqkvp[1, rows, lanes] = (dot(gs, q, 0, 0) * factor).astype(jnp.bfloat16)
+            gqkvp[2, rows, lanes] = dot(prob.astype(jnp.bfloat16), ga, 0, 0).astype(jnp.bfloat16)
+        return carry
+
+    lax.fori_loop(0, slots, attend_back, 0)
+    gqkv[...] = jnp.zeros_like(gqkv)
+    for i, lane in enumerate((0, 576, 1152)):
+        low = lane // 128 * 128
+        gather_heads = one_hot(
+            (1024, 640), lambda a, b: (b - (lane - low) == (a // 128) * 72 + a % 128) & (a % 128 < 72)
+        )
+        piece = dot(gqkvp[i], gather_heads).astype(jnp.bfloat16)
+        gqkv[:, low : low + 640] = gqkv[:, low : low + 640] + piece
+    grad_bqkv[...] = jnp.sum(gqkv[...].astype(jnp.float32), axis=0, keepdims=True)
+    back_to_width(gqkv[...], w1, slice(0, 1792), slice(0, 1792), False)
+    narrow_start(7, 3)
+
+    columns_loop(6, lambda cols: weight_grad(flip1, gqkv, cols, g1, 0))
+    for low, high in ((1536, 1664), (1664, 1792), (1792, 2304)):
+        made = 0.0
+        if low < 1792:
+            made = made + dot(flip1[...], gqkv[:, low:high])
+        if high > 1664:
+            made = made + dot(flipb[...], att[:, low - 1664 : high - 1664])
+        made = made.astype(jnp.bfloat16)
+        g1[:, :, low:high] = made[:1024].reshape(64, 16, high - low)
+        tail_g[:, low:high] = made[1024:]
+    tail_g[:, 6912:] = jnp.zeros((128, 256), jnp.bfloat16)
+    total = jnp.zeros((1024, 896), jnp.float32)
+    for j in range(8):
+        pick = one_hot((1024, 128), lambda a, b: a == (b // 2) * 16 + (b % 2) * 8 + j)
+        total = total + dot(pick, tail_g[:, 896 * j : 896 * j + 896])
+    gt[...] = total.astype(jnp.bfloat16).reshape(64, 16, 896)
+
+    narrow_end(7, 3)
+    for s in range(slots):
+        gh = narrowed(3, s)
+        unit, inverse = normed(lat[s].astype(jnp.float32))
+        grad_mod[s, 0:1] = jnp.sum(gh, axis=0, keepdims=True)
+        grad_mod[s, 1:2] = jnp.sum(gh * unit, axis=0, keepdims=True)
+        grad_lat[s] = middle[s] + norm_back(gh * (1.0 + mod(s, 1)), unit, inverse)
+        grad_mod[s, 6:8] = jnp.zeros((2, 1152), jnp.float32)
+
+
+def middle_block(args, collective_id):
+    f32, bf = jnp.float32, jnp.bfloat16
+    vmem = pl.BlockSpec(memory_space=pltpu.VMEM)
+    shape = jax.ShapeDtypeStruct
+    return pl.pallas_call(
+        middle_kernel,
+        out_shape=[
+            shape((2, 64, 1152), bf), shape((2, 64, 1152), f32),
+            shape((64, 16, 2304), bf), shape((64, 16, 2304), bf), shape((64, 16, 2304), bf), shape((64, 16, 896), bf),
+            shape((2, 8, 1152), f32), shape((2, 1152), f32), shape((1, 1792), f32), shape((1, 2304), f32),
+        ],
+        in_specs=[vmem] * len(args),
+        out_specs=[vmem] * 10,
+        scratch_shapes=[
+            pltpu.VMEM((128, 7168), bf), pltpu.VMEM((128, 7168), bf),
+            *[pltpu.VMEM((2, 2, 64, 1152), bf)] * 4,
+            *[pltpu.VMEM((1152, 256), bf)] * 4,
+            pltpu.VMEM((4, 2, 64, 1152), bf), pltpu.VMEM((4, 2, 64, 1152), bf),
+            pltpu.VMEM((2, 2, 64, 1152), f32),
+            pltpu.VMEM((3, 256, 1024), bf), pltpu.VMEM((256, 1024), bf), pltpu.VMEM((2, 8, 128, 128), f32),
+            pltpu.VMEM((256, 1024), bf), pltpu.VMEM((3, 256, 1024), bf),
+            pltpu.VMEM((256, 2304), bf), pltpu.VMEM((256, 1792), bf), pltpu.VMEM((256, 640), bf),
+            pltpu.VMEM((256, 2304), f32), pltpu.VMEM((256, 2304), bf), pltpu.VMEM((256, 2304), bf),
+            *[pltpu.VMEM((2, 64, 1152), f32)] * 4,
+            pltpu.SemaphoreType.DMA((8,)), pltpu.SemaphoreType.DMA((8,)),
+        ],
+        compiler_params=pltpu.CompilerParams(
+            collective_id=collective_id, has_side_effects=True, vmem_limit_bytes=62 * 1024 * 1024
+        ),
+    )(*args)
+
+
 MAIN = 1024
 CHUNK = 896
-LEFT = 3968
 
 
 def shuffle_matrix(width):
@@ -483,74 +788,16 @@
 
 
 def pack_rows(all_rows):
+    third = all_rows.shape[1] // 3
     main, tail = all_rows[:16], all_rows[16:]
-    tail = jnp.pad(tail, ((0, 0), (0, 8 * CHUNK - tail.shape[1]))).reshape(16, CHUNK)
-    whole = jnp.concatenate([tail, main], axis=1)
-    return whole[:, :LEFT], whole[:, LEFT:]
-
-
-def unpack_rows(left, right, width):
-    whole = jnp.concatenate([left, right], axis=1)
-    return jnp.concatenate([whole[:, CHUNK:], whole[:, :CHUNK].reshape(2, 8 * CHUNK)[:, :width]], axis=0)
-
-
-def unpack_all(left, right, width):
-    left, right = left.reshape(MAIN, -1), right.reshape(MAIN, -1)
-    tail = left[:, :CHUNK].reshape(128, 8 * CHUNK)[:, :width]
-    third = width // 3
-    most = third - (right.shape[1] - third)
-    one = jnp.concatenate([left[:, CHUNK : CHUNK + third], tail[:, :third]], axis=0)
-    two = jnp.concatenate(
-        [
-            jnp.concatenate([left[:, CHUNK + third :], right[:, : right.shape[1] - third]], axis=1),
-            tail[:, third : 2 * third],
-        ],
-        axis=0,
-    )
-    three = jnp.concatenate([right[:, right.shape[1] - third :], tail[:, 2 * third :]], axis=0)
-    return one, two, three
-
-
-def pack_all(grads):
-    whole = jnp.concatenate(grads, axis=1)
-    main, tail = whole[:MAIN], whole[MAIN:]
-    tail = jnp.pad(tail, ((0, 0), (0, 8 * CHUNK - tail.shape[1]))).reshape(MAIN, CHUNK)
-    whole = jnp.concatenate([tail, main], axis=1)
-    shape = (2, 4, 4, 2, 16)
-    return whole[:, :LEFT].reshape(*shape, LEFT), whole[:, LEFT:].reshape(*shape, -1)
-
-
-def attend_forward(pieces):
-    queries, keys, values = pieces
-    factor = queries.shape[-1] ** (-0.5)
-    scores = jnp.einsum("lhe,mhe->hlm", queries, keys, preferred_element_type=jnp.float32) * factor
-    peak = jnp.max(scores, axis=-1, keepdims=True)
-    raised = jnp.exp(scores - peak)
-    total = jnp.sum(raised, axis=-1, keepdims=True)
-    weights = (raised / total).astype(jnp.bfloat16)
-    mixed = jnp.einsum("hlm,mhe->lhe", weights, values, preferred_element_type=jnp.float32)
-    return (mixed.astype(jnp.bfloat16), (peak + jnp.log(total))[..., 0])
-
-
-def attend_backward(pieces):
-    queries, keys, values, log_total, grad_mixed = pieces
-    factor = queries.shape[-1] ** (-0.5)
-    scores = jnp.einsum("lhe,mhe->hlm", queries, keys, preferred_element_type=jnp.float32) * factor
-    probs = jnp.exp(scores - log_total[..., None])
-    grad_probs = jnp.einsum("lhe,mhe->hlm", grad_mixed, values, preferred_element_type=jnp.float32)
-    inner = jnp.sum(probs * grad_probs, axis=-1, keepdims=True)
-    grad_scores = (probs * (grad_probs - inner)).astype(jnp.bfloat16)
-    grad_queries = (
-        jnp.einsum("hlm,mhe->lhe", grad_scores, keys, preferred_element_type=jnp.float32) * factor
-    ).astype(jnp.bfloat16)
-    grad_keys = (
-        jnp.einsum("hlm,lhe->mhe", grad_scores, queries, preferred_element_type=jnp.float32)
-        * factor
-    ).astype(jnp.bfloat16)
-    grad_values = jnp.einsum(
-        "hlm,lhe->mhe", probs.astype(jnp.bfloat16), grad_mixed, preferred_element_type=jnp.float32
-    ).astype(jnp.bfloat16)
-    return (grad_queries, grad_keys, grad_values)
+    tail = jnp.pad(tail, ((0, 0), (0, 8 * CHUNK - tail.shape[1]))).reshape(1, 16, CHUNK)
+    return [*(main[None, :, i * third : (i + 1) * third] for i in range(3)), tail]
+
+
+def unpack_rows(one, two, three, tail):
+    width = one.shape[1] * 3
+    main = jnp.concatenate([one, two, three], axis=1)
+    return jnp.concatenate([main, tail.reshape(2, 8 * CHUNK)[:, :width]], axis=0)
 
 
 def local(
@@ -598,129 +845,33 @@
     mod_got = exchange(mod_send, True, devices, 1)[:, :slots, : 6 * columns]
     slot_mod = jnp.transpose(mod_got.reshape(devices, slots, 6, columns), (1, 2, 0, 3)).reshape(slots, 6, -1)
     slot_mod = shuffled(slot_mod, matrix).astype(jnp.float32)
-    shift_one = slot_mod[:, 0:1]
-    scale_one = slot_mod[:, 1:2]
-    gate_one = slot_mod[:, 2:3]
-    shift_two = slot_mod[:, 3:4]
-    scale_two = slot_mod[:, 4:5]
-    gate_two = slot_mod[:, 5:6]
-    rows = shuffled(latents, matrix).astype(jnp.float32)
+    rows = shuffled(latents, matrix)
     cotangent = shuffled(cotangent, matrix)
-    b_proj, b_down = shuffled_wide(jnp.stack([b_proj, b_down]), matrix)
+    bias_d = shuffled_wide(jnp.stack([b_proj, b_down]), matrix)
     own_rows = jnp.concatenate([w_qkv[0], w_qkv[1], w_qkv[2], w_proj.T, w_up, w_down.T], axis=1)
     width = own_rows.shape[1]
     head_part = w_qkv.shape[2]
-    left, right = gather_blocks(FIRSTS, pack_rows(own_rows), 2)
-    inner_all, up_all, down_all = unpack_all(left, right, width)
-    qkv_all, proj_all = inner_all[:, : 3 * head_part], inner_all[:, 3 * head_part :]
-    normed_one = widen(modulate(rows, shift_one, scale_one).astype(jnp.bfloat16))
-    length = normed_one.shape[1]
-    head_dim = HEAD_DIM
-    head_count = head_part // head_dim
-    bias_three = jnp.stack([b_qv[0], jnp.zeros_like(b_qv[0]), b_qv[1]])
-    triple = (
-        jnp.einsum("bld,de->ble", normed_one, qkv_all, preferred_element_type=jnp.float32)
-        + bias_three.reshape(-1)
-    ).astype(jnp.bfloat16)
-    triple = [triple[..., i * head_part : (i + 1) * head_part] for i in range(3)]
-    heads_shape = (slots, length, head_count, head_dim)
-    queries = triple[0].reshape(heads_shape)
-    keys = triple[1].reshape(heads_shape)
-    values = triple[2].reshape(heads_shape)
-    attended_heads, log_total = lax.map(attend_forward, (queries, keys, values))
-    attended = attended_heads.reshape(slots, length, head_part)
-    branch = (
-        narrow(jnp.einsum("ble,de->bld", attended, proj_all, preferred_element_type=jnp.float32))
-        + b_proj
+    weights = gather_blocks(pack_rows(own_rows), 2)
+    mods = jnp.concatenate(
+        [slot_mod, jnp.broadcast_to(live[:, None, None], (slots, 2, slot_mod.shape[2]))], axis=1
     )
-    middle = rows + gate_one * branch
-    normed_two = widen(modulate(middle, shift_two, scale_two).astype(jnp.bfloat16))
-    upper = jnp.einsum("bld,df->blf", normed_two, up_all, preferred_element_type=jnp.float32) + b_up
-    acted = gelu_tanh(upper).astype(jnp.bfloat16)
-    down = (
-        narrow(jnp.einsum("blf,df->bld", acted, down_all, preferred_element_type=jnp.float32))
-        + b_down
+    nothing = jnp.zeros_like(b_qv[0])
+    bias_qkv = jnp.concatenate([b_qv[0], nothing, b_qv[1], nothing])[None]
+    block_output, grad_latents, *grads, grad_mod, grad_bd, grad_bqkv, grad_bup = middle_block(
+        (rows, cotangent, mods, bias_d, bias_qkv, b_up[None], *weights), 6
     )
-    alive = live[:, None, None]
-    block_output = straight(((middle + gate_two * down) * alive).astype(jnp.bfloat16), matrix)
-    grad_rows = cotangent.astype(jnp.float32) * alive
-    grad_gate_two = jnp.sum(grad_rows * down, axis=1, keepdims=True)
-    down_low = (gate_two * grad_rows).astype(jnp.bfloat16)
-    grad_b_down = jnp.sum(down_low.astype(jnp.float32), axis=(0, 1))
-    down_wide = widen(down_low)
-    up_use, down_use = (up_all, down_all)
-    grad_acted = jnp.einsum("bld,df->blf", down_wide, down_use, preferred_element_type=jnp.float32)
-    grad_upper = jax.vjp(gelu_tanh, upper)[1](grad_acted)[0]
-    upper_low = grad_upper.astype(jnp.bfloat16)
-    grad_b_up_local = jnp.sum(upper_low.astype(jnp.float32), axis=(0, 1))
-    grad_w_down = jnp.einsum("bld,blf->df", down_wide, acted, preferred_element_type=jnp.float32)
-    grad_w_up = jnp.einsum("bld,blf->df", normed_two, upper_low, preferred_element_type=jnp.float32)
-    grad_normed_two = narrow(
-        jnp.einsum("blf,df->bld", upper_low, up_use, preferred_element_type=jnp.float32)
-    )
-    grad_middle_norm, grad_shift_two, grad_scale_two = jax.vjp(
-        modulate, middle, shift_two, scale_two
-    )[1](grad_normed_two)
-    grad_middle = grad_rows + grad_middle_norm
-    grad_gate_one = jnp.sum(grad_middle * branch, axis=1, keepdims=True)
-    branch_low = (gate_one * grad_middle).astype(jnp.bfloat16)
-    grad_b_proj = jnp.sum(branch_low.astype(jnp.float32), axis=(0, 1))
-    branch_wide = widen(branch_low)
-    qkv_use, proj_use = (qkv_all, proj_all)
-    grad_attended = jnp.einsum(
-        "bld,de->ble", branch_wide, proj_use, preferred_element_type=jnp.float32
-    ).astype(jnp.bfloat16)
-    grad_w_proj = jnp.einsum(
-        "bld,ble->de", branch_wide, attended, preferred_element_type=jnp.float32
-    )
-    grad_queries, grad_keys, grad_values = lax.map(
-        attend_backward, (queries, keys, values, log_total, grad_attended.reshape(heads_shape))
-    )
-    flat_shape = (slots, length, head_part)
-    grad_triple = jnp.concatenate(
-        [
-            grad_queries.reshape(flat_shape),
-            grad_keys.reshape(flat_shape),
-            grad_values.reshape(flat_shape),
-        ],
-        axis=-1,
-    )
-    grad_b_qv_local = jnp.stack(
-        [
-            jnp.sum(grad_queries.astype(jnp.float32), axis=(0, 1)).reshape(-1),
-            jnp.sum(grad_values.astype(jnp.float32), axis=(0, 1)).reshape(-1),
-        ]
-    )
-    grad_w_qkv = jnp.einsum(
-        "bld,ble->de", normed_one, grad_triple, preferred_element_type=jnp.float32
-    )
-    grad_normed_one = narrow(
-        jnp.einsum("ble,de->bld", grad_triple, qkv_use, preferred_element_type=jnp.float32)
-    )
-    grad_rows_norm, grad_shift_one, grad_scale_one = jax.vjp(modulate, rows, shift_one, scale_one)[
-        1
-    ](grad_normed_one)
-    grad_latents = straight_wide(grad_middle + grad_rows_norm, matrix)
-    packed = pack_all(
-        [grads.astype(jnp.bfloat16) for grads in (grad_w_qkv, grad_w_proj, grad_w_up, grad_w_down)]
-    )
-    summed = unpack_rows(*scatter_blocks(FIRSTS, packed, 3), width)
+    block_output = straight(block_output, matrix)
+    grad_latents = straight_wide(grad_latents, matrix)
+    grad_b_qv_local = jnp.stack([grad_bqkv[0, :head_part], grad_bqkv[0, 2 * head_part : 3 * head_part]])
+    grad_b_up_local = grad_bup[0]
+    grad_b_proj, grad_b_down = grad_bd[0], grad_bd[1]
+    summed = unpack_rows(*scatter_blocks(grads, 3))
     grad_w_qkv = jnp.stack([summed[:, i * head_part : (i + 1) * head_part] for i in range(3)])
     grad_w_proj = summed[:, 3 * head_part : 4 * head_part].T
     up_part = w_up.shape[1]
     grad_w_up = summed[:, 4 * head_part : 4 * head_part + up_part]
     grad_w_down = summed[:, 4 * head_part + up_part :].T
-    grad_mod = jnp.concatenate(
-        [
-            grad_shift_one,
-            grad_scale_one,
-            grad_gate_one,
-            grad_shift_two,
-            grad_scale_two,
-            grad_gate_two,
-        ],
-        axis=1,
-    )
+    grad_mod = grad_mod[:, :6]
     grad_mod = straight_wide(grad_mod, matrix).reshape(slots, 6, devices, columns)
     grad_send = jnp.transpose(grad_mod, (2, 0, 1, 3)).reshape(devices, slots, 6 * columns)
     grad_send = jnp.pad(grad_send, ((0, 0), (0, 8 - slots), (0, 128 - 6 * columns)))

time: 480 us -> 344 us (0.72); the launches traced: 471 us -> 340 us
  Pallas kernels: 189 us -> 285 us
  local copies, waits for them, and re-layouts: 105 us -> 21.8 us
  matrix products: 64 us -> 21.6 us
  blocking collectives: 38.1 us -> 0 us
  other arithmetic: 37.6 us -> 9.13 us
  waiting for transfers between devices: 20.4 us -> 0 us
  between operations: 15.2 us -> 1.66 us
    pallas_call x2 -> x3, Pallas kernels: 127 us -> 222 us  [the longest x1 89.1 us: middle_block(): pl.pallas_call(middle_kernel, out_shape=[shape((2, 64, 1152), bf), shape(...]
    dot_general x26 -> x0, matrix products: 43.7 us -> none  [the longest x1 5.33 us: local(): jnp.einsum('bld,blf->df', normed_two, upper_low, preferred_element_type=j...]
    all_gather x4 -> x0, blocking collectives: 38.1 us -> none  [widen(): return lax.all_gather(rows, 'tp', axis=1, tiled=True)]
    slice x13 -> x4, local copies, waits for them, and re-layouts: 34.1 us -> 0.06 us  [the longest x1 0.03 us: local(): grad_b_proj, grad_b_down = (grad_bd[0], grad_bd[1])]
    concatenate x2 -> x1, local copies, waits for them, and re-layouts: 25.1 us -> 0.08 us  [local(): bias_qkv = jnp.concatenate([b_qv[0], nothing, b_qv[1], nothing])[None]]
    reduce_scatter x4 -> x0, waiting for transfers between devices: 20.3 us -> none  [narrow(): lax.psum_scatter(terms.astype(jnp.bfloat16), 'tp', scatter_dimension=1, t...]
    concatenate x4 -> x1, other arithmetic: 16.3 us -> 0.65 us  [local(): jnp.concatenate([slot_mod, jnp.broadcast_to(live[:, None, None], (slots,...]
    reduce_sum x14 -> x0, other arithmetic: 12.6 us -> none  [the longest x2 3.31 us: modulate(): return normed * (1.0 + scale) + shift]
  transfers between devices with their start and end apart: 4 -> 0, of which waited for: 2 -> 0; matrix products, arithmetic and copies ran while one was open for 13% -> 0% of each run, Pallas kernels for 14% -> 0%
where the time goes in v2:
time: 344 us; the launch traced here: 340 us
  Pallas kernels  285 us (83%)
  local copies, waits for them, and re-layouts  21.8 us (6%)
  matrix products  21.6 us (6%)
  other arithmetic  9.13 us (3%)
    pallas_call x1, Pallas kernels, middle_block(): pl.pallas_call(middle_kernel, out_shape=[shape((2, 64, 1152), bf), shape(...  89.1 us
    pallas_call x1, Pallas kernels, scatter_blocks(): pl.pallas_call(scatter_kernel, out_shape=[jax.ShapeDtypeStruct((16, width...  69 us
    pallas_call x1, Pallas kernels, gather_blocks(): pl.pallas_call(gather_kernel, out_shape=[jax.ShapeDtypeStruct((64, 16, wi...  64.2 us
    pallas_call x2, Pallas kernels, exchange(): pl.pallas_call(functools.partial(exchange_kernel, halve), out_shape=jax.S...  35.8 us
    pallas_call x1, Pallas kernels, total_everywhere(): pl.pallas_call(total_kernel, out_shape=jax.ShapeDtypeStruct(parts.shape,...  27.4 us
    dot_general x3, matrix products, straight_wide(): jnp.einsum('...e,de->...d', rows, matrix.astype(jnp.float32), precision=h...  8.41 us

profile of v2, /device:TPU:1, one launch (start us, length us, event | category | flops | bytes accessed | tf_op | source)
XLA Modules:
  0.0 339.5 jit_solution(16174434774532961130)
XLA Ops:
  0.7 0.8 slice_bitcast_fusion.3
  1.5 0.9 concatenate.23
  2.4 1.5 slice_bitcast_fusion
  3.9 1.1 concatenate.24
  5.1 0.6 reshape.282.refs_3_
  5.7 1.6 slice_bitcast_fusion.2.refs_1_
  7.3 64.2 %shard_map.247 = (bf16[64,16,2304]{2,1,0:T(8,128)(2,1)}, bf16[64,16,2304]{2,1,0:T(8,128)(2,1)}, bf16[64,16,2304]{2,1,0:T(8,128)(2,1)}, bf16[64,16,896]{2,1,0:T(8,128)(2,1)}) custom-call(bf16[1,16,2304]{2,1,0:T(8,128)(2,1)} %get-tuple-element.112.refs_0_, bf16[1,16,2304]{2,1,0:T(8,128)(2,1)} %slice_bitcast_fusion.2.refs_1_, ...), custom_call_target="tpu_custom_call" | custom-call | tf_op jit(solution)/shard_map/pallas_call | solution.py:160
  71.5 0.7 copy.47
  72.2 0.1 reduce-window.9
  72.3 0.1 reduce
  72.4 1.3 fusion.114
  73.8 0.1 min.12
  73.9 0.8 select_reduce_fusion
  74.7 1.5 fusion.44
  76.3 0.1 convolution_convert_fusion
  76.4 0.1 copy.49
  76.5 0.8 pad.16.in_ref
  77.3 17.5 %shard_map.246 = bf16[128,16,128]{2,1,0:T(8,128)(2,1)} custom-call(bf16[64,16,128]{2,1,0:T(8,128)(2,1)} %pad.16.in_ref), custom_call_target="tpu_custom_call" | custom-call | tf_op jit(solution)/shard_map/pallas_call | solution.py:407
  94.8 1.0 slice.92
  95.8 0.1 copy.50
  95.9 0.3 copy.61
  96.2 0.5 reshape.298
  96.7 1.0 fusion.41
  97.7 0.7 compare_convert_fusion
  98.5 0.7 pad_maximum_fusion.5.refs_2_
  99.1 1.9 fusion.32.refs_1_
  101.0 1.9 fusion.35.refs_0_
  102.9 2.3 fusion.refs_3_
  105.3 0.6 broadcast_in_dim.74.refs_4_
  105.9 0.6 broadcast_in_dim.75.refs_5_
  106.5 89.1 %shard_map.248 = (bf16[2,64,1152]{2,1,0:T(8,128)(2,1)}, f32[2,64,1152]{2,1,0:T(8,128)}, bf16[64,16,2304]{2,1,0:T(8,128)(2,1)}, bf16[64,16,2304]{2,1,0:T(8,128)(2...) custom-call(bf16[2,64,1152]{2,1,0:T(8,128)(2,1)} %fusion.35.refs_0_,, ...), custom_call_target="tpu_custom_call" | custom-call | tf_op jit(solution)/shard_map/pallas_call | solution.py:732
  195.7 69.0 %shard_map.251 = (f32[16,2304]{1,0:T(8,128)}, f32[16,2304]{1,0:T(8,128)}, f32[16,2304]{1,0:T(8,128)}, f32[16,896]{1,0:T(8,128)}) custom-call(bf16[64,16,2304]{2,1,0:T(8,128)(2,1)} %get-tuple-element.41.refs_0_, bf16[64,16,2304]{2,1,0:T(8,128)(2,1)} %get-tuple-element.42.refs_1_, bf16[64,16,2304]{2,1,0:T(8,128)(2,1)} %get-tuple-element.43.refs_2_, ...), custom_call_target="tpu_custom_call" | custom-call | tf_op jit(solution)/shard_map/pallas_call | solution.py:325
  264.7 0.9 reshape.291
  265.6 1.8 fusion.56
  267.4 0.3 dynamic_update_slice.6
  267.7 2.5 fusion.3
  270.3 0.7 reshape.283
  271.0 0.3 copy.54
  271.3 0.1 copy.55
  271.4 0.8 pad.18.in_ref
  272.2 18.3 %shard_map.249 = f32[128,8,128]{2,1,0:T(8,128)} custom-call(f32[128,8,128]{2,1,0:T(8,128)} %pad.18.in_ref), custom_call_target="tpu_custom_call" | custom-call | tf_op jit(solution)/shard_map/pallas_call | solution.py:407
  290.5 1.1 bitcast_reduce_fusion
  291.8 0.2 lt.160
  291.9 0.1 select_bitcast_fusion
  292.1 0.9 fusion.115
  293.0 0.4 convolution_bitcast_fusion
  293.6 0.3 dynamic_update_slice.7
  294.0 0.8 pad_bitcast_fusion.in_ref
  294.8 27.4 %shard_map.250 = f32[128,8,128]{2,1,0:T(8,128)} custom-call(f32[128,8,128]{2,1,0:T(8,128)} %pad_bitcast_fusion.in_ref), custom_call_target="tpu_custom_call" | custom-call | tf_op jit(solution)/shard_map/pallas_call | solution.py:437
  322.2 0.8 fusion.112
  323.0 2.4 fusion.1
  325.4 0.7 slice_reduce_fusion
  326.1 0.7 maximum_bitcast_fusion
  326.8 0.7 pad_maximum_fusion.4
  327.5 1.0 slice.108
  328.5 0.1 reshape.290
  328.6 0.9 fusion.50
  329.6 0.7 slice.127
  330.3 0.7 dynamic_slice.7
  331.0 0.7 slice.124
  331.7 0.7 constant_dynamic-slice_fusion
  332.4 1.3 fusion.51
  333.7 3.5 %fusion.5 = f32[2,64,1152]{2,1,0:T(8,128)} fusion(f32[2,64,1152]{2,1,0:T(8,128)S(1)} %copy-done.14, s32[1152]{0:T(1024)S(1)} %fusion.84), kind=kOutput, calls=%fused_computation.5 | convolution fusion | flops 2039758848 | bytes 1184256 | tf_op jit(solution)/shard_map/...e,de->...d/dot_general | solution.py:787
  337.2 1.8 fusion.29
  (68 shorter events, 0.9 us)
Async XLA Ops:
  0.6 98.5 %copy-start = (bf16[2,64,1152]{2,1,0:T(8,128)(2,1)S(1)}, bf16[2,64,1152]{2,1,0:T(8,128)(2,1)}, u32[]{:S(2)}) copy-start(bf16[2,64,1152]{2,1,0:T(8,128)(2,1)} %param.29) | copy-start | bytes 884740
  5.7 95.3 %copy-start.15 = (bf16[2,64,1152]{2,1,0:T(8,128)(2,1)S(1)}, bf16[2,64,1152]{2,1,0:T(8,128)(2,1)}, u32[]{:S(2)}) copy-start(bf16[2,64,1152]{2,1,0:T(8,128)(2,1)} %param.15) | copy-start | bytes 884740
  76.2 26.6 %copy-start.9 = (f32[1152]{0:T(1024)S(1)}, f32[1152]{0:T(1024)}, u32[]{:S(2)}) copy-start(f32[1152]{0:T(1024)} %param.24) | copy-start | bytes 13828
  76.2 26.6 %copy-start.10 = (f32[1152]{0:T(1024)S(1)}, f32[1152]{0:T(1024)}, u32[]{:S(2)}) copy-start(f32[1152]{0:T(1024)} %param.28) | copy-start | bytes 13828
  94.8 10.4 %copy-start.11 = (f32[2,576]{1,0:T(2,128)S(1)}, f32[2,576]{1,0:T(2,128)}, u32[]{:S(2)}) copy-start(f32[2,576]{1,0:T(2,128)} %param.22) | copy-start | bytes 13828
  94.8 11.1 %copy-start.6 = (f32[2304]{0:T(1024)S(1)}, f32[2304]{0:T(1024)}, u32[]{:S(2)}) copy-start(f32[2304]{0:T(1024)} %param.26) | copy-start | bytes 27652
  195.6 71.7 %copy-start.13 = (f32[1,1792]{1,0:T(1,128)S(1)}, f32[1,1792]{1,0:T(1,128)}, u32[]{:S(2)}) copy-start(f32[1,1792]{1,0:T(1,128)} %get-tuple-element.39) | copy-start | bytes 21508
  195.7 72.1 %copy-start.17 = (f32[2,8,1152]{2,1,0:T(8,128)S(1)}, f32[2,8,1152]{2,1,0:T(8,128)}, u32[]{:S(2)}) copy-start(f32[2,8,1152]{2,1,0:T(8,128)} %get-tuple-element.37) | copy-start | bytes 221188
  264.7 27.0 %copy-start.12 = (s32[64]{0:T(128)S(1)}, s32[64]{0:T(128)}, u32[]{:S(2)}) copy-start(s32[64]{0:T(128)} %param.17) | copy-start | bytes 772
  264.7 28.3 %copy-start.4 = (bf16[1152,6,9]{0,1,2:T(8,128)(2,1)S(1)}, bf16[1152,6,9]{0,1,2:T(8,128)(2,1)}, u32[]{:S(2)}) copy-start(bf16[1152,6,9]{0,1,2:T(8,128)(2,1)} %param.19) | copy-start | bytes 373252
  264.7 28.8 %copy-start.7 = (f32[2,1152]{1,0:T(2,128)S(1)}, f32[2,1152]{1,0:T(2,128)}, u32[]{:S(2)}) copy-start(f32[2,1152]{1,0:T(2,128)} %get-tuple-element.38) | copy-start | bytes 27652
  265.6 28.0 %copy-start.8 = (f32[1,2304]{1,0:T(1,128)S(1)}, f32[1,2304]{1,0:T(1,128)}, u32[]{:S(2)}) copy-start(f32[1,2304]{1,0:T(1,128)} %get-tuple-element.40) | copy-start | bytes 27652
  271.0 55.1 %copy-start.1 = (f32[16,2304]{1,0:T(8,128)S(1)}, f32[16,2304]{1,0:T(8,128)}, u32[]{:S(2)}) copy-start(f32[16,2304]{1,0:T(8,128)} %get-tuple-element.45) | copy-start | bytes 442372
  271.0 55.1 %copy-start.2 = (f32[16,2304]{1,0:T(8,128)S(1)}, f32[16,2304]{1,0:T(8,128)}, u32[]{:S(2)}) copy-start(f32[16,2304]{1,0:T(8,128)} %get-tuple-element.46) | copy-start | bytes 442372
  271.0 55.1 %copy-start.3 = (f32[16,2304]{1,0:T(8,128)S(1)}, f32[16,2304]{1,0:T(8,128)}, u32[]{:S(2)}) copy-start(f32[16,2304]{1,0:T(8,128)} %get-tuple-element.47) | copy-start | bytes 442372
  291.9 36.7 %copy-start.5 = (bf16[96,1152]{1,0:T(8,128)(2,1)S(1)}, bf16[96,1152]{1,0:T(8,128)(2,1)}, u32[]{:S(2)}) copy-start(bf16[96,1152]{1,0:T(8,128)(2,1)} %param.16) | copy-start | bytes 663556
  294.0 39.7 %copy-start.14 = (f32[2,64,1152]{2,1,0:T(8,128)S(1)}, f32[2,64,1152]{2,1,0:T(8,128)}, u32[]{:S(2)}) copy-start(f32[2,64,1152]{2,1,0:T(8,128)} %get-tuple-element.36) | copy-start | bytes 1769476
  323.0 14.2 %copy-start.16 = (bf16[2,64,1152]{2,1,0:T(8,128)(2,1)S(1)}, bf16[2,64,1152]{2,1,0:T(8,128)(2,1)}, u32[]{:S(2)}) copy-start(bf16[2,64,1152]{2,1,0:T(8,128)(2,1)} %get-tuple-element.35) | copy-start | bytes 884740

commit v3 on v2

--- a/solution.py
+++ b/solution.py
@@ -19,6 +19,9 @@
     (2, 0, 1152, "z"),
     (2, 1152, 1152, "y"),
 )
+ONE, TWO, THREE = (0, 1, 2), (3, 4), (5, 6)
+ALL = ONE + TWO + THREE
+BACK = (3, 2, 1, 0)
 
 
 highest = lax.Precision.HIGHEST
@@ -39,138 +42,16 @@
         "y": (at(z, (y + 3) % 4, x, c), at(z, (y + 1) % 4, x, c)),
         "x": at(z, y, 1 - x, c),
         "c": at(z, y, x, 1 - c),
+        "t": (z * 16 + y * 4 + x * 2 + c, 1 - t),
     }
 
 
 def greet(near):
     barrier = pltpu.get_barrier_semaphore()
-    group = (*near["z"], *near["y"], near["x"], near["c"])
+    group = (*near["z"], *near["y"], near["x"], near["c"], near["t"])
     for peer in group:
         pl.semaphore_signal(barrier, inc=1, device_id=peer, device_id_type=MESH)
     pl.semaphore_wait(barrier, len(group))
-
-
-def gather_kernel(*refs):
-    n, m = len(PIECES), len(WIDTHS)
-    ins, outs = refs[:m], refs[m : 2 * m]
-    local_sem, send_sem, recv_sem, core_send, core_recv = refs[2 * m :]
-    z, y, x, c, t = place_of()
-    near = peers(z, y, x, c, t)
-    greet(near)
-    started = []
-
-    def spot(p, u, v, core=c):
-        return core * 32 + (u * 8 + v * 2 if PIECES[p][3] == "z" else v * 8 + u * 2)
-
-    def block(p, at, count=1):
-        r, low, width, first = PIECES[p]
-        return outs[r].at[pl.ds(at, count), :, pl.ds(low, width)]
-
-    def remote(src, dst, ssem, rsem, peer):
-        return pltpu.make_async_remote_copy(
-            src_ref=src, dst_ref=dst, send_sem=ssem, recv_sem=rsem, device_id=peer, device_id_type=MESH
-        )
-
-    def send(p, k, ref, peer, src=None):
-        cp = remote(ref if src is None else src, ref, send_sem.at[p, k], recv_sem.at[p, k], peer)
-        cp.start()
-        started.append(cp)
-
-    def arrive(p, k, ref):
-        remote(ref, ref, send_sem.at[p, k], recv_sem.at[p, k], near["x"]).wait_recv()
-
-    def share(p, k, ref):
-        cp = remote(ref, ref, core_send.at[p, k], core_recv.at[p, k], near["c"])
-        cp.start()
-        started.append(cp)
-
-    def axes(p):
-        if PIECES[p][3] == "z":
-            return z, y, near["z"], near["y"]
-        return y, z, near["y"], near["z"]
-
-    locals_ = []
-    for p in range(n):
-        r, low, width, first = PIECES[p]
-        mine = ins[r].at[:, :, pl.ds(low, width)]
-        own = block(p, c * 32 + z * 8 + y * 2 + x)
-        send(p, 0, own, near["x"], mine)
-        cp = pltpu.make_async_copy(mine, own, local_sem.at[p])
-        cp.start()
-        locals_.append(cp)
-    for p in range(n):
-        u, v, one, two = axes(p)
-        locals_[p].wait()
-        arrive(p, 0, block(p, c * 32 + z * 8 + y * 2 + 1 - x))
-        pair = block(p, spot(p, u, v), 2)
-        send(p, 1, pair, one[1])
-        send(p, 2, pair, one[0])
-        share(p, 0, pair)
-    for p in range(n):
-        u, v, one, two = axes(p)
-        pair = block(p, spot(p, u, v), 2)
-        send(p, 5, pair, two[1])
-        send(p, 6, pair, two[0])
-    for p in range(n):
-        u, v, one, two = axes(p)
-        for k, way in ((1, 1), (2, 0)):
-            uu = (u + OFFS[k]) % 4
-            pair = block(p, spot(p, uu, v), 2)
-            arrive(p, k, pair)
-            send(p, 2 + k, block(p, spot(p, uu, v) + 1 - way), one[way])
-            send(p, 5 + 4 * k, pair, two[1])
-            send(p, 6 + 4 * k, pair, two[0])
-            share(p, 4 * k, pair)
-    for p in range(n):
-        u, v, one, two = axes(p)
-        uu = (u + 2) % 4
-        arrive(p, 3, block(p, spot(p, uu, v) + 0))
-        arrive(p, 4, block(p, spot(p, uu, v) + 1))
-        pair = block(p, spot(p, uu, v), 2)
-        send(p, 17, pair, two[1])
-        send(p, 18, pair, two[0])
-        share(p, 12, pair)
-    for k in range(4):
-        for p in range(n):
-            u, v, one, two = axes(p)
-            uu = (u + OFFS[k]) % 4
-            for side, way in ((1, 1), (2, 0)):
-                vv = (v + OFFS[side]) % 4
-                pair = block(p, spot(p, uu, vv), 2)
-                arrive(p, 4 + 4 * k + side, pair)
-                send(p, 6 + 4 * k + side, block(p, spot(p, uu, vv) + 1 - way), two[way])
-                share(p, 4 * k + side, pair)
-    for k in range(4):
-        for p in range(n):
-            u, v, one, two = axes(p)
-            uu, vv = (u + OFFS[k]) % 4, (v + 2) % 4
-            arrive(p, 7 + 4 * k, block(p, spot(p, uu, vv) + 0))
-            arrive(p, 8 + 4 * k, block(p, spot(p, uu, vv) + 1))
-            share(p, 4 * k + 3, block(p, spot(p, uu, vv), 2))
-    for p in range(n):
-        for k in range(16):
-            ref = block(p, (1 - c) * 32 + 2 * k, 2)
-            remote(ref, ref, core_send.at[p, k], core_recv.at[p, k], near["c"]).wait_recv()
-    for cp in started:
-        cp.wait_send()
-
-
-def gather_blocks(parts, collective_id):
-    n, m = len(PIECES), len(WIDTHS)
-    return pl.pallas_call(
-        gather_kernel,
-        out_shape=[jax.ShapeDtypeStruct((64, 16, width), jnp.bfloat16) for width in WIDTHS],
-        in_specs=[pl.BlockSpec(memory_space=pl.ANY)] * m,
-        out_specs=[pl.BlockSpec(memory_space=pl.ANY)] * m,
-        scratch_shapes=[
-            pltpu.SemaphoreType.DMA((n,)),
-            pltpu.SemaphoreType.DMA((n, 21)),
-            pltpu.SemaphoreType.DMA((n, 21)),
-            pltpu.SemaphoreType.DMA((n, 16)),
-            pltpu.SemaphoreType.DMA((n, 16)),
-        ],
-        compiler_params=pltpu.CompilerParams(collective_id=collective_id, has_side_effects=True),
-    )(*parts)
 
 
 def add_into(dst, *srcs):
@@ -186,164 +67,6 @@
         return carry
 
     lax.fori_loop(0, width // 128, step, 0)
-
-
-def scatter_kernel(*refs):
-    n, m = len(PIECES), len(WIDTHS)
-    grads, outs = refs[:m], refs[m : 2 * m]
-    refs = refs[2 * m :]
-    twins, sums, inner, mids, outer, ends, last = (refs[i * n : (i + 1) * n] for i in range(7))
-    send_sem, recv_sem, core_send, core_recv = refs[7 * n :]
-    z, y, x, c, t = place_of()
-    near = peers(z, y, x, c, t)
-    greet(near)
-    started = []
-
-    def remote(src, dst, ssem, rsem, peer):
-        return pltpu.make_async_remote_copy(
-            src_ref=src, dst_ref=dst, send_sem=ssem, recv_sem=rsem, device_id=peer, device_id_type=MESH
-        )
-
-    def axes(p):
-        if PIECES[p][3] == "z":
-            return z, y, near["z"], near["y"]
-        return y, z, near["y"], near["z"]
-
-    def spot(p, u, v):
-        return u * 8 + v * 2 if PIECES[p][3] == "z" else v * 8 + u * 2
-
-    def grad(p, at, count):
-        r, low, width, first = PIECES[p]
-        return grads[r].at[pl.ds(at, count), :, pl.ds(low, width)]
-
-    def total(p, at, count):
-        return sums[p].at[pl.ds(at, count)]
-
-    def send(p, k, src, dst, peer):
-        cp = remote(src, dst, send_sem.at[p, k], recv_sem.at[p, k], peer)
-        cp.start()
-        started.append(cp)
-
-    def arrive(p, k, ref):
-        remote(ref, ref, send_sem.at[p, k], recv_sem.at[p, k], near["x"]).wait_recv()
-
-    order = (3, 2, 1, 0)
-    sides = (3, 2, 1, 0)
-    for side in sides:
-        for k in order:
-            for p in range(n):
-                u, v, one, two = axes(p)
-                at = spot(p, (u + OFFS[k]) % 4, (v + OFFS[side]) % 4)
-                j = 4 * k + side
-                cp = remote(
-                    grad(p, (1 - c) * 32 + at, 2), twins[p].at[pl.ds(at, 2)], core_send.at[p, j], core_recv.at[p, j], near["c"]
-                )
-                cp.start()
-                started.append(cp)
-
-    def combine(p, k, side):
-        u, v, one, two = axes(p)
-        at = spot(p, (u + OFFS[k]) % 4, (v + OFFS[side]) % 4)
-        j = 4 * k + side
-        twin = twins[p].at[pl.ds(at, 2)]
-        remote(twin, twin, core_send.at[p, j], core_recv.at[p, j], near["c"]).wait_recv()
-        add_into(total(p, at, 2), grad(p, c * 32 + at, 2), twin)
-
-    for k in order:
-        for p in range(n):
-            u, v, one, two = axes(p)
-            combine(p, k, 3)
-            src = sums[p].at[pl.ds(spot(p, (u + OFFS[k]) % 4, (v + 2) % 4), 2)]
-            send(p, 6 * k, src.at[0], inner[p].at[k, 0], two[1])
-            send(p, 6 * k + 1, src.at[1], inner[p].at[k, 1], two[0])
-    for k in order:
-        for p in range(n):
-            u, v, one, two = axes(p)
-            combine(p, k, 2)
-            src = sums[p].at[pl.ds(spot(p, (u + OFFS[k]) % 4, (v + 1) % 4), 2)]
-            send(p, 6 * k + 2, src.at[1], inner[p].at[k, 2], two[1])
-            combine(p, k, 1)
-            src = sums[p].at[pl.ds(spot(p, (u + OFFS[k]) % 4, (v + 3) % 4), 2)]
-            send(p, 6 * k + 4, src.at[0], inner[p].at[k, 4], two[0])
-    for k in order:
-        for p in range(n):
-            u, v, one, two = axes(p)
-            arrive(p, 6 * k, inner[p].at[k, 0])
-            src = sums[p].at[spot(p, (u + OFFS[k]) % 4, (v + 1) % 4) + 0]
-            add_into(src, src, inner[p].at[k, 0])
-            send(p, 6 * k + 3, src, inner[p].at[k, 3], two[1])
-            arrive(p, 6 * k + 1, inner[p].at[k, 1])
-            src = sums[p].at[spot(p, (u + OFFS[k]) % 4, (v + 3) % 4) + 1]
-            add_into(src, src, inner[p].at[k, 1])
-            send(p, 6 * k + 5, src, inner[p].at[k, 5], two[0])
-    for k in order:
-        for p in range(n):
-            combine(p, k, 0)
-    for k in order:
-        for p in range(n):
-            u, v, one, two = axes(p)
-            own = sums[p].at[pl.ds(spot(p, (u + OFFS[k]) % 4, v), 2)]
-            for j in range(2, 6):
-                arrive(p, 6 * k + j, inner[p].at[k, j])
-            add_into(mids[p].at[k, 0], own.at[0], inner[p].at[k, 3], inner[p].at[k, 4])
-            add_into(mids[p].at[k, 1], own.at[1], inner[p].at[k, 2], inner[p].at[k, 5])
-            if k == 3:
-                send(p, 24, mids[p].at[3, 0], outer[p].at[0], one[1])
-                send(p, 25, mids[p].at[3, 1], outer[p].at[1], one[0])
-            if k == 2:
-                send(p, 26, mids[p].at[2, 1], outer[p].at[2], one[1])
-            if k == 1:
-                send(p, 28, mids[p].at[1, 0], outer[p].at[4], one[0])
-    for p in range(n):
-        u, v, one, two = axes(p)
-        arrive(p, 24, outer[p].at[0])
-        add_into(mids[p].at[2, 0], mids[p].at[2, 0], outer[p].at[0])
-        send(p, 27, mids[p].at[2, 0], outer[p].at[3], one[1])
-        arrive(p, 25, outer[p].at[1])
-        add_into(mids[p].at[1, 1], mids[p].at[1, 1], outer[p].at[1])
-        send(p, 29, mids[p].at[1, 1], outer[p].at[5], one[0])
-    for p in range(n):
-        for j in range(2, 6):
-            arrive(p, 24 + j, outer[p].at[j])
-        add_into(ends[p].at[0], mids[p].at[0, 0], outer[p].at[3], outer[p].at[4])
-        add_into(ends[p].at[1], mids[p].at[0, 1], outer[p].at[2], outer[p].at[5])
-        send(p, 30, ends[p].at[1 - x], last[p], near["x"])
-    for p in range(n):
-        arrive(p, 30, last[p])
-        r, low, width, first = PIECES[p]
-        add_into(outs[r].at[:, pl.ds(low, width)], ends[p].at[x], last[p])
-    for cp in started:
-        cp.wait_send()
-
-
-def scatter_blocks(parts, collective_id):
-    n, m = len(PIECES), len(WIDTHS)
-
-    def room(*lead):
-        return [pltpu.VMEM(lead + (16, piece[2]), jnp.bfloat16) for piece in PIECES]
-
-    return pl.pallas_call(
-        scatter_kernel,
-        out_shape=[jax.ShapeDtypeStruct((16, width), jnp.float32) for width in WIDTHS],
-        in_specs=[pl.BlockSpec(memory_space=pltpu.VMEM)] * m,
-        out_specs=[pl.BlockSpec(memory_space=pltpu.VMEM)] * m,
-        scratch_shapes=[
-            *room(32),
-            *room(32),
-            *room(4, 6),
-            *room(4, 2),
-            *room(6),
-            *room(2),
-            *room(),
-            pltpu.SemaphoreType.DMA((n, 31)),
-            pltpu.SemaphoreType.DMA((n, 31)),
-            pltpu.SemaphoreType.DMA((n, 16)),
-            pltpu.SemaphoreType.DMA((n, 16)),
-        ],
-        compiler_params=pltpu.CompilerParams(
-            collective_id=collective_id, has_side_effects=True, vmem_limit_bytes=60 * 1024 * 1024
-        ),
-    )(*parts)
 
 
 def everyone():
@@ -496,26 +219,231 @@
     lax.fori_loop(0, count, step, 0)
 
 
-def middle_kernel(*refs):
-    (lat, cot, mods, bias_d, bias_qkv, bias_up, w1, w2, w3, wt) = refs[:10]
-    (out, grad_lat, g1, g2, g3, gt, grad_mod, grad_bd, grad_bqkv, grad_bup) = refs[10:20]
+def block_kernel(*refs):
+    n, m = len(PIECES), len(WIDTHS)
+    (lat, cot, mods, bias_d, bias_qkv, bias_up), ins = refs[:6], refs[6 : 6 + m]
+    refs = refs[6 + m :]
+    (out, grad_lat), outs, (grad_mod, grad_bd, grad_bqkv, grad_bup) = refs[:2], refs[2 : 2 + m], refs[2 + m : 6 + m]
+    refs = refs[6 + m :]
+    ws, twins = refs[:m], refs[m : 2 * m]
+    refs = refs[2 * m :]
+    inner, outer, last = (refs[i * n : (i + 1) * n] for i in range(3))
     (
         tail_w, tail_g, wide1, wideg, wide2, wideb, flip1, flipg, flip2, flipb,
-        narrow_send, narrow_recv, part, qkvp, mixp, probs, gattp, gqkvp, qk, gqkv, att,
-        upper, acted, gup, middle, branch, down_keep, unit2, send_sem, recv_sem,
-    ) = refs[20:]
+        narrow_send, narrow_recv, part, qkvp, probs, gattp, qk, gqkv, att,
+        upper, acted, gup, middle, branch, down_keep, send_sem, recv_sem,
+        local_sem, way_send, core_send, way_recv, core_recv, back_recv, back_core,
+    ) = refs[3 * n :]
+    w1, w2, w3, wt = ws
     slots = lat.shape[0]
     z, y, x, c, t = place_of()
-    partner = (lax.axis_index("fsdp"), 1 - t)
-    barrier = pltpu.get_barrier_semaphore()
-    pl.semaphore_signal(barrier, inc=1, device_id=partner, device_id_type=MESH)
-    pl.semaphore_wait(barrier, 1)
+    near = peers(z, y, x, c, t)
+    partner = near["t"]
+    greet(near)
+    pending = {p: [] for p in range(n)}
+
+    def far(src, dst, ssem, rsem, peer):
+        return pltpu.make_async_remote_copy(
+            src_ref=src, dst_ref=dst, send_sem=ssem, recv_sem=rsem, device_id=peer, device_id_type=MESH
+        )
+
+    def axes(p):
+        if PIECES[p][3] == "z":
+            return z, y, near["z"], near["y"]
+        return y, z, near["y"], near["z"]
+
+    def spot(p, u, v, core=c):
+        return core * 32 + (u * 8 + v * 2 if PIECES[p][3] == "z" else v * 8 + u * 2)
+
+    def block(p, at, count=1, of=ws):
+        r, low, width, first = PIECES[p]
+        return of[r].at[pl.ds(at, count), :, pl.ds(low, width)]
+
+    def push(p, k, ref, peer, src=None):
+        cp = far(ref if src is None else src, ref, way_send.at[p, k], way_recv.at[p, k], peer)
+        cp.start()
+        pending[p].append(cp)
+
+    def arrive(p, k, ref):
+        far(ref, ref, way_send.at[p, k], way_recv.at[p, k], near["x"]).wait_recv()
+
+    def share(p, k, ref):
+        cp = far(ref, ref, core_send.at[p, k], core_recv.at[p, k], near["c"])
+        cp.start()
+        pending[p].append(cp)
+
+    def gather_begin(p):
+        r, low, width, first = PIECES[p]
+        mine = ins[r].at[:, :, pl.ds(low, width)]
+        own = block(p, c * 32 + z * 8 + y * 2 + x)
+        push(p, 0, own, near["x"], mine)
+        pltpu.make_async_copy(mine, own, local_sem.at[p]).start()
+
+    def gather_x(p):
+        u, v, one, two = axes(p)
+        r, low, width, first = PIECES[p]
+        own = block(p, c * 32 + z * 8 + y * 2 + x)
+        pltpu.make_async_copy(ins[r].at[:, :, pl.ds(low, width)], own, local_sem.at[p]).wait()
+        arrive(p, 0, block(p, c * 32 + z * 8 + y * 2 + 1 - x))
+        pair = block(p, spot(p, u, v), 2)
+        push(p, 1, pair, one[1])
+        push(p, 2, pair, one[0])
+        share(p, 0, pair)
+
+    def gather_first(p):
+        u, v, one, two = axes(p)
+        for k, way in ((1, 1), (2, 0)):
+            uu = (u + OFFS[k]) % 4
+            pair = block(p, spot(p, uu, v), 2)
+            arrive(p, k, pair)
+            push(p, 2 + k, block(p, spot(p, uu, v) + 1 - way), one[way])
+            share(p, 4 * k, pair)
+
+    def gather_first_end(p):
+        u, v, one, two = axes(p)
+        uu = (u + 2) % 4
+        arrive(p, 3, block(p, spot(p, uu, v)))
+        arrive(p, 4, block(p, spot(p, uu, v) + 1))
+        share(p, 12, block(p, spot(p, uu, v), 2))
+
+    def gather_second(p, ks):
+        u, v, one, two = axes(p)
+        for k in ks:
+            pair = block(p, spot(p, (u + OFFS[k]) % 4, v), 2)
+            push(p, 5 + 4 * k, pair, two[1])
+            push(p, 6 + 4 * k, pair, two[0])
+
+    def gather_relay(p, ks):
+        u, v, one, two = axes(p)
+        for k in ks:
+            uu = (u + OFFS[k]) % 4
+            for side, way in ((1, 1), (2, 0)):
+                vv = (v + OFFS[side]) % 4
+                pair = block(p, spot(p, uu, vv), 2)
+                arrive(p, 4 + 4 * k + side, pair)
+                push(p, 6 + 4 * k + side, block(p, spot(p, uu, vv) + 1 - way), two[way])
+                share(p, 4 * k + side, pair)
+
+    def gather_end(p, ks):
+        u, v, one, two = axes(p)
+        for k in ks:
+            uu, vv = (u + OFFS[k]) % 4, (v + 2) % 4
+            arrive(p, 7 + 4 * k, block(p, spot(p, uu, vv)))
+            arrive(p, 8 + 4 * k, block(p, spot(p, uu, vv) + 1))
+            share(p, 4 * k + 3, block(p, spot(p, uu, vv), 2))
+
+    def gather_core(p):
+        for k in range(16):
+            ref = block(p, (1 - c) * 32 + 2 * k, 2)
+            far(ref, ref, core_send.at[p, k], core_recv.at[p, k], near["c"]).wait_recv()
+
+    def sent(p):
+        for cp in pending[p]:
+            cp.wait_send()
+        pending[p].clear()
+
+    def back(p, k, src, dst, peer):
+        cp = far(src, dst, way_send.at[p, k], back_recv.at[p, k], peer)
+        cp.start()
+        pending[p].append(cp)
+
+    def came(p, k, ref):
+        far(ref, ref, way_send.at[p, k], back_recv.at[p, k], near["x"]).wait_recv()
+
+    def twin_of(p, at):
+        return block(p, at, 2, twins)
+
+    def scatter_twin(p):
+        u, v, one, two = axes(p)
+        for side in BACK:
+            for k in BACK:
+                at = spot(p, (u + OFFS[k]) % 4, (v + OFFS[side]) % 4, 0)
+                j = 4 * k + side
+                cp = far(block(p, (1 - c) * 32 + at, 2), twin_of(p, at), core_send.at[p, j], back_core.at[p, j], near["c"])
+                cp.start()
+                pending[p].append(cp)
+
+    def combine(p, k, side):
+        u, v, one, two = axes(p)
+        at = spot(p, (u + OFFS[k]) % 4, (v + OFFS[side]) % 4, 0)
+        j = 4 * k + side
+        twin = twin_of(p, at)
+        far(twin, twin, core_send.at[p, j], back_core.at[p, j], near["c"]).wait_recv()
+        own = block(p, c * 32 + at, 2)
+        add_into(own, own, twin)
+        return c * 32 + at
+
+    def scatter_relay(p, ks):
+        u, v, one, two = axes(p)
+        for k in ks:
+            at = combine(p, k, 3)
+            back(p, 6 * k, block(p, at), inner[p].at[k, pl.ds(0, 1)], two[1])
+            back(p, 6 * k + 1, block(p, at + 1), inner[p].at[k, pl.ds(1, 1)], two[0])
+
+    def scatter_direct(p, ks):
+        u, v, one, two = axes(p)
+        for k in ks:
+            at = combine(p, k, 2)
+            back(p, 6 * k + 2, block(p, at + 1), inner[p].at[k, pl.ds(2, 1)], two[1])
+            at = combine(p, k, 1)
+            back(p, 6 * k + 4, block(p, at), inner[p].at[k, pl.ds(4, 1)], two[0])
+
+    def scatter_on(p, ks):
+        u, v, one, two = axes(p)
+        for k in ks:
+            for j, side, way in ((0, 2, 1), (1, 1, 0)):
+                came(p, 6 * k + j, inner[p].at[k, pl.ds(j, 1)])
+                own = block(p, spot(p, (u + OFFS[k]) % 4, (v + OFFS[side]) % 4) + j)
+                add_into(own, own, inner[p].at[k, pl.ds(j, 1)])
+                back(p, 6 * k + 3 + 2 * j, own, inner[p].at[k, pl.ds(3 + 2 * j, 1)], two[way])
+
+    def scatter_middle(p, ks):
+        u, v, one, two = axes(p)
+        for k in ks:
+            at = combine(p, k, 0)
+            for j in range(2, 6):
+                came(p, 6 * k + j, inner[p].at[k, pl.ds(j, 1)])
+            held = [inner[p].at[k, pl.ds(j, 1)] for j in range(6)]
+            add_into(block(p, at), block(p, at), held[3], held[4])
+            add_into(block(p, at + 1), block(p, at + 1), held[2], held[5])
+            if k == 3:
+                back(p, 24, block(p, at), outer[p].at[pl.ds(0, 1)], one[1])
+                back(p, 25, block(p, at + 1), outer[p].at[pl.ds(1, 1)], one[0])
+            if k == 2:
+                back(p, 26, block(p, at + 1), outer[p].at[pl.ds(2, 1)], one[1])
+            if k == 1:
+                back(p, 28, block(p, at), outer[p].at[pl.ds(4, 1)], one[0])
+
+    def scatter_outer(p):
+        u, v, one, two = axes(p)
+        for j, side, way in ((0, 2, 1), (1, 1, 0)):
+            came(p, 24 + j, outer[p].at[pl.ds(j, 1)])
+            own = block(p, spot(p, (u + OFFS[side]) % 4, v) + j)
+            add_into(own, own, outer[p].at[pl.ds(j, 1)])
+            back(p, 27 + 2 * j, own, outer[p].at[pl.ds(3 + 2 * j, 1)], one[way])
+
+    def scatter_x(p):
+        u, v, one, two = axes(p)
+        for j in range(2, 6):
+            came(p, 24 + j, outer[p].at[pl.ds(j, 1)])
+        held = [outer[p].at[pl.ds(j, 1)] for j in range(6)]
+        at = spot(p, u, v)
+        add_into(block(p, at), block(p, at), held[3], held[4])
+        add_into(block(p, at + 1), block(p, at + 1), held[2], held[5])
+        back(p, 30, block(p, at + 1 - x), last[p], near["x"])
+
+    def scatter_end(p):
+        r, low, width, first = PIECES[p]
+        u, v, one, two = axes(p)
+        came(p, 30, last[p])
+        add_into(outs[r].at[:, :, pl.ds(low, width)], block(p, spot(p, u, v) + x), last[p])
+
+    def each(step, group, *rest):
+        for p in group:
+            step(p, *rest)
 
     def remote(k, src, dst):
-        return pltpu.make_async_remote_copy(
-            src_ref=src, dst_ref=dst, send_sem=send_sem.at[k], recv_sem=recv_sem.at[k],
-            device_id=partner, device_id_type=MESH,
-        )
+        return far(src, dst, send_sem.at[k], recv_sem.at[k], partner)
 
     def widen_start(k, wide):
         remote(k, wide.at[:, t], wide.at[:, t]).start()
@@ -538,6 +466,7 @@
     def mod(s, k):
         return mods[s, k : k + 1, :]
 
+    each(gather_begin, ALL)
     for s in range(slots):
         unit, inverse = normed(lat[s].astype(jnp.float32))
         wide1[s, t] = (unit * (1.0 + mod(s, 1)) + mod(s, 0)).astype(jnp.bfloat16)
@@ -548,6 +477,18 @@
     widen_start(1, wideg)
     grad_bd[1:2] = sum(jnp.sum(wideg[s, t].astype(jnp.float32), axis=0, keepdims=True) for s in range(slots))
 
+    each(gather_x, ALL)
+    each(gather_first, ONE)
+    each(gather_second, ONE, (0, 1, 2))
+    each(gather_first, TWO + THREE)
+    each(gather_first_end, ONE)
+    each(gather_second, ONE, (3,))
+    for k in range(4):
+        each(gather_relay, ONE, (k,))
+    each(gather_first_end, TWO)
+    each(gather_second, TWO, range(4))
+    each(gather_end, ONE, range(4))
+    each(gather_core, ONE)
     for j in range(8):
         pick = one_hot((128, 1024), lambda a, b: b == (a // 2) * 16 + (a % 2) * 8 + j)
         tail_w[:, 896 * j : 896 * j + 896] = dot(pick, wt[...].reshape(1024, 896)).astype(jnp.bfloat16)
@@ -565,6 +506,10 @@
         qk[:, cols] = flat.astype(jnp.bfloat16)
 
     columns_loop(9, to_qkv)
+    for k in range(4):
+        each(gather_relay, TWO, (k,))
+    each(gather_first_end, THREE)
+    each(gather_second, THREE, range(4))
     for i, lane in enumerate((0, 576, 1152)):
         low = lane // 128 * 128
         spread_heads = one_hot(
@@ -583,12 +528,15 @@
             raised = jnp.exp(scores - jnp.max(scores, axis=-1, keepdims=True))
             prob = raised / jnp.sum(raised, axis=-1, keepdims=True)
             probs[i, h] = prob
-            mixp[rows, lanes] = dot(prob.astype(jnp.bfloat16), v).astype(jnp.bfloat16)
+            gattp[rows, lanes] = dot(prob.astype(jnp.bfloat16), v).astype(jnp.bfloat16)
         return carry
 
     lax.fori_loop(0, slots, attend, 0)
+    each(gather_end, TWO, range(4))
+    for k in range(4):
+        each(gather_relay, THREE, (k,))
     join = one_hot((1024, 640), lambda a, b: (b - 64 == (a // 128) * 72 + a % 128) & (a % 128 < 72))
-    att[...] = dot(mixp[...], join).astype(jnp.bfloat16)
+    att[...] = dot(gattp[...], join).astype(jnp.bfloat16)
 
     def back_to_width(rows, w, cols, tail_cols, add):
         total = dot(rows, w[:, :, cols].reshape(1024, -1), 1, 1)
@@ -612,6 +560,8 @@
     widen_start(3, wide2)
     gd = widen_end(1, wideg)
     flipg[...] = gd.T
+    each(gather_core, TWO)
+    each(gather_end, THREE, range(4))
     h2 = widen_end(3, wide2)
     flip2[...] = h2.T
 
@@ -621,6 +571,7 @@
         acted[:, cols] = gelu_value(up).astype(jnp.bfloat16)
 
     columns_loop(9, feed)
+    each(gather_core, THREE)
     back_to_width(acted[...], w3, slice(0, 2304), slice(4608, 6912), False)
     narrow_start(4, 1)
     for s in range(slots):
@@ -642,8 +593,9 @@
         g[:, :, cols] = made[:1024].reshape(64, 16, 256)
         tail_g[:, pl.ds(pl.multiple_of(offset + cols.start, 256), 256)] = made[1024:]
 
-    columns_loop(9, lambda cols: weight_grad(flipg, acted, cols, g3, 4608))
-    columns_loop(9, lambda cols: weight_grad(flip2, gup, cols, g2, 2304))
+    each(sent, THREE)
+    columns_loop(9, lambda cols: weight_grad(flipg, acted, cols, w3, 4608))
+    each(scatter_twin, THREE)
 
     narrow_end(4, 1)
     for s in range(slots):
@@ -664,10 +616,17 @@
         middle[s] = gm
         wideb[s, t] = (mod(s, 2) * gm).astype(jnp.bfloat16)
     widen_start(6, wideb)
+    each(scatter_relay, THREE, BACK)
+    each(sent, TWO)
+    columns_loop(9, lambda cols: weight_grad(flip2, gup, cols, w2, 2304))
+    each(scatter_twin, TWO)
+    each(scatter_direct, THREE, BACK)
     grad_bd[0:1] = sum(jnp.sum(wideb[s, t].astype(jnp.float32), axis=0, keepdims=True) for s in range(slots))
     gb = widen_end(6, wideb)
     flipb[...] = gb.T
     gatt = dot(gb[:, :1024], w1[:, :, 1664:2304].reshape(1024, 640)) + dot(gb[:, 1024:], tail_w[:, 1664:2304])
+    each(scatter_on, THREE, BACK)
+    each(scatter_relay, TWO, BACK)
     gattp[...] = dot(gatt.astype(jnp.bfloat16), join, 1, 1).astype(jnp.bfloat16)
 
     def attend_back(i, carry):
@@ -680,25 +639,32 @@
             grad = dot(ga, v, 1, 1)
             inner = jnp.sum(prob * grad, axis=-1, keepdims=True)
             gs = (prob * (grad - inner)).astype(jnp.bfloat16)
-            gqkvp[0, rows, lanes] = (dot(gs, k) * factor).astype(jnp.bfloat16)
-            gqkvp[1, rows, lanes] = (dot(gs, q, 0, 0) * factor).astype(jnp.bfloat16)
-            gqkvp[2, rows, lanes] = dot(prob.astype(jnp.bfloat16), ga, 0, 0).astype(jnp.bfloat16)
+            qkvp[0, rows, lanes] = (dot(gs, k) * factor).astype(jnp.bfloat16)
+            qkvp[1, rows, lanes] = (dot(gs, q, 0, 0) * factor).astype(jnp.bfloat16)
+            qkvp[2, rows, lanes] = dot(prob.astype(jnp.bfloat16), ga, 0, 0).astype(jnp.bfloat16)
         return carry
 
-    lax.fori_loop(0, slots, attend_back, 0)
+    attend_back(0, 0)
+    each(scatter_direct, TWO, BACK)
+    each(scatter_middle, THREE, BACK)
+    attend_back(1, 0)
+    each(scatter_on, TWO, BACK)
     gqkv[...] = jnp.zeros_like(gqkv)
     for i, lane in enumerate((0, 576, 1152)):
         low = lane // 128 * 128
         gather_heads = one_hot(
             (1024, 640), lambda a, b: (b - (lane - low) == (a // 128) * 72 + a % 128) & (a % 128 < 72)
         )
-        piece = dot(gqkvp[i], gather_heads).astype(jnp.bfloat16)
+        piece = dot(qkvp[i], gather_heads).astype(jnp.bfloat16)
         gqkv[:, low : low + 640] = gqkv[:, low : low + 640] + piece
     grad_bqkv[...] = jnp.sum(gqkv[...].astype(jnp.float32), axis=0, keepdims=True)
     back_to_width(gqkv[...], w1, slice(0, 1792), slice(0, 1792), False)
     narrow_start(7, 3)
 
-    columns_loop(6, lambda cols: weight_grad(flip1, gqkv, cols, g1, 0))
+    each(scatter_middle, TWO, BACK)
+    each(scatter_outer, THREE)
+    each(sent, ONE)
+    columns_loop(6, lambda cols: weight_grad(flip1, gqkv, cols, w1, 0))
     for low, high in ((1536, 1664), (1664, 1792), (1792, 2304)):
         made = 0.0
         if low < 1792:
@@ -706,14 +672,18 @@
         if high > 1664:
             made = made + dot(flipb[...], att[:, low - 1664 : high - 1664])
         made = made.astype(jnp.bfloat16)
-        g1[:, :, low:high] = made[:1024].reshape(64, 16, high - low)
+        w1[:, :, low:high] = made[:1024].reshape(64, 16, high - low)
         tail_g[:, low:high] = made[1024:]
     tail_g[:, 6912:] = jnp.zeros((128, 256), jnp.bfloat16)
     total = jnp.zeros((1024, 896), jnp.float32)
     for j in range(8):
         pick = one_hot((1024, 128), lambda a, b: a == (b // 2) * 16 + (b % 2) * 8 + j)
         total = total + dot(pick, tail_g[:, 896 * j : 896 * j + 896])
-    gt[...] = total.astype(jnp.bfloat16).reshape(64, 16, 896)
+    wt[...] = total.astype(jnp.bfloat16).reshape(64, 16, 896)
+    each(scatter_twin, ONE)
+    each(scatter_x, THREE)
+    each(scatter_outer, TWO)
+    each(scatter_relay, ONE, BACK)
 
     narrow_end(7, 3)
     for s in range(slots):
@@ -723,38 +693,58 @@
         grad_mod[s, 1:2] = jnp.sum(gh * unit, axis=0, keepdims=True)
         grad_lat[s] = middle[s] + norm_back(gh * (1.0 + mod(s, 1)), unit, inverse)
         grad_mod[s, 6:8] = jnp.zeros((2, 1152), jnp.float32)
-
-
-def middle_block(args, collective_id):
+    each(scatter_x, TWO)
+    each(scatter_direct, ONE, BACK)
+    each(scatter_end, THREE)
+    each(scatter_on, ONE, BACK)
+    each(scatter_end, TWO)
+    each(scatter_middle, ONE, BACK)
+    each(scatter_outer, ONE)
+    each(scatter_x, ONE)
+    each(scatter_end, ONE)
+    each(sent, ALL)
+
+
+def whole_block(args, weights, collective_id):
     f32, bf = jnp.float32, jnp.bfloat16
+    m = len(WIDTHS)
     vmem = pl.BlockSpec(memory_space=pltpu.VMEM)
     shape = jax.ShapeDtypeStruct
+    n = len(PIECES)
+
+    def room(*lead):
+        return [pltpu.VMEM(lead + (16, piece[2]), bf) for piece in PIECES]
+
+    dma = pltpu.SemaphoreType.DMA
     return pl.pallas_call(
-        middle_kernel,
+        block_kernel,
         out_shape=[
             shape((2, 64, 1152), bf), shape((2, 64, 1152), f32),
-            shape((64, 16, 2304), bf), shape((64, 16, 2304), bf), shape((64, 16, 2304), bf), shape((64, 16, 896), bf),
+            *[shape((1, 16, width), f32) for width in WIDTHS],
             shape((2, 8, 1152), f32), shape((2, 1152), f32), shape((1, 1792), f32), shape((1, 2304), f32),
         ],
-        in_specs=[vmem] * len(args),
-        out_specs=[vmem] * 10,
+        in_specs=[vmem] * (len(args) + m),
+        out_specs=[vmem] * (6 + m),
         scratch_shapes=[
+            *[pltpu.VMEM((64, 16, width), bf) for width in WIDTHS],
+            *[pltpu.VMEM((32, 16, width), bf) for width in WIDTHS],
+            *room(4, 6), *room(6), *room(1),
             pltpu.VMEM((128, 7168), bf), pltpu.VMEM((128, 7168), bf),
             *[pltpu.VMEM((2, 2, 64, 1152), bf)] * 4,
             *[pltpu.VMEM((1152, 256), bf)] * 4,
             pltpu.VMEM((4, 2, 64, 1152), bf), pltpu.VMEM((4, 2, 64, 1152), bf),
             pltpu.VMEM((2, 2, 64, 1152), f32),
-            pltpu.VMEM((3, 256, 1024), bf), pltpu.VMEM((256, 1024), bf), pltpu.VMEM((2, 8, 128, 128), f32),
-            pltpu.VMEM((256, 1024), bf), pltpu.VMEM((3, 256, 1024), bf),
+            pltpu.VMEM((3, 256, 1024), bf), pltpu.VMEM((2, 8, 128, 128), f32), pltpu.VMEM((256, 1024), bf),
             pltpu.VMEM((256, 2304), bf), pltpu.VMEM((256, 1792), bf), pltpu.VMEM((256, 640), bf),
             pltpu.VMEM((256, 2304), f32), pltpu.VMEM((256, 2304), bf), pltpu.VMEM((256, 2304), bf),
-            *[pltpu.VMEM((2, 64, 1152), f32)] * 4,
-            pltpu.SemaphoreType.DMA((8,)), pltpu.SemaphoreType.DMA((8,)),
+            *[pltpu.VMEM((2, 64, 1152), f32)] * 3,
+            dma((8,)), dma((8,)),
+            dma((n,)), dma((n, 31)), dma((n, 16)), dma((n, 21)), dma((n, 16)), dma((n, 31)), dma((n, 16)),
         ],
         compiler_params=pltpu.CompilerParams(
-            collective_id=collective_id, has_side_effects=True, vmem_limit_bytes=62 * 1024 * 1024
+            collective_id=collective_id, has_side_effects=True, vmem_limit_bytes=63 * 1024 * 1024
         ),
-    )(*args)
+    )(*args, *weights)
 
 
 MAIN = 1024
@@ -851,21 +841,21 @@
     own_rows = jnp.concatenate([w_qkv[0], w_qkv[1], w_qkv[2], w_proj.T, w_up, w_down.T], axis=1)
     width = own_rows.shape[1]
     head_part = w_qkv.shape[2]
-    weights = gather_blocks(pack_rows(own_rows), 2)
+    weights = pack_rows(own_rows)
     mods = jnp.concatenate(
         [slot_mod, jnp.broadcast_to(live[:, None, None], (slots, 2, slot_mod.shape[2]))], axis=1
     )
     nothing = jnp.zeros_like(b_qv[0])
     bias_qkv = jnp.concatenate([b_qv[0], nothing, b_qv[1], nothing])[None]
-    block_output, grad_latents, *grads, grad_mod, grad_bd, grad_bqkv, grad_bup = middle_block(
-        (rows, cotangent, mods, bias_d, bias_qkv, b_up[None], *weights), 6
+    block_output, grad_latents, *grads, grad_mod, grad_bd, grad_bqkv, grad_bup = whole_block(
+        (rows, cotangent, mods, bias_d, bias_qkv, b_up[None]), weights, 2
     )
     block_output = straight(block_output, matrix)
     grad_latents = straight_wide(grad_latents, matrix)
     grad_b_qv_local = jnp.stack([grad_bqkv[0, :head_part], grad_bqkv[0, 2 * head_part : 3 * head_part]])
     grad_b_up_local = grad_bup[0]
     grad_b_proj, grad_b_down = grad_bd[0], grad_bd[1]
-    summed = unpack_rows(*scatter_blocks(grads, 3))
+    summed = unpack_rows(*(each[0] for each in grads))
     grad_w_qkv = jnp.stack([summed[:, i * head_part : (i + 1) * head_part] for i in range(3)])
     grad_w_proj = summed[:, 3 * head_part : 4 * head_part].T
     up_part = w_up.shape[1]

time: 344 us -> 287 us (0.83)
  Pallas kernels: 285 us -> 238 us
  local copies, waits for them, and re-layouts: 21.8 us -> 15.7 us
    pallas_call x3 -> x1, Pallas kernels: 222 us -> 168 us  [whole_block(): pl.pallas_call(block_kernel, out_shape=[shape((2, 64, 1152), bf), shape((...]
    pallas_call x2, Pallas kernels: 35.8 us -> 42.5 us  [exchange(): pl.pallas_call(functools.partial(exchange_kernel, halve), out_shape=jax.S...]
where the time goes in v3:
time: 287 us; the launch traced here: 284 us
  Pallas kernels  238 us (83%)
  matrix products  21.6 us (8%)
  local copies, waits for them, and re-layouts  15.7 us (5%)
  other arithmetic  6.84 us (2%)
    pallas_call x1, Pallas kernels, whole_block(): pl.pallas_call(block_kernel, out_shape=[shape((2, 64, 1152), bf), shape((...  168 us
    pallas_call x2, Pallas kernels, exchange(): pl.pallas_call(functools.partial(exchange_kernel, halve), out_shape=jax.S...  42.5 us
    pallas_call x1, Pallas kernels, total_everywhere(): pl.pallas_call(total_kernel, out_shape=jax.ShapeDtypeStruct(parts.shape,...  27.9 us
    dot_general x3, matrix products, straight_wide(): jnp.einsum('...e,de->...d', rows, matrix.astype(jnp.float32), precision=h...  8.41 us

profile of v3, /device:TPU:1, one launch (start us, length us, event | category | flops | bytes accessed | tf_op | source)
XLA Modules:
  0.0 283.5 jit_solution(17410102298591873653)
XLA Ops:
  0.7 0.8 stack.33
  1.5 0.7 stack.34
  2.3 2.3 fusion.refs_3_
  4.6 0.1 iota_compare_fusion.6
  4.7 0.2 lt.160
  4.9 0.1 concatenate.22
  5.0 0.6 broadcast_in_dim.74.refs_4_
  5.6 0.6 broadcast_in_dim.75.refs_5_
  6.2 0.5 fusion.44
  6.8 0.1 copy.47
  6.9 0.1 reduce-window.9
  7.0 0.1 reduce
  7.1 0.6 fusion.114
  7.7 0.6 compare_convert_fusion
  8.4 0.1 broadcast_in_dim.72
  8.5 0.1 add_clamp_fusion
  8.5 0.1 min.12
  8.7 0.1 select_reduce_fusion
  8.8 0.1 convolution_convert_fusion
  8.9 0.1 copy.49
  9.1 0.6 slice_bitcast_fusion.2.refs_7_
  9.7 0.1 concatenate.23
  9.9 0.7 slice_bitcast_fusion
  10.5 0.7 pad.16.in_ref
  11.3 0.1 concatenate.24
  11.4 0.6 reshape.279.refs_9_
  12.1 22.7 %shard_map.246 = bf16[128,16,128]{2,1,0:T(8,128)(2,1)} custom-call(bf16[64,16,128]{2,1,0:T(8,128)(2,1)} %pad.16.in_ref), custom_call_target="tpu_custom_call" | custom-call | tf_op jit(solution)/shard_map/pallas_call | solution.py:130
  34.8 1.0 slice.92
  35.8 0.1 copy.50
  35.9 1.9 fusion.32.refs_1_
  37.8 1.9 fusion.35.refs_0_
  39.6 0.3 copy.61
  39.9 0.5 reshape.294
  40.4 1.0 fusion.41
  41.5 0.7 pad_maximum_fusion.5.refs_2_
  42.1 167.6 %shard_map.247 = (bf16[2,64,1152]{2,1,0:T(8,128)(2,1)}, f32[2,64,1152]{2,1,0:T(8,128)}, f32[1,16,2304]{2,1,0:T(8,128)}, f32[1,16,2304]{2,1,0:T(8,128)}, f32[1,16...) custom-call(bf16[2,64,1152]{2,1,0:T(8,128)(2,1)} %fusion.35.refs_0_,, ...), custom_call_target="tpu_custom_call" | custom-call | tf_op jit(solution)/shard_map/pallas_call | solution.py:719
  209.8 2.9 %fusion.29 = bf16[2,64,1152]{2,1,0:T(8,128)(2,1)} fusion(bf16[2,64,1152]{2,1,0:T(8,128)(2,1)} %get-tuple-element.23, s32[1152]{0:T(1024)S(1)} %fusion.84), kind=kOutput, calls=%fused_computation.20 | convolution fusion | flops 341213184 | bytes 594432 | tf_op jit(solution)/shard_map/...e,de->...d/dot_general | solution.py:773
  212.7 0.3 dynamic_update_slice.6
  213.0 0.3 dynamic_update_slice.7
  213.5 2.5 fusion.3
  216.1 0.7 maximum_bitcast_fusion
  216.8 0.8 fusion.56
  217.6 0.7 pad_maximum_fusion.4
  218.3 3.5 %fusion.5 = f32[2,64,1152]{2,1,0:T(8,128)} fusion(f32[2,64,1152]{2,1,0:T(8,128)S(1)} %copy-done.18, s32[1152]{0:T(1024)S(1)} %fusion.84), kind=kOutput, calls=%fused_computation.5 | convolution fusion | flops 2039758848 | bytes 1184256 | tf_op jit(solution)/shard_map/...e,de->...d/dot_general | solution.py:777
  221.8 0.7 reshape.280
  222.5 0.3 copy.54
  222.7 0.1 copy.55
  222.9 0.8 pad.18.in_ref
  223.7 19.8 %shard_map.248 = f32[128,8,128]{2,1,0:T(8,128)} custom-call(f32[128,8,128]{2,1,0:T(8,128)} %pad.18.in_ref), custom_call_target="tpu_custom_call" | custom-call | tf_op jit(solution)/shard_map/pallas_call | solution.py:130
  243.5 1.1 bitcast_reduce_fusion
  244.6 0.1 select_bitcast_fusion
  244.8 0.9 fusion.115
  245.7 1.3 fusion.51
  247.0 0.4 convolution_bitcast_fusion
  247.6 0.8 pad_bitcast_fusion.in_ref
  248.4 27.9 %shard_map.249 = f32[128,8,128]{2,1,0:T(8,128)} custom-call(f32[128,8,128]{2,1,0:T(8,128)} %pad_bitcast_fusion.in_ref), custom_call_target="tpu_custom_call" | custom-call | tf_op jit(solution)/shard_map/pallas_call | solution.py:160
  276.2 0.8 slice.124
  277.0 0.7 constant_dynamic-slice_fusion
  277.7 0.8 fusion.112
  278.5 2.4 fusion.1
  280.9 0.7 slice_reduce_fusion
  281.6 0.7 dynamic_slice.7
  282.3 0.1 reshape.287
  282.4 0.9 fusion.50
  (76 shorter events, 0.6 us)
Async XLA Ops:
  0.6 35.2 %copy-start = (bf16[2,64,1152]{2,1,0:T(8,128)(2,1)S(1)}, bf16[2,64,1152]{2,1,0:T(8,128)(2,1)}, u32[]{:S(2)}) copy-start(bf16[2,64,1152]{2,1,0:T(8,128)(2,1)} %param.29) | copy-start | bytes 884740
  0.7 3.9 %copy-start.16 = (s32[64]{0:T(128)S(1)}, s32[64]{0:T(128)}, u32[]{:S(2)}) copy-start(s32[64]{0:T(128)} %param.17) | copy-start | bytes 772
  0.7 5.5 %copy-start.8 = (bf16[96,1152]{1,0:T(8,128)(2,1)S(1)}, bf16[96,1152]{1,0:T(8,128)(2,1)}, u32[]{:S(2)}) copy-start(bf16[96,1152]{1,0:T(8,128)(2,1)} %param.16) | copy-start | bytes 663556
  0.7 5.5 %copy-start.7 = (bf16[1152,6,9]{0,1,2:T(8,128)(2,1)S(1)}, bf16[1152,6,9]{0,1,2:T(8,128)(2,1)}, u32[]{:S(2)}) copy-start(bf16[1152,6,9]{0,1,2:T(8,128)(2,1)} %param.19) | copy-start | bytes 373252
  0.7 4.9 %copy-start.12 = (f32[2304]{0:T(1024)S(1)}, f32[2304]{0:T(1024)}, u32[]{:S(2)}) copy-start(f32[2304]{0:T(1024)} %param.26) | copy-start | bytes 27652
  0.7 4.1 %copy-start.15 = (f32[2,576]{1,0:T(2,128)S(1)}, f32[2,576]{1,0:T(2,128)}, u32[]{:S(2)}) copy-start(f32[2,576]{1,0:T(2,128)} %param.22) | copy-start | bytes 13828
  0.7 5.5 %copy-start.21 = (f32[6,9]{1,0:T(8,128)S(1)}, f32[6,9]{1,0:T(8,128)}, u32[]{:S(2)}) copy-start(f32[6,9]{1,0:T(8,128)} %param.20) | copy-start | bytes 652
  6.2 2.5 copy-start.22
  6.2 2.9 %copy-start.5 = (bf16[18,2304]{1,0:T(8,128)(2,1)S(1)}, bf16[18,2304]{1,0:T(8,128)(2,1)}, u32[]{:S(2)}) copy-start(bf16[18,2304]{1,0:T(8,128)(2,1)} %param.25) | copy-start | bytes 248836
  6.2 3.5 %copy-start.10 = (bf16[3,18,576]{2,1,0:T(8,128)(2,1)S(1)}, bf16[3,18,576]{2,1,0:T(8,128)(2,1)}, u32[]{:S(2)}) copy-start(bf16[3,18,576]{2,1,0:T(8,128)(2,1)} %param.21) | copy-start | bytes 186628
  6.2 3.5 %copy-start.9 = (bf16[576,18]{0,1:T(8,128)(2,1)S(1)}, bf16[576,18]{0,1:T(8,128)(2,1)}, u32[]{:S(2)}) copy-start(bf16[576,18]{0,1:T(8,128)(2,1)} %param.23) | copy-start | bytes 62212
  6.7 3.1 %copy-start.6 = (bf16[2304,18]{0,1:T(8,128)(2,1)S(1)}, bf16[2304,18]{0,1:T(8,128)(2,1)}, u32[]{:S(2)}) copy-start(bf16[2304,18]{0,1:T(8,128)(2,1)} %param.27) | copy-start | bytes 248836
  35.9 1.9 copy-start.19
  209.7 2.9 %copy-start.17 = (f32[1,1792]{1,0:T(1,128)S(1)}, f32[1,1792]{1,0:T(1,128)}, u32[]{:S(2)}) copy-start(f32[1,1792]{1,0:T(1,128)} %get-tuple-element.27) | copy-start | bytes 21508
  209.7 3.2 %copy-start.14 = (f32[1,2304]{1,0:T(1,128)S(1)}, f32[1,2304]{1,0:T(1,128)}, u32[]{:S(2)}) copy-start(f32[1,2304]{1,0:T(1,128)} %get-tuple-element.28) | copy-start | bytes 27652
  209.8 3.6 %copy-start.13 = (f32[2,1152]{1,0:T(2,128)S(1)}, f32[2,1152]{1,0:T(2,128)}, u32[]{:S(2)}) copy-start(f32[2,1152]{1,0:T(2,128)} %get-tuple-element.26) | copy-start | bytes 27652
  209.8 3.6 %copy-start.11 = (f32[1,16,896]{2,1,0:T(8,128)S(1)}, f32[1,16,896]{2,1,0:T(8,128)}, u32[]{:S(2)}) copy-start(f32[1,16,896]{2,1,0:T(8,128)} %get-tuple-element.32) | copy-start | bytes 172036
  209.8 3.7 %copy-start.20 = (f32[2,8,1152]{2,1,0:T(8,128)S(1)}, f32[2,8,1152]{2,1,0:T(8,128)}, u32[]{:S(2)}) copy-start(f32[2,8,1152]{2,1,0:T(8,128)} %get-tuple-element.25) | copy-start | bytes 221188
  213.5 2.6 copy-start.2
  213.5 2.6 copy-start.3
  213.5 2.6 copy-start.4
  216.8 1.5 copy-start.18
  276.2 5.3 %copy-start.1 = (f32[128,8,128]{2,1,0:T(8,128)S(1)}, f32[128,8,128]{2,1,0:T(8,128)}, u32[]{:S(2)}) copy-start(f32[128,8,128]{2,1,0:T(8,128)} %shard_map.249) | copy-start | bytes 1572868
